TPU v7x, 32 devices: a whole 2x2x4 slice. The times are simulated.
32 devices in a mesh: section: 4 (over z), seq: 8 (over y, x, core).
Axes of the slice: x: 2, y: 2, z: 4, core: 2. Of those that a mesh axis runs over, the one named last changes fastest.
Arguments:
- tokens: bfloat16 [4, 64, 8192], P('section', 'seq'), may hold values from -6 to 6
- norm_gain: bfloat16 [4, 8192], P('section'), may hold values from 0.099609375 to 1.8984375
- w_query: bfloat16 [4, 8192, 8192], P('section', None, 'seq'), may hold values from -0.0625 to 0.0625
- key_projection: bfloat16 [4, 8192, 1024], P('section', None, 'seq'), may hold values from -0.1875 to 0.1875
- value_projection: bfloat16 [4, 8192, 1024], P('section', None, 'seq'), may hold values from -0.0625 to 0.0625
- w_out: bfloat16 [4, 8192, 8192], P('section', 'seq'), may hold values from -0.0625 to 0.0625
- key_cache: bfloat16 [4, 16384, 8, 128], P('section', 'seq'), may hold values from -400 to 400
- cached_value_rows: bfloat16 [4, 16384, 8, 128], P('section', 'seq'), may hold values from -6 to 6
- cache_mask: int32 [4, 2, 128], P('section', None, 'seq'), may hold values 0 or 1
- span_offset: int32 [4], P('section'), may hold values from 0 to 32767
Outputs:
- handed: bfloat16 [4, 64, 8192], P('section', 'seq')
All inputs are finite; a program needn't handle non-finite values. No bound on the sum of `cache_mask` on one device may be relied on, other than what follows from the above.
Results may differ from a plain program's by a relative error of at most 0.014.
Values may be sent and summed in bfloat16 or wider, within the bound.
No kernel may reach another device: no remote copies, remote signals or barrier semaphores. Data moves between devices by JAX's collectives and lax.ppermute only.
A program may use at most 192 MiB of HBM per device.

v0:
```python
import jax
import jax.numpy as jnp
from jax import lax
from jax.sharding import PartitionSpec as P

QB = 32
KB = 128


rope_base = 500000.0
neg_fill = -1e30
norm_eps = 1e-05


def passed_along(block, axis, distance):
    devices = range(lax.axis_size(axis))
    route = [((i - distance) % len(devices), i) for i in devices]
    return lax.ppermute(block, axis, route)


def apply_rotation(values, token_positions):
    half = values.shape[-1] // 2
    freqs = rope_base ** (-2.0 * jnp.arange(half, dtype=jnp.float32) / values.shape[-1])
    angles = token_positions[:, None] * freqs[None, :]
    cosine = jnp.cos(angles)[:, None, :]
    sine = jnp.sin(angles)[:, None, :]
    first = values[..., :half]
    second = values[..., half:]
    return jnp.concatenate(
        [first * cosine - second * sine, second * cosine + first * sine], axis=-1
    )


def on_device(
    tokens,
    norm_gain,
    w_query,
    key_projection,
    value_projection,
    w_out,
    key_cache,
    cached_value_rows,
    cache_mask,
    span_offset,
):
    n_seq = lax.axis_size("seq")
    rank = lax.axis_index("seq")
    head_dim = key_cache.shape[3]
    kv_heads = key_cache.shape[2]
    own_heads = w_query.shape[2] // head_dim
    all_heads = own_heads * n_seq
    group = all_heads // kv_heads
    tok_local = tokens.shape[1]
    tok_all = tok_local * n_seq
    ctx_local = key_cache.shape[1]
    scale = head_dim ** (-0.5)
    query_cols = own_heads * head_dim
    key_cols = key_projection.shape[2]
    offset = span_offset[0].astype(jnp.float32)
    resid = tokens[0].astype(jnp.float32)
    mean_square = jnp.mean(resid * resid, axis=-1, keepdims=True)
    input_normalized = (
        resid * lax.rsqrt(mean_square + norm_eps) * norm_gain[0].astype(jnp.float32)
    ).astype(jnp.bfloat16)
    piece = lax.all_gather(input_normalized, "seq", axis=0, tiled=True)
    rows = piece.shape[0]
    token_positions = offset + jnp.arange(rows, dtype=jnp.int32).astype(jnp.float32)
    query = jnp.dot(piece, w_query[0], preferred_element_type=jnp.float32)
    query = apply_rotation(query.reshape(rows, own_heads, head_dim), token_positions).reshape(
        rows, query_cols
    )
    key_unrotated = jnp.dot(piece, key_projection[0], preferred_element_type=jnp.float32)
    value_raw = jnp.dot(piece, value_projection[0], preferred_element_type=jnp.float32)
    fresh = jnp.concatenate([query, key_unrotated, value_raw], axis=1).astype(jnp.bfloat16)
    own_query = fresh[:, :query_cols]
    query_all, key_all, value_all = (
        lax.all_gather(own_query, "seq", axis=1, tiled=True),
        lax.all_gather(fresh[:, query_cols : query_cols + key_cols], "seq", axis=1, tiled=True),
        lax.all_gather(fresh[:, query_cols + key_cols :], "seq", axis=1, tiled=True),
    )
    positions_all = offset + jnp.arange(tok_all, dtype=jnp.int32).astype(jnp.float32)
    key_rot = apply_rotation(
        key_all.astype(jnp.float32).reshape(tok_all, kv_heads, head_dim), positions_all
    ).astype(jnp.bfloat16)
    value_heads = value_all.reshape(tok_all, kv_heads, head_dim)
    query_grouped = query_all.reshape(tok_all, kv_heads, group, head_dim)
    block = min(512, ctx_local)
    per_block = block // KB
    q_blocks = tok_all // QB

    def cache_step(index, carry):
        top, total, summed = carry
        keys = lax.dynamic_slice_in_dim(key_cache[0], index * block, block, 0)
        values = lax.dynamic_slice_in_dim(cached_value_rows[0], index * block, block, 0)
        visible = lax.dynamic_slice_in_dim(cache_mask[0], index * per_block, per_block, 1) > 0
        scores = (
            jnp.einsum("tgjd,cgd->tgjc", query_grouped, keys, preferred_element_type=jnp.float32)
            * scale
        )
        shaped = scores.reshape(q_blocks, QB, kv_heads, group, per_block, KB)
        allowed = visible[:, None, None, None, :, None]
        shaped = jnp.where(allowed, shaped, neg_fill)
        block_top = jnp.max(shaped, axis=(4, 5)).reshape(tok_all, kv_heads, group)
        new_top = jnp.maximum(top, block_top)
        lifted = new_top.reshape(q_blocks, QB, kv_heads, group, 1, 1)
        weights = jnp.where(allowed, jnp.exp(shaped - lifted), 0.0).reshape(
            tok_all, kv_heads, group, block
        )
        factor = jnp.exp(top - new_top)
        total = total * factor + jnp.sum(weights, axis=-1)
        summed = summed * factor[..., None] + jnp.einsum(
            "tgjc,cgd->tgjd",
            weights.astype(jnp.bfloat16),
            values,
            preferred_element_type=jnp.float32,
        )
        return (new_top, total, summed)

    start_top = jnp.full((tok_all, kv_heads, group), neg_fill, jnp.float32)
    start_total = jnp.zeros((tok_all, kv_heads, group), jnp.float32)
    start_sum = jnp.zeros((tok_all, kv_heads, group, head_dim), jnp.float32)
    top, total, summed = lax.fori_loop(
        0, ctx_local // block, cache_step, (start_top, start_total, start_sum)
    )
    top = top.reshape(tok_all, all_heads)
    total = total.reshape(tok_all, all_heads)
    summed = summed.reshape(tok_all, all_heads, head_dim)
    got_sum, got_top, got_total = (
        lax.all_to_all(summed[None], "seq", split_axis=2, concat_axis=0, tiled=True),
        lax.all_to_all(top[None], "seq", split_axis=2, concat_axis=0, tiled=True),
        lax.all_to_all(total[None], "seq", split_axis=2, concat_axis=0, tiled=True),
    )
    cache_top = jnp.max(got_top, axis=0)
    factor = jnp.exp(got_top - cache_top[None])
    cache_total = jnp.sum(got_total * factor, axis=0)
    cache_sum = jnp.sum(got_sum * factor[..., None], axis=0)
    kv_index = (rank * own_heads + jnp.arange(own_heads, dtype=jnp.int32)) // group
    own_keys = jnp.take(key_rot, kv_index, axis=1)
    own_values = jnp.take(value_heads, kv_index, axis=1)
    own_q = own_query.reshape(tok_all, own_heads, head_dim)
    self_scores = (
        jnp.einsum("thd,shd->ths", own_q, own_keys, preferred_element_type=jnp.float32) * scale
    )
    row_ids = jnp.arange(tok_all, dtype=jnp.int32)
    causal = (row_ids[None, :] <= row_ids[:, None])[:, None, :]
    self_scores = jnp.where(causal, self_scores, neg_fill)
    top_all = jnp.maximum(cache_top, jnp.max(self_scores, axis=-1))
    cache_factor = jnp.exp(cache_top - top_all)
    self_weights = jnp.where(causal, jnp.exp(self_scores - top_all[..., None]), 0.0)
    total_all = cache_total * cache_factor + jnp.sum(self_weights, axis=-1)
    sum_all = cache_sum * cache_factor[..., None] + jnp.einsum(
        "ths,shd->thd",
        self_weights.astype(jnp.bfloat16),
        own_values,
        preferred_element_type=jnp.float32,
    )
    attention = (sum_all / total_all[..., None]).reshape(tok_all, query_cols).astype(jnp.bfloat16)
    projected = lax.psum_scatter(
        jnp.dot(attention, w_out[0], preferred_element_type=jnp.float32).astype(jnp.bfloat16),
        "seq",
        scatter_dimension=0,
        tiled=True,
    ).astype(jnp.float32)
    layer_out = (resid + projected).astype(jnp.bfloat16)
    handed = passed_along(layer_out, "section", 1)
    return handed[None]


def solution(mesh):
    placed = (
        P("section", "seq", None),
        P("section", None),
        P("section", None, "seq"),
        P("section", None, "seq"),
        P("section", None, "seq"),
        P("section", "seq", None),
        P("section", "seq", None, None),
        P("section", "seq", None, None),
        P("section", None, "seq"),
        P("section"),
    )
    return jax.shard_map(
        on_device, mesh=mesh, in_specs=placed, out_specs=P("section", "seq", None), check_vma=False
    )
```

profile of v0, /device:TPU:0, one launch (start us, length us, event | category | flops | bytes accessed | tf_op | source)
XLA Modules:
  0.0 270.0 jit_solution(7629238576497510951)
XLA Ops:
  11.0 21.0 %copy.38 = bf16[1024,8192]{1,0:T(8,128)(2,1)} copy(bf16[1024,8192]{0,1:T(8,128)(2,1)} %bitcast.156) | data formatting | bytes 33554432 | tf_op jit(solution)/shard_map/dot_general | solution.py:68
  32.2 4.4 %all-gather.3.cloned.1.call-done = bf16[64,8192]{1,0:T(8,128)(2,1)} async-done(((bf16[8,8192]{1,0:T(8,128)(2,1)}), bf16[64,8192]{1,0:T(8,128)(2,1)}) %all-gather.3.cloned.1.call-update) | async-done | bytes 1048592 | tf_op jit(solution)/shard_map/all_gather | solution.py:65
  36.6 1.7 fusion.28
  38.3 9.0 %all_gather.14 = bf16[64,1024]{1,0:T(8,128)(2,1)S(1)} all-gather(bf16[64,128]{1,0:T(8,128)(2,1)S(1)} %fusion.28), channel_id=1, replica_groups=mesh['section'=4,'seq'=8] {'seq'}, dimensions={1}, use_global_device_ids=true | all-gather | bytes 147456 | tf_op jit(solution)/shard_map/all_gather | solution.py:78
  47.6 9.0 %fusion.34 = f32[64,8,128]{2,0,1:T(8,128)S(1)} fusion(bf16[8,128,8192]{2,1,0:T(8,128)(2,1)} %bitcast.155, bf16[64,8192]{1,0:T(8,128)(2,1)} %all-gather.3.cloned.1.call-done), kind=kOutput, calls=%fused_computation.43 | convolution fusion | flops 1073741824 | bytes 18087936 | tf_op jit(solution)/shard_map/dot_general | solution.py:68
  58.3 23.6 %all-gather.5.cloned.1.call-done = bf16[64,8192]{1,0:T(8,128)(2,1)} async-done(((bf16[64,1024]{1,0:T(8,128)(2,1)}), bf16[64,8192]{1,0:T(8,128)(2,1)}) %all-gather.5.cloned.1.call-update) | async-done | bytes 1048592 | tf_op jit(solution)/shard_map/all_gather | solution.py:77
  84.2 69.2 %while.18 = (s32[]{:T(128)}, f32[64,8,8]{0,2,1:T(8,128)S(1)}, f32[64,8,8]{0,2,1:T(8,128)S(1)}, f32[64,8,8,128]{3,0,2,1:T(8,128)}, s32[1,2,16]{2,1,0:T(2,128)S(1)...) while((s32[]{:T(128)}, f32[64,8,8]{0,2,1:T(8,128)S(1)}, ...), condition=%wide.region_4.5_spmd.clone, body=%wide.region_1.4_spmd.clone.sunk | while | flops 1102598144 | bytes 70713664 | solution.py:122
  84.2 1.7 constant_dynamic-slice_fusion.3
  86.1 4.6 %fusion.76 = (f32[64,8,8]{0,2,1:T(8,128)S(1)}, f32[8,512,64,8]{1,2,3,0:T(8,128)}) fusion(pred[64,512]{1,0:T(8,128)(4,1)S(1)} %bitcast.158, bf16[64,8,8,128]{3,0,2,1:T(8,128)(2,1)S(1)} %get-tuple-element.336, bf16[1,512,8,128]{3,2,1,0:T(8,128)(2,1)S(1)} %get-tuple-element.296), kind=kOutput, calls=%fused_computation.4.clone.1 | convolution fusion | flops 543158272 | bytes 10534912 | tf_op jit(solution)/shard_map/while/body/eval_jaxpr/tgjd,cgd->tgjc/dot_general | solution.py:97
  90.7 5.6 %fusion.77 = f32[64,8,8]{0,2,1:T(8,128)S(1)} fusion(f32[8,512,64,8]{1,2,3,0:T(8,128)} %get-tuple-element.298, f32[64,8,8]{0,2,1:T(8,128)S(1)} %select_maximum_fusion.2, pred[64,512]{1,0:T(8,128)(4,1)S(1)} %bitcast.159), kind=kLoop, calls=%fused_computation.6.clone.1 | loop fusion | flops 10481664 | bytes 8454144 | tf_op jit(solution)/shard_map/while/body/eval_jaxpr/reduce_sum | solution.py:110
  96.5 3.9 %bitcast_add_fusion.2 = f32[64,8,8,128]{3,0,2,1:T(8,128)} fusion(f32[64,8,8,128]{3,0,2,1:T(8,128)} %get-tuple-element.319, f32[8,512,64,8]{1,2,3,0:T(8,128)S(1)} %copy-done.2, f32[64,8,8]{0,2,1:T(8,128)S(1)} %select_maximum_fusion.2, pred[64,512]{1,0:T(8,128)(4,1)S(1)} %bitcast.160, bf16[1,512,8,128]{3,2,1,0:T(8,128)(2,1)S(1)} %get-tuple-element.300, ...), kind=kOutput, calls=%fused_computation.9.clone.1 | convolution fusion | flops 548929536 | bytes 13697025 | tf_op jit(solution)/shard_map/while/body/eval_jaxpr/tgjc,cgd->tgjd/dot_general | solution.py:111
  100.4 1.7 constant_dynamic-slice_fusion.3
  102.3 4.6 %fusion.76 = (f32[64,8,8]{0,2,1:T(8,128)S(1)}, f32[8,512,64,8]{1,2,3,0:T(8,128)}) fusion(pred[64,512]{1,0:T(8,128)(4,1)S(1)} %bitcast.158, bf16[64,8,8,128]{3,0,2,1:T(8,128)(2,1)S(1)} %get-tuple-element.336, bf16[1,512,8,128]{3,2,1,0:T(8,128)(2,1)S(1)} %get-tuple-element.296), kind=kOutput, calls=%fused_computation.4.clone.1 | convolution fusion | flops 543158272 | bytes 10534912 | tf_op jit(solution)/shard_map/while/body/eval_jaxpr/tgjd,cgd->tgjc/dot_general | solution.py:97
  106.9 5.6 %fusion.77 = f32[64,8,8]{0,2,1:T(8,128)S(1)} fusion(f32[8,512,64,8]{1,2,3,0:T(8,128)} %get-tuple-element.298, f32[64,8,8]{0,2,1:T(8,128)S(1)} %select_maximum_fusion.2, pred[64,512]{1,0:T(8,128)(4,1)S(1)} %bitcast.159), kind=kLoop, calls=%fused_computation.6.clone.1 | loop fusion | flops 10481664 | bytes 8454144 | tf_op jit(solution)/shard_map/while/body/eval_jaxpr/reduce_sum | solution.py:110
  112.7 5.4 %bitcast_add_fusion.2 = f32[64,8,8,128]{3,0,2,1:T(8,128)} fusion(f32[64,8,8,128]{3,0,2,1:T(8,128)} %get-tuple-element.319, f32[8,512,64,8]{1,2,3,0:T(8,128)S(1)} %copy-done.2, f32[64,8,8]{0,2,1:T(8,128)S(1)} %select_maximum_fusion.2, pred[64,512]{1,0:T(8,128)(4,1)S(1)} %bitcast.160, bf16[1,512,8,128]{3,2,1,0:T(8,128)(2,1)S(1)} %get-tuple-element.300, ...), kind=kOutput, calls=%fused_computation.9.clone.1 | convolution fusion | flops 548929536 | bytes 13697025 | tf_op jit(solution)/shard_map/while/body/eval_jaxpr/tgjc,cgd->tgjd/dot_general | solution.py:111
  119.9 4.6 %fusion.76 = (f32[64,8,8]{0,2,1:T(8,128)S(1)}, f32[8,512,64,8]{1,2,3,0:T(8,128)}) fusion(pred[64,512]{1,0:T(8,128)(4,1)S(1)} %bitcast.158, bf16[64,8,8,128]{3,0,2,1:T(8,128)(2,1)S(1)} %get-tuple-element.336, bf16[1,512,8,128]{3,2,1,0:T(8,128)(2,1)S(1)} %get-tuple-element.296), kind=kOutput, calls=%fused_computation.4.clone.1 | convolution fusion | flops 543158272 | bytes 10534912 | tf_op jit(solution)/shard_map/while/body/eval_jaxpr/tgjd,cgd->tgjc/dot_general | solution.py:97
  124.5 5.6 %fusion.77 = f32[64,8,8]{0,2,1:T(8,128)S(1)} fusion(f32[8,512,64,8]{1,2,3,0:T(8,128)} %get-tuple-element.298, f32[64,8,8]{0,2,1:T(8,128)S(1)} %select_maximum_fusion.2, pred[64,512]{1,0:T(8,128)(4,1)S(1)} %bitcast.159), kind=kLoop, calls=%fused_computation.6.clone.1 | loop fusion | flops 10481664 | bytes 8454144 | tf_op jit(solution)/shard_map/while/body/eval_jaxpr/reduce_sum | solution.py:110
  130.4 5.4 %bitcast_add_fusion.2 = f32[64,8,8,128]{3,0,2,1:T(8,128)} fusion(f32[64,8,8,128]{3,0,2,1:T(8,128)} %get-tuple-element.319, f32[8,512,64,8]{1,2,3,0:T(8,128)S(1)} %copy-done.2, f32[64,8,8]{0,2,1:T(8,128)S(1)} %select_maximum_fusion.2, pred[64,512]{1,0:T(8,128)(4,1)S(1)} %bitcast.160, bf16[1,512,8,128]{3,2,1,0:T(8,128)(2,1)S(1)} %get-tuple-element.300, ...), kind=kOutput, calls=%fused_computation.9.clone.1 | convolution fusion | flops 548929536 | bytes 13697025 | tf_op jit(solution)/shard_map/while/body/eval_jaxpr/tgjc,cgd->tgjd/dot_general | solution.py:111
  135.7 1.7 constant_dynamic-slice_fusion.3
  137.6 4.6 %fusion.76 = (f32[64,8,8]{0,2,1:T(8,128)S(1)}, f32[8,512,64,8]{1,2,3,0:T(8,128)}) fusion(pred[64,512]{1,0:T(8,128)(4,1)S(1)} %bitcast.158, bf16[64,8,8,128]{3,0,2,1:T(8,128)(2,1)S(1)} %get-tuple-element.336, bf16[1,512,8,128]{3,2,1,0:T(8,128)(2,1)S(1)} %get-tuple-element.296), kind=kOutput, calls=%fused_computation.4.clone.1 | convolution fusion | flops 543158272 | bytes 10534912 | tf_op jit(solution)/shard_map/while/body/eval_jaxpr/tgjd,cgd->tgjc/dot_general | solution.py:97
  142.2 5.6 %fusion.77 = f32[64,8,8]{0,2,1:T(8,128)S(1)} fusion(f32[8,512,64,8]{1,2,3,0:T(8,128)} %get-tuple-element.298, f32[64,8,8]{0,2,1:T(8,128)S(1)} %select_maximum_fusion.2, pred[64,512]{1,0:T(8,128)(4,1)S(1)} %bitcast.159), kind=kLoop, calls=%fused_computation.6.clone.1 | loop fusion | flops 10481664 | bytes 8454144 | tf_op jit(solution)/shard_map/while/body/eval_jaxpr/reduce_sum | solution.py:110
  148.0 5.4 %bitcast_add_fusion.2 = f32[64,8,8,128]{3,0,2,1:T(8,128)} fusion(f32[64,8,8,128]{3,0,2,1:T(8,128)} %get-tuple-element.319, f32[8,512,64,8]{1,2,3,0:T(8,128)S(1)} %copy-done.2, f32[64,8,8]{0,2,1:T(8,128)S(1)} %select_maximum_fusion.2, pred[64,512]{1,0:T(8,128)(4,1)S(1)} %bitcast.160, bf16[1,512,8,128]{3,2,1,0:T(8,128)(2,1)S(1)} %get-tuple-element.300, ...), kind=kOutput, calls=%fused_computation.9.clone.1 | convolution fusion | flops 548929536 | bytes 13697025 | tf_op jit(solution)/shard_map/while/body/eval_jaxpr/tgjc,cgd->tgjd/dot_general | solution.py:111
  155.4 3.3 %all-to-all-start.1 = ((f32[8,1,512]{2,1,0:T(1,128)}), f32[8,1,512]{2,1,0:T(1,128)S(1)}, u32[]{:S(2)}, u32[]{:S(2)}) async-start(f32[8,1,512]{2,1,0:T(1,128)} %reshape.212), calls=%async_computation.1 | async-start | bytes 32768 | tf_op jit(solution)/shard_map/all_to_all | solution.py:130
  160.1 3.2 %all-to-all-done.1 = f32[8,1,512]{2,1,0:T(1,128)S(1)} async-done(((f32[8,1,512]{2,1,0:T(1,128)}), f32[8,1,512]{2,1,0:T(1,128)S(1)}, u32[]{:S(2)}, u32[]{:S(2)}) %all-to-all-start.1) | async-done | bytes 16416 | tf_op jit(solution)/shard_map/all_to_all | solution.py:130
  163.4 3.3 %all-to-all-start.2 = ((f32[8,1,512]{2,1,0:T(1,128)}), f32[8,1,512]{2,1,0:T(1,128)S(1)}, u32[]{:S(2)}, u32[]{:S(2)}) async-start(f32[8,1,512]{2,1,0:T(1,128)} %reshape.214), calls=%async_computation.2 | async-start | bytes 32768 | tf_op jit(solution)/shard_map/all_to_all | solution.py:131
  166.7 4.7 %all-to-all-done.2 = f32[8,1,512]{2,1,0:T(1,128)S(1)} async-done(((f32[8,1,512]{2,1,0:T(1,128)}), f32[8,1,512]{2,1,0:T(1,128)S(1)}, u32[]{:S(2)}, u32[]{:S(2)}) %all-to-all-start.2) | async-done | bytes 16416 | tf_op jit(solution)/shard_map/all_to_all | solution.py:131
  171.4 3.6 %all-to-all-start = ((f32[1,64,64,128]{3,1,0,2:T(8,128)}), f32[1,64,64,128]{3,1,0,2:T(8,128)S(1)}, u32[]{:S(2)}, u32[]{:S(2)}) async-start(f32[1,64,64,128]{3,1,0,2:T(8,128)} %bitcast.165), calls=%async_computation | async-start | bytes 4194304 | tf_op jit(solution)/shard_map/all_to_all | solution.py:129
  176.8 2.4 fusion.31
  179.2 25.7 %all_gather.15 = bf16[64,1024]{1,0:T(8,128)(2,1)S(1)} all-gather(bf16[64,128]{1,0:T(8,128)(2,1)S(1)} %fusion.31), channel_id=1, replica_groups=mesh['section'=4,'seq'=8] {'seq'}, dimensions={1}, use_global_device_ids=true | all-gather | bytes 147456 | tf_op jit(solution)/shard_map/all_gather | solution.py:79
  208.6 10.1 %fusion.15 = bf16[64,8192]{1,0:T(8,128)(2,1)} fusion(bf16[1,1024,8192]{2,1,0:T(8,128)(2,1)} %param.19, bf16[8,8,8,128]{3,2,1,0:T(8,128)(2,1)S(1)} %fusion.27), kind=kOutput, calls=%fused_computation.27 | convolution fusion | flops 1074266112 | bytes 17956864 | tf_op jit(solution)/shard_map/dot_general | solution.py:159
  218.7 36.2 %reduce-scatter.2.cloned.1.call-done = bf16[8,8192]{1,0:T(8,128)(2,1)} async-done(((bf16[64,8192]{1,0:T(8,128)(2,1)}), bf16[8,8192]{1,0:T(8,128)(2,1)}) %reduce-scatter.2.cloned.1.call-update) | async-done | bytes 131088 | tf_op jit(solution)/shard_map/reduce_scatter | solution.py:158
  257.4 5.4 %collective-permute-done = bf16[8,8192]{1,0:T(8,128)(2,1)S(1)} collective-permute-done((bf16[8,8192]{1,0:T(8,128)(2,1)S(1)}, bf16[8,8192]{1,0:T(8,128)(2,1)S(1)}, u32[]{:S(2)}, u32[]{:S(2)}) %collective-permute-start) | collective-permute-done | bytes 131104 | tf_op jit(solution)/shard_map/ppermute | solution.py:18
  (92 shorter events, 23.5 us)
Async XLA Ops:
  6.5 30.1 %copy-start = (bf16[1,8192,128]{2,1,0:T(8,128)(2,1)S(1)}, bf16[1,8192,128]{2,1,0:T(8,128)(2,1)}, u32[]{:S(2)}) copy-start(bf16[1,8192,128]{2,1,0:T(8,128)(2,1)} %param.17) | copy-start | bytes 6291460
  6.5 30.1 %all-gather.3.cloned.1.call-start = ((), (), s32[]{:S(2)}) async-start(), calls=%async_computation.4 | async-start | bytes 1179648 | tf_op jit(solution)/shard_map/all_gather | solution.py:65
  10.3 71.7 %all-gather.5.cloned.1.call-start = ((), (), s32[]{:S(2)}) async-start(), calls=%async_computation.5 | async-start | bytes 1179648 | tf_op jit(solution)/shard_map/all_gather | solution.py:77
  47.6 36.6 %copy-start.4 = (s32[1,2,16]{2,1,0:T(2,128)S(1)}, s32[1,2,16]{2,1,0:T(2,128)}, u32[]{:S(2)}) copy-start(s32[1,2,16]{2,1,0:T(2,128)} %param.22) | copy-start | bytes 388
  90.6 5.8 %copy-start.2 = (f32[8,512,64,8]{1,2,3,0:T(8,128)S(1)}, f32[8,512,64,8]{1,2,3,0:T(8,128)}, u32[]{:S(2)}) copy-start(f32[8,512,64,8]{1,2,3,0:T(8,128)} %get-tuple-element.298) | copy-start | bytes 25165828 | tf_op jit(solution)/shard_map/while
  106.9 5.8 %copy-start.2 = (f32[8,512,64,8]{1,2,3,0:T(8,128)S(1)}, f32[8,512,64,8]{1,2,3,0:T(8,128)}, u32[]{:S(2)}) copy-start(f32[8,512,64,8]{1,2,3,0:T(8,128)} %get-tuple-element.298) | copy-start | bytes 25165828 | tf_op jit(solution)/shard_map/while
  124.5 5.8 %copy-start.2 = (f32[8,512,64,8]{1,2,3,0:T(8,128)S(1)}, f32[8,512,64,8]{1,2,3,0:T(8,128)}, u32[]{:S(2)}) copy-start(f32[8,512,64,8]{1,2,3,0:T(8,128)} %get-tuple-element.298) | copy-start | bytes 25165828 | tf_op jit(solution)/shard_map/while
  142.2 5.8 %copy-start.2 = (f32[8,512,64,8]{1,2,3,0:T(8,128)S(1)}, f32[8,512,64,8]{1,2,3,0:T(8,128)}, u32[]{:S(2)}) copy-start(f32[8,512,64,8]{1,2,3,0:T(8,128)} %get-tuple-element.298) | copy-start | bytes 25165828 | tf_op jit(solution)/shard_map/while
  155.4 8.0 %all-to-all-start.1 = ((f32[8,1,512]{2,1,0:T(1,128)}), f32[8,1,512]{2,1,0:T(1,128)S(1)}, u32[]{:S(2)}, u32[]{:S(2)}) async-start(f32[8,1,512]{2,1,0:T(1,128)} %reshape.212), calls=%async_computation.1 | async-start | bytes 32768 | tf_op jit(solution)/shard_map/all_to_all | solution.py:130
  163.4 8.0 %all-to-all-start.2 = ((f32[8,1,512]{2,1,0:T(1,128)}), f32[8,1,512]{2,1,0:T(1,128)S(1)}, u32[]{:S(2)}, u32[]{:S(2)}) async-start(f32[8,1,512]{2,1,0:T(1,128)} %reshape.214), calls=%async_computation.2 | async-start | bytes 32768 | tf_op jit(solution)/shard_map/all_to_all | solution.py:131
  171.4 36.2 %all-to-all-start = ((f32[1,64,64,128]{3,1,0,2:T(8,128)}), f32[1,64,64,128]{3,1,0,2:T(8,128)S(1)}, u32[]{:S(2)}, u32[]{:S(2)}) async-start(f32[1,64,64,128]{3,1,0,2:T(8,128)} %bitcast.165), calls=%async_computation | async-start | bytes 4194304 | tf_op jit(solution)/shard_map/all_to_all | solution.py:129
  175.0 80.0 %reduce-scatter.2.cloned.1.call-start = ((), (), s32[]{:S(2)}) async-start(), calls=%async_computation.6 | async-start | bytes 1179648 | tf_op jit(solution)/shard_map/reduce_scatter | solution.py:158
  208.3 55.2 %copy-start.1 = (bf16[1,8192,128]{2,1,0:T(8,128)(2,1)S(1)}, bf16[1,8192,128]{2,1,0:T(8,128)(2,1)}, u32[]{:S(2)}) copy-start(bf16[1,8192,128]{2,1,0:T(8,128)(2,1)} %param.17) | copy-start | bytes 6291460
  208.6 46.4 %copy-start.3 = (bf16[1,8,8192]{2,1,0:T(8,128)(2,1)S(1)}, bf16[1,8,8192]{2,1,0:T(8,128)(2,1)}, u32[]{:S(2)}) copy-start(bf16[1,8,8192]{2,1,0:T(8,128)(2,1)} %param.14) | copy-start | bytes 393220
  255.9 7.0 %collective-permute-start = (bf16[8,8192]{1,0:T(8,128)(2,1)S(1)}, bf16[8,8192]{1,0:T(8,128)(2,1)S(1)}, u32[]{:S(2)}, u32[]{:S(2)}) collective-permute-start(bf16[8,8192]{1,0:T(8,128)(2,1)S(1)} %fusion.39), channel_id=1, source_target_pairs={{24,0},{0,8},{8,16},{16,24},{25,1},{1,9},{9,17},{17,25},{26,2},{2,... | collective-permute-start | bytes 393224 | tf_op jit(solution)/shard_map/ppermute | solution.py:18
Sparse Core Ops, SparseCore 0:
  10.4 26.1 all-gather.2
  58.4 23.5 all-gather.4
  218.8 36.0 reduce-scatter.1
where the time goes:
time: 271 us; the launch traced here: 270 us
  waiting for transfers between devices  77.7 us (29%)
  matrix products  62.1 us (23%)
  local copies, waits for them, and re-layouts  35.4 us (13%)
  blocking collectives  34.7 us (13%)
  other arithmetic  34.1 us (13%)
  between operations  14.1 us (5%)
  starting transfers between devices  11.8 us (4%)
    reduce_scatter x1, waiting for transfers between devices, on_device(): lax.psum_scatter(jnp.dot(attention, w_out[0], preferred_element_type=jnp....  36.2 us
    all_gather x1, blocking collectives, on_device(): lax.all_gather(fresh[:, query_cols + key_cols:], 'seq', axis=1, tiled=True)  25.7 us
    all_gather x1, waiting for transfers between devices, on_device(): lax.all_gather(own_query, 'seq', axis=1, tiled=True)  23.6 us
    reduce_sum x4, other arithmetic, cache_step(): total = total * factor + jnp.sum(weights, axis=-1)  22.2 us
    dot_general x1, local copies, waits for them, and re-layouts, on_device(): query = jnp.dot(piece, w_query[0], preferred_element_type=jnp.float32)  21 us
    dot_general x4, matrix products, cache_step(): jnp.einsum('tgjc,cgd->tgjd', weights.astype(jnp.bfloat16), values, prefer...  20 us
    dot_general x4, matrix products, cache_step(): jnp.einsum('tgjd,cgd->tgjc', query_grouped, keys, preferred_element_type=...  18.3 us
    dot_general x1, matrix products, on_device(): jnp.dot(attention, w_out[0], preferred_element_type=jnp.float32)  10.1 us
  transfers between devices with their start and end apart: 7, of which 6 were waited for; matrix products, arithmetic and copies ran while one was open for 11% of the time, Pallas kernels for 0%

commit v1 on v0

--- a/solution.py
+++ b/solution.py
@@ -1,6 +1,8 @@
 import jax
 import jax.numpy as jnp
 from jax import lax
+from jax.experimental import pallas as pl
+from jax.experimental.pallas import tpu as pltpu
 from jax.sharding import PartitionSpec as P
 
 QB = 32
@@ -31,7 +33,7 @@
     )
 
 
-def on_device(
+def on_device_any(
     tokens,
     norm_gain,
     w_query,
@@ -166,6 +168,441 @@
     return handed[None]
 
 
+MIB = 1 << 20
+log2e = 1.4426950408889634
+IN_VMEM = pl.BlockSpec(memory_space=pltpu.VMEM)
+IN_SMEM = pl.BlockSpec(memory_space=pltpu.SMEM)
+SAME_CORE = (2, 4, 6)
+EVEN = (0, 2, 4, 6)
+ODD = (1, 3, 5, 7)
+
+
+def swapped(block, bits):
+    n = lax.axis_size("seq")
+    return lax.ppermute(block, "seq", [(i, i ^ bits) for i in range(n)])
+
+
+def call(kernel, name, out_shape, in_specs, flops=0, nbytes=0, scratch=(), vmem=16, **grid):
+    out_specs = grid.pop("out_specs", jax.tree.map(lambda _: IN_VMEM, out_shape))
+    return pl.pallas_call(
+        kernel,
+        out_shape=out_shape,
+        in_specs=in_specs,
+        out_specs=out_specs,
+        scratch_shapes=list(scratch),
+        name=name,
+        cost_estimate=pl.CostEstimate(flops=flops, bytes_accessed=nbytes, transcendentals=0),
+        compiler_params=pltpu.CompilerParams(vmem_limit_bytes=vmem * MIB),
+        **grid,
+    )
+
+
+def held(array):
+    return pltpu.with_memory_space_constraint(array, pltpu.VMEM)
+
+
+def by_head_kernel(keys, values, keys_out, values_out):
+    keys_out[...] = jnp.swapaxes(keys[...], 0, 1)
+    turned = jnp.swapaxes(values[...], 0, 1)
+    for g in range(turned.shape[0]):
+        values_out[g] = turned[g].T
+
+
+def cache_by_head(keys, values):
+    ctx, heads, dim = keys.shape
+    block = 256
+    source = pl.BlockSpec((block, heads, dim), lambda i: (i, 0, 0))
+    return call(
+        by_head_kernel,
+        "cache_by_head",
+        [
+            jax.ShapeDtypeStruct((heads, ctx, dim), jnp.bfloat16),
+            jax.ShapeDtypeStruct((heads, dim, ctx), jnp.bfloat16),
+        ],
+        [source, source],
+        nbytes=4 * ctx * heads * dim * 2,
+        grid=(ctx // block,),
+        out_specs=[
+            pl.BlockSpec((heads, block, dim), lambda i: (0, i, 0)),
+            pl.BlockSpec((heads, dim, block), lambda i: (0, 0, i)),
+        ],
+    )(keys, values)
+
+
+def rotated(heads, cosine, sine):
+    half = heads.shape[1] // 2
+    return heads * cosine + pltpu.roll(heads, half, 1) * sine
+
+
+def query_kernel(rank, *refs):
+    blocks = refs[:8]
+    gain, cosine, sine, weights, query, normed, rows = refs[8:]
+    width = rows.shape[1]
+    count = blocks[0].shape[0]
+    step = 1024
+    for bits in range(8):
+        at = pl.multiple_of((rank[0] ^ bits) * count, count)
+        rows[pl.ds(at, count), :] = blocks[bits][...].astype(jnp.float32)
+    squares = jnp.zeros((rows.shape[0], 128), jnp.float32)
+    for c in range(0, width, 128):
+        part = rows[:, c : c + 128]
+        squares = squares + part * part
+    mean_square = jnp.sum(squares, axis=-1, keepdims=True) / width
+    factor = lax.rsqrt(mean_square + norm_eps)
+    for c in range(0, width, step):
+        normed[:, c : c + step] = (
+            rows[:, c : c + step] * factor * gain[:, c : c + step].astype(jnp.float32)
+        ).astype(jnp.bfloat16)
+    dim = cosine.shape[1]
+    for c in range(0, weights.shape[1], 2 * dim):
+        raw = jnp.dot(
+            normed[...], weights[:, c : c + 2 * dim], preferred_element_type=jnp.float32
+        )
+        for d in range(0, 2 * dim, dim):
+            query[:, c + d : c + d + dim] = rotated(
+                raw[:, d : d + dim], cosine[...], sine[...]
+            ).astype(jnp.bfloat16)
+
+
+def query_rows(query, q_block, heads, dim):
+    rows = slice(q_block * QB, (q_block + 1) * QB)
+    return jnp.concatenate([query[rows, j * dim : (j + 1) * dim] for j in range(heads)], axis=0)
+
+
+def matmul_nt(a, b):
+    return lax.dot_general(a, b, (((1,), (1,)), ((), ())), preferred_element_type=jnp.float32)
+
+
+def new_kernel(scale, query, normed, w_key, w_value, cosine, sine, summed, stats):
+    tok, dim = cosine.shape
+    heads = query.shape[1] // dim
+    raw = jnp.dot(normed[...], w_key[...], preferred_element_type=jnp.float32)
+    raw = raw.astype(jnp.bfloat16).astype(jnp.float32)
+    keys = rotated(raw, cosine[...], sine[...]).astype(jnp.bfloat16)
+    values = jnp.dot(normed[...], w_value[...], preferred_element_type=jnp.float32)
+    values = values.astype(jnp.bfloat16).astype(jnp.float32).T.astype(jnp.bfloat16)
+    cols = heads * QB
+    for q_block in range(tok // QB):
+        scores = matmul_nt(keys, query_rows(query, q_block, heads, dim)) * scale
+        u = lax.broadcasted_iota(jnp.int32, (tok, cols), 0)
+        t = lax.broadcasted_iota(jnp.int32, (tok, cols), 1) % QB + q_block * QB
+        allowed = u <= t
+        scores = jnp.where(allowed, scores, neg_fill)
+        top = jnp.max(scores, axis=0, keepdims=True)
+        weights = jnp.where(allowed, jnp.exp2(scores - top), 0.0)
+        at = slice(q_block * cols, (q_block + 1) * cols)
+        stats[0:1, at] = top
+        stats[1:2, at] = jnp.sum(weights, axis=0, keepdims=True)
+        summed[:, at] = jnp.dot(
+            values, weights.astype(jnp.bfloat16), preferred_element_type=jnp.float32
+        )
+
+
+def split_rows(level, rows):
+    high = level.astype(jnp.bfloat16).astype(jnp.float32)
+    rest = level - high
+    middle = rest.astype(jnp.bfloat16).astype(jnp.float32)
+    low = rest - middle
+    row = lax.broadcasted_iota(jnp.int32, (rows, level.shape[1]), 0)
+    return jnp.where(row == 0, high, jnp.where(row == 1, middle, jnp.where(row == 2, low, 0.0)))
+
+
+def level_of(tail):
+    tail = tail.astype(jnp.float32)
+    return tail[0:1] + tail[1:2] + tail[2:3]
+
+
+def cache_kernel(scale, order, rank, mask, *refs):
+    queries = refs[:4]
+    keys, values, out, q_rows, summed, visible = refs[4:]
+    dim = keys.shape[2]
+    heads = queries[0].shape[1] // dim
+    cols = heads * QB
+    tail = out.shape[1] - dim
+    groups = [rank[0] ^ bits for bits in order]
+    for q_block in range(mask.shape[0]):
+        count = jnp.int32(0)
+        for b in range(mask.shape[1]):
+            visible[count] = b
+            count = count + (mask[q_block, b] > 0).astype(jnp.int32)
+        visible[count] = 0
+        for i in range(4):
+            q_rows[i] = query_rows(queries[i], q_block, heads, dim)
+            summed[i] = jnp.zeros((dim, cols), jnp.float32)
+
+        def step(pair, carry):
+            at_first = pl.multiple_of(visible[2 * pair] * KB, KB)
+            at_second = pl.multiple_of(visible[2 * pair + 1] * KB, KB)
+            hidden = jnp.where(2 * pair + 1 < count, jnp.float32(0.0), jnp.float32(neg_fill))
+            after = []
+            for i in range(4):
+                top, total = carry[2 * i], carry[2 * i + 1]
+                g = groups[i]
+                first = matmul_nt(keys[g, pl.ds(at_first, KB), :], q_rows[i]) * scale
+                second = matmul_nt(keys[g, pl.ds(at_second, KB), :], q_rows[i]) * scale + hidden
+                new_top = jnp.maximum(
+                    top,
+                    jnp.maximum(
+                        jnp.max(first, axis=0, keepdims=True),
+                        jnp.max(second, axis=0, keepdims=True),
+                    ),
+                )
+                first = jnp.exp2(first - new_top)
+                second = jnp.exp2(second - new_top)
+                factor = jnp.exp2(top - new_top)
+                total = (
+                    total * factor
+                    + jnp.sum(first, axis=0, keepdims=True)
+                    + jnp.sum(second, axis=0, keepdims=True)
+                )
+                weights = jnp.concatenate([first, second], axis=0).astype(jnp.bfloat16)
+                block = jnp.concatenate(
+                    [values[g, :, pl.ds(at_first, KB)], values[g, :, pl.ds(at_second, KB)]], axis=1
+                )
+                summed[i] = summed[i] * factor + jnp.dot(
+                    block, weights, preferred_element_type=jnp.float32
+                )
+                after += [new_top, total]
+            return tuple(after)
+
+        start = (jnp.full((1, cols), neg_fill, jnp.float32), jnp.zeros((1, cols), jnp.float32)) * 4
+        ended = lax.fori_loop(0, (count + 1) // 2, step, start)
+        at = slice(q_block * cols, (q_block + 1) * cols)
+        for i in range(4):
+            top, total = ended[2 * i], ended[2 * i + 1]
+            seen = total > 0.0
+            safe = jnp.where(seen, total, 1.0)
+            level = jnp.where(seen, top + jnp.log2(safe), neg_fill)
+            out[i, 0:dim, at] = (summed[i] / safe).astype(out.dtype)
+            out[i, dim:, at] = split_rows(level, tail).astype(out.dtype)
+
+
+def cache_part(scale, order, rank, mask, queries, keys, values, dtype, name):
+    heads, ctx, dim = keys.shape
+    cols = (queries[0].shape[1] // dim) * QB
+    tail = 16 if dtype == jnp.bfloat16 else 8
+    return call(
+        lambda *refs: cache_kernel(scale, order, *refs),
+        name,
+        jax.ShapeDtypeStruct((4, dim + tail, mask.shape[0] * cols), dtype),
+        [IN_SMEM, IN_SMEM] + [IN_VMEM] * 6,
+        flops=4 * 4 * queries[0].shape[0] * heads * ctx * dim // 4,
+        nbytes=4 * MIB,
+        scratch=[
+            pltpu.VMEM((4, cols, dim), jnp.bfloat16),
+            pltpu.VMEM((4, dim, cols), jnp.float32),
+            pltpu.SMEM((mask.shape[1] + 2,), jnp.int32),
+        ],
+    )(rank, mask, *queries, held(keys), held(values))
+
+
+def merge_kernel(own, got, kept, *sent):
+    dim = own.shape[1] - 8
+    for i in range(4):
+        mine, other = level_of(own[i, dim:, :]), level_of(got[i, dim:, :])
+        top = jnp.maximum(mine, other)
+        mine, other = jnp.exp2(mine - top), jnp.exp2(other - top)
+        total = mine + other
+        level = top + jnp.log2(total)
+        mine, other = mine / total, other / total
+        joined = own[i, :dim, :] * mine + got[i, :dim, :].astype(jnp.float32) * other
+        target = kept if i == 0 else sent[i - 1]
+        target[:dim, :] = joined.astype(target.dtype)
+        target[dim:, :] = split_rows(level, target.shape[0] - dim).astype(target.dtype)
+
+
+def output_kernel(rank, kept, got_a, got_b, got_c, summed, stats, weights, own, sent, rows, sorted_rows):
+    dim = summed.shape[0]
+    levels = [level_of(part[dim:, :]) for part in (kept, got_a, got_b, got_c)]
+    top = stats[0:1, :]
+    for level in levels:
+        top = jnp.maximum(top, level)
+    factor = jnp.exp2(stats[0:1, :] - top)
+    total = stats[1:2, :] * factor
+    joined = summed[...] * factor
+    for part, level in zip((kept, got_a, got_b, got_c), levels):
+        factor = jnp.exp2(level - top)
+        total = total + factor
+        joined = joined + part[:dim, :].astype(jnp.float32) * factor
+    joined = joined / total
+    heads = rows.shape[1] // dim
+    cols = heads * QB
+    for q_block in range(rows.shape[0] // QB):
+        turned = joined[:, q_block * cols : (q_block + 1) * cols].T
+        for j in range(heads):
+            rows[q_block * QB : (q_block + 1) * QB, j * dim : (j + 1) * dim] = turned[
+                j * QB : (j + 1) * QB, :
+            ]
+    count = rows.shape[0] // 8
+    for pair in range(4):
+        chunk = [
+            rows[pl.ds(pl.multiple_of((rank[0] ^ bits) * count, count), count), :]
+            for bits in (EVEN + ODD)[2 * pair : 2 * pair + 2]
+        ]
+        sorted_rows[2 * count * pair : 2 * count * (pair + 1), :] = jnp.concatenate(
+            chunk, axis=0
+        ).astype(jnp.bfloat16)
+    half = rows.shape[0] // 2
+    step = 512
+    for c in range(0, weights.shape[1], step):
+        product = jnp.dot(
+            sorted_rows[...], weights[:, c : c + step], preferred_element_type=jnp.float32
+        )
+        own[:, c : c + step] = product[:half]
+        sent[:, c : c + step] = product[half:].astype(jnp.bfloat16)
+
+
+def on_device_owned(
+    tokens,
+    norm_gain,
+    w_query,
+    key_projection,
+    value_projection,
+    w_out,
+    key_cache,
+    cached_value_rows,
+    cache_mask,
+    span_offset,
+):
+    n_seq = lax.axis_size("seq")
+    rank = lax.axis_index("seq").astype(jnp.int32)[None]
+    dim = key_cache.shape[3]
+    count = tokens.shape[1]
+    width = tokens.shape[2]
+    tok = count * n_seq
+    own_cols = w_query.shape[2]
+    scale = dim ** (-0.5) * log2e
+    mask = cache_mask[0]
+
+    with jax.named_scope("gather_tokens"):
+        blocks = {0: tokens[0]}
+        blocks[1] = swapped(tokens[0], 1)
+        for bits in SAME_CORE:
+            blocks[bits] = swapped(tokens[0], bits)
+        for bits in SAME_CORE:
+            blocks[bits ^ 1] = swapped(blocks[bits], 1)
+
+    with jax.named_scope("tables"):
+        positions = span_offset[0].astype(jnp.float32) + jnp.arange(tok, dtype=jnp.int32).astype(
+            jnp.float32
+        )
+        freqs = rope_base ** (-2.0 * jnp.arange(dim // 2, dtype=jnp.float32) / dim)
+        angles = positions[:, None] * freqs[None, :]
+        cosine, sine = jnp.cos(angles), jnp.sin(angles)
+        cosine = jnp.concatenate([cosine, cosine], axis=1)
+        sine = jnp.concatenate([-sine, sine], axis=1)
+
+    with jax.named_scope("cache_layout"):
+        keys, values = cache_by_head(key_cache[0], cached_value_rows[0])
+
+    with jax.named_scope("queries"):
+        query, normed = call(
+            query_kernel,
+            "queries",
+            [
+                jax.ShapeDtypeStruct((tok, own_cols), jnp.bfloat16),
+                jax.ShapeDtypeStruct((tok, width), jnp.bfloat16),
+            ],
+            [IN_SMEM] + [IN_VMEM] * 12,
+            flops=2 * tok * width * own_cols,
+            nbytes=16 * MIB,
+            scratch=[pltpu.VMEM((tok, width), jnp.float32)],
+        )(
+            rank,
+            *[blocks[bits] for bits in range(8)],
+            norm_gain,
+            cosine,
+            sine,
+            held(w_query[0]),
+        )
+
+    with jax.named_scope("gather_queries"):
+        queries = {0: query}
+        for bits in ODD:
+            queries[bits] = swapped(query, bits)
+        for bits in SAME_CORE:
+            queries[bits] = swapped(queries[bits ^ 1], 1)
+
+    with jax.named_scope("new_tokens"):
+        summed, stats = call(
+            lambda *refs: new_kernel(scale, *refs),
+            "new_tokens",
+            [
+                jax.ShapeDtypeStruct((dim, tok * own_cols // dim), jnp.float32),
+                jax.ShapeDtypeStruct((8, tok * own_cols // dim), jnp.float32),
+            ],
+            [IN_VMEM] * 6,
+            flops=4 * tok * width * dim,
+            nbytes=5 * MIB,
+        )(query, normed, held(key_projection[0]), held(value_projection[0]), cosine, sine)
+
+    with jax.named_scope("cache_odd"):
+        odd = cache_part(
+            scale, ODD, rank, mask, [queries[b] for b in ODD], keys, values, jnp.bfloat16, "cache_odd"
+        )
+    with jax.named_scope("swap_odd"):
+        got = swapped(odd, 1)
+    with jax.named_scope("cache_even"):
+        even = cache_part(
+            scale, EVEN, rank, mask, [queries[b] for b in EVEN], keys, values, jnp.float32, "cache_even"
+        )
+    with jax.named_scope("merge_cores"):
+        cols = even.shape[2]
+        kept, *sent = call(
+            merge_kernel,
+            "merge_cores",
+            [jax.ShapeDtypeStruct((dim + 8, cols), jnp.float32)]
+            + [jax.ShapeDtypeStruct((dim + 16, cols), jnp.bfloat16)] * 3,
+            [IN_VMEM] * 2,
+            nbytes=2 * MIB,
+        )(even, got)
+    with jax.named_scope("exchange_parts"):
+        parts = [swapped(block, bits) for block, bits in zip(sent, SAME_CORE)]
+    with jax.named_scope("project"):
+        own, other = call(
+            output_kernel,
+            "project",
+            [
+                jax.ShapeDtypeStruct((tok // 2, width), jnp.float32),
+                jax.ShapeDtypeStruct((tok // 2, width), jnp.bfloat16),
+            ],
+            [IN_SMEM] + [IN_VMEM] * 7,
+            flops=2 * tok * width * own_cols,
+            nbytes=18 * MIB,
+            scratch=[
+                pltpu.VMEM((tok, own_cols), jnp.float32),
+                pltpu.VMEM((tok, own_cols), jnp.bfloat16),
+            ],
+        )(rank, kept, *parts, summed, stats, held(w_out[0]))
+    with jax.named_scope("reduce_cores"):
+        pair = own + swapped(other, 1).astype(jnp.float32)
+    with jax.named_scope("reduce_chips"):
+        total = tokens[0].astype(jnp.float32) + pair[:count]
+        for i, bits in enumerate(SAME_CORE):
+            block = pair[(i + 1) * count : (i + 2) * count].astype(jnp.bfloat16)
+            total = total + swapped(block, bits).astype(jnp.float32)
+        layer_out = total.astype(jnp.bfloat16)
+    with jax.named_scope("hand_on"):
+        handed = passed_along(layer_out, "section", 1)
+    return handed[None]
+
+
+def on_device(*arrays):
+    tokens, w_query, key_projection, key_cache = arrays[0], arrays[2], arrays[3], arrays[6]
+    head_dim = key_cache.shape[3]
+    kv_heads = key_cache.shape[2]
+    n_seq = lax.axis_size("seq")
+    tok_all = tokens.shape[1] * n_seq
+    if (
+        n_seq == kv_heads == 8
+        and key_projection.shape[2] == head_dim == 128
+        and tokens.shape[1] == 8
+        and tok_all == 2 * QB
+    ):
+        return on_device_owned(*arrays)
+    return on_device_any(*arrays)
+
+
 def solution(mesh):
     placed = (
         P("section", "seq", None),

time: 271 us -> 85.7 us (0.32)
  matrix products: 62.1 us -> 0 us
  waiting for transfers between devices: 77.7 us -> 30.2 us
  blocking collectives: 34.7 us -> 0 us
  other arithmetic: 34.1 us -> 0.48 us
  Pallas kernels: 0 us -> 27.3 us
  local copies, waits for them, and re-layouts: 35.4 us -> 8.16 us
  between operations: 14.1 us -> 0.88 us
  starting transfers between devices: 11.8 us -> 18.1 us
    dot_general x14 -> x0, matrix products: 62.1 us -> none  [the longest x4 20 us: cache_step(): jnp.einsum('tgjc,cgd->tgjd', weights.astype(jnp.bfloat16), values, prefer...]
    reduce_scatter x1 -> x0, waiting for transfers between devices: 36.2 us -> none  [on_device(): lax.psum_scatter(jnp.dot(attention, w_out[0], preferred_element_type=jnp....]
    all_gather x2 -> x0, blocking collectives: 34.7 us -> none  [the longest x1 25.7 us: on_device(): lax.all_gather(fresh[:, query_cols + key_cols:], 'seq', axis=1, tiled=True)]
    all_gather x2 -> x0, waiting for transfers between devices: 28.1 us -> none  [the longest x1 23.6 us: on_device(): lax.all_gather(own_query, 'seq', axis=1, tiled=True)]
    pallas_call x0 -> x7, Pallas kernels: none -> 27.3 us  [the longest x2 16.1 us: cache_part(): call(lambda *refs: cache_kernel(scale, order, *refs), name, jax.ShapeDtyp...]
    ppermute x0 -> x22, waiting for transfers between devices: none -> 25.2 us  [swapped(): return lax.ppermute(block, 'seq', [(i, i ^ bits) for i in range(n)])]
    reduce_sum x8 -> x0, other arithmetic: 24.1 us -> none  [the longest x4 22.2 us: cache_step(): total = total * factor + jnp.sum(weights, axis=-1)]
    dot_general x1 -> x0, local copies, waits for them, and re-layouts: 21 us -> none  [on_device(): query = jnp.dot(piece, w_query[0], preferred_element_type=jnp.float32)]
  transfers between devices with their start and end apart: 7 -> 23, of which waited for: 6 -> 19; matrix products, arithmetic and copies ran while one was open for 11% -> 0% of each run, Pallas kernels for 0% -> 14%
where the time goes in v1:
time: 85.7 us; the launch traced here: 85.2 us
  waiting for transfers between devices  30.2 us (35%)
  Pallas kernels  27.3 us (32%)
  starting transfers between devices  18.1 us (21%)
  local copies, waits for them, and re-layouts  8.16 us (10%)
  between operations  0.88 us (1%)
    ppermute x22, waiting for transfers between devices, swapped(): return lax.ppermute(block, 'seq', [(i, i ^ bits) for i in range(n)])  25.2 us
    ppermute x22, starting transfers between devices, swapped(): return lax.ppermute(block, 'seq', [(i, i ^ bits) for i in range(n)])  16.4 us
    pallas_call x2, Pallas kernels, cache_part(): call(lambda *refs: cache_kernel(scale, order, *refs), name, jax.ShapeDtyp...  16.1 us
    unnamed x27, local copies, waits for them, and re-layouts  8.13 us
    ppermute x1, waiting for transfers between devices, passed_along(): return lax.ppermute(block, axis, route)  5.06 us
    pallas_call x1, Pallas kernels, on_device_owned(): call(query_kernel, 'queries', [jax.ShapeDtypeStruct((tok, own_cols), jnp....  3.58 us
    pallas_call x1, Pallas kernels, on_device_owned(): call(output_kernel, 'project', [jax.ShapeDtypeStruct((tok // 2, width), j...  3.24 us
    pallas_call x1, Pallas kernels, cache_by_head(): call(by_head_kernel, 'cache_by_head', [jax.ShapeDtypeStruct((heads, ctx,...  2.92 us
  transfers between devices with their start and end apart: 23, of which 19 were waited for; matrix products, arithmetic and copies ran while one was open for 0% of the time, Pallas kernels for 14%

profile of v1, /device:TPU:0, one launch (start us, length us, event | category | flops | bytes accessed | tf_op | source)
XLA Modules:
  0.0 85.2 jit_solution(5958856599722162057)
XLA Ops:
  0.0 3.9 %collective-permute-start.5 = (bf16[8,8192]{1,0:T(8,128)(2,1)}, bf16[8,8192]{1,0:T(8,128)(2,1)S(1)}, u32[]{:S(2)}, u32[]{:S(2)}) collective-permute-start(bf16[8,8192]{1,0:T(8,128)(2,1)} %bitcast.20), channel_id=1, source_target_pairs={{0,6},{1,7},{2,4},{3,5},{4,2},{5,3},{6,0},{7,1},{8,14},{9,15},{10,... | collective-permute-start | bytes 393224 | tf_op jit(solution)/shard_map/gather_tokens/ppermute | solution.py:182
  5.1 3.0 %collective-permute-done.5.refs_6_ = bf16[8,8192]{1,0:T(8,128)(2,1)S(1)} collective-permute-done((bf16[8,8192]{1,0:T(8,128)(2,1)}, bf16[8,8192]{1,0:T(8,128)(2,1)S(1)}, u32[]{:S(2)}, u32[]{:S(2)}) %collective-permute-start.5) | collective-permute-done | bytes 131104 | tf_op jit(solution)/shard_map/gather_tokens/ppermute | solution.py:182
  8.1 2.3 %collective-permute-done.3.refs_4_ = bf16[8,8192]{1,0:T(8,128)(2,1)S(1)} collective-permute-done((bf16[8,8192]{1,0:T(8,128)(2,1)}, bf16[8,8192]{1,0:T(8,128)(2,1)S(1)}, u32[]{:S(2)}, u32[]{:S(2)}) %collective-permute-start.3) | collective-permute-done | bytes 131104 | tf_op jit(solution)/shard_map/gather_tokens/ppermute | solution.py:182
  11.2 0.5 collective-permute-done.4.refs_5_
  12.0 5.8 %copy-done = bf16[1,8192,1024]{2,1,0:T(8,128)(2,1)S(1)} copy-done((bf16[1,8192,1024]{2,1,0:T(8,128)(2,1)S(1)}, bf16[1,8192,1024]{2,1,0:T(8,128)(2,1)}, u32[]{:S(2)}) %copy-start) | copy-done | bytes 16777240
  17.8 0.9 %copy-done.5 = bf16[1,8,8192]{2,1,0:T(8,128)(2,1)S(1)} copy-done((bf16[1,8,8192]{2,1,0:T(8,128)(2,1)S(1)}, bf16[1,8,8192]{2,1,0:T(8,128)(2,1)}, u32[]{:S(2)}) %copy-start.5) | copy-done | bytes 131096
  18.7 0.8 copy-done.7
  19.4 3.6 %queries.1 = (bf16[64,1024]{1,0:T(8,128)(2,1)S(1)}, bf16[64,8192]{1,0:T(8,128)(2,1)S(1)}) custom-call(s32[1]{0:T(128)} %bitcast.1.rank.refs_0_, bf16[8,8192]{1,0:T(8,128)(2,1)S(1)} %bitcast.24, bf16[8,8192]{1,0:T(8,128)(2,1)S(1)} %collective-permute-done.refs_1_, bf16[8,8192]{1,0:T(8,128)(2,1)S(1)} %collective-permute-done.1.refs_2_, ...), custom_call_target="tpu_custom_call" | custom-call | flops 1073741824 | bytes 16777216 | tf_op jit(solution)/shard_map/queries/queries/pallas_call | solution.py:499
  23.4 1.5 %collective-permute-start.11 = (bf16[64,1024]{1,0:T(8,128)(2,1)S(1)}, bf16[64,1024]{1,0:T(8,128)(2,1)S(1)}, u32[]{:S(2)}, u32[]{:S(2)}) collective-permute-start(bf16[64,1024]{1,0:T(8,128)(2,1)S(1)} %get-tuple-element.17.refs_2_.refs_0_), channel_id=1, source_target_pairs={{0,7},{1,6},{2,5},{3,4},{4,3},{5,2},{6,1},{7,0},{8,15},{9,14},{10,... | collective-permute-start | bytes 393224 | tf_op jit(solution)/shard_map/gather_queries/ppermute | solution.py:182
  24.9 1.3 %collective-permute-start.9 = (bf16[64,1024]{1,0:T(8,128)(2,1)S(1)}, bf16[64,1024]{1,0:T(8,128)(2,1)S(1)}, u32[]{:S(2)}, u32[]{:S(2)}) collective-permute-start(bf16[64,1024]{1,0:T(8,128)(2,1)S(1)} %get-tuple-element.17.refs_2_.refs_0_), channel_id=1, source_target_pairs={{0,5},{1,4},{2,7},{3,6},{4,1},{5,0},{6,3},{7,2},{8,13},{9,12},{10,... | collective-permute-start | bytes 393224 | tf_op jit(solution)/shard_map/gather_queries/ppermute | solution.py:182
  26.4 2.9 %cache_by_head.1 = (bf16[8,2048,128]{2,1,0:T(8,128)(2,1)S(1)}, bf16[8,128,2048]{2,1,0:T(8,128)(2,1)S(1)}) custom-call(bf16[2048,8,128]{2,1,0:T(8,128)(2,1)S(1)} %bitcast.16, bf16[2048,8,128]{2,1,0:T(8,128)(2,1)S(1)} %bitcast.17), custom_call_target="tpu_custom_call" | custom-call | bytes 16777216 | tf_op jit(solution)/shard_map/cache_layout/cache_by_head/pallas_call | solution.py:215
  29.8 3.0 %collective-permute-done.9.refs_4_ = bf16[64,1024]{1,0:T(8,128)(2,1)S(1)} collective-permute-done((bf16[64,1024]{1,0:T(8,128)(2,1)S(1)}, bf16[64,1024]{1,0:T(8,128)(2,1)S(1)}, u32[]{:S(2)}, u32[]{:S(2)}) %collective-permute-start.9) | collective-permute-done | bytes 131104 | tf_op jit(solution)/shard_map/gather_queries/ppermute | solution.py:182
  32.9 8.0 %cache_odd.1 = bf16[4,144,512]{2,1,0:T(8,128)(2,1)S(1)} custom-call(s32[1]{0:T(128)} %bitcast.1.rank.refs_0_, s32[2,16]{1,0:T(2,128)S(1)} %bitcast.25, bf16[64,1024]{1,0:T(8,128)(2,1)S(1)} %collective-permute-done.13.refs_2_, bf16[64,1024]{1,0:T(8,128)(2,1)S(1)} %collective-permute-done.7.refs_3_, bf16[64,1024]{1,0:T(8,128)(2,1)S(1)} %collective-permute-done.9.refs_4_, ...), custom_call_target="tpu_custom_call" | custom-call | flops 536870912 | bytes 4194304 | tf_op jit(solution)/shard_map/cache_odd/cache_odd/pallas_call | solution.py:384
  42.0 1.2 %collective-permute-done.12.refs_5_ = bf16[64,1024]{1,0:T(8,128)(2,1)S(1)} collective-permute-done((bf16[64,1024]{1,0:T(8,128)(2,1)S(1)}, bf16[64,1024]{1,0:T(8,128)(2,1)S(1)}, u32[]{:S(2)}, u32[]{:S(2)}) %collective-permute-start.12) | collective-permute-done | bytes 131104 | tf_op jit(solution)/shard_map/gather_queries/ppermute | solution.py:182
  43.5 8.2 %cache_even.1.own = f32[4,136,512]{2,1,0:T(8,128)S(1)} custom-call(s32[1]{0:T(128)} %bitcast.1.rank.refs_0_, s32[2,16]{1,0:T(2,128)S(1)} %bitcast.26, bf16[64,1024]{1,0:T(8,128)(2,1)S(1)} %get-tuple-element.17.refs_2_.refs_0_, bf16[64,1024]{1,0:T(8,128)(2,1)S(1)} %collective-permute-done.8.refs_3_, bf16[64,1024]{1,0:T(8,128)(2,1)S(1)} %collective-permute-done.10.refs_4_, ...), custom_call_target="tpu_custom_call" | custom-call | flops 536870912 | bytes 4194304 | tf_op jit(solution)/shard_map/cache_even/cache_even/pallas_call | solution.py:384
  52.1 1.7 %collective-permute-start.16 = (bf16[144,512]{1,0:T(8,128)(2,1)S(1)}, bf16[144,512]{1,0:T(8,128)(2,1)S(1)}, u32[]{:S(2)}, u32[]{:S(2)}) collective-permute-start(bf16[144,512]{1,0:T(8,128)(2,1)S(1)} %get-tuple-element.22), channel_id=1, source_target_pairs={{0,4},{1,5},{2,6},{3,7},{4,0},{5,1},{6,2},{7,3},{8,12},{9,13},{10,... | collective-permute-start | bytes 442376 | tf_op jit(solution)/shard_map/exchange_parts/ppermute | solution.py:182
  53.8 1.7 %collective-permute-start.17 = (bf16[144,512]{1,0:T(8,128)(2,1)S(1)}, bf16[144,512]{1,0:T(8,128)(2,1)S(1)}, u32[]{:S(2)}, u32[]{:S(2)}) collective-permute-start(bf16[144,512]{1,0:T(8,128)(2,1)S(1)} %get-tuple-element.23), channel_id=1, source_target_pairs={{0,6},{1,7},{2,4},{3,5},{4,2},{5,3},{6,0},{7,1},{8,14},{9,15},{10,... | collective-permute-start | bytes 442376 | tf_op jit(solution)/shard_map/exchange_parts/ppermute | solution.py:182
  55.6 1.2 %new_tokens.1 = (f32[128,512]{1,0:T(8,128)S(1)}, f32[8,512]{1,0:T(8,128)S(1)}) custom-call(bf16[64,1024]{1,0:T(8,128)(2,1)S(1)} %get-tuple-element.17.refs_2_.refs_0_, bf16[64,8192]{1,0:T(8,128)(2,1)S(1)} %get-tuple-element.24.refs_1_, bf16[8192,128]{1,0:T(8,128)(2,1)S(1)} %bitcast.18, bf16[8192,128]{1,0:T(8,128)(2,1)S(1)} %bitcast.19, ...), custom_call_target="tpu_custom_call" | custom-call | flops 268435456 | bytes 5242880 | tf_op jit(solution)/shard_map/new_tokens/new_tokens/pallas_call | solution.py:527
  56.7 2.0 %collective-permute-done.15.got_a = bf16[144,512]{1,0:T(8,128)(2,1)S(1)} collective-permute-done((bf16[144,512]{1,0:T(8,128)(2,1)S(1)}, bf16[144,512]{1,0:T(8,128)(2,1)S(1)}, u32[]{:S(2)}, u32[]{:S(2)}) %collective-permute-start.15) | collective-permute-done | bytes 147488 | tf_op jit(solution)/shard_map/exchange_parts/ppermute | solution.py:182
  58.8 1.7 %collective-permute-done.16.got_b = bf16[144,512]{1,0:T(8,128)(2,1)S(1)} collective-permute-done((bf16[144,512]{1,0:T(8,128)(2,1)S(1)}, bf16[144,512]{1,0:T(8,128)(2,1)S(1)}, u32[]{:S(2)}, u32[]{:S(2)}) %collective-permute-start.16) | collective-permute-done | bytes 147488 | tf_op jit(solution)/shard_map/exchange_parts/ppermute | solution.py:182
  60.4 1.8 %collective-permute-done.17.got_c = bf16[144,512]{1,0:T(8,128)(2,1)S(1)} collective-permute-done((bf16[144,512]{1,0:T(8,128)(2,1)S(1)}, bf16[144,512]{1,0:T(8,128)(2,1)S(1)}, u32[]{:S(2)}, u32[]{:S(2)}) %collective-permute-start.17) | collective-permute-done | bytes 147488 | tf_op jit(solution)/shard_map/exchange_parts/ppermute | solution.py:182
  62.3 3.2 %project.1 = (f32[32,8192]{1,0:T(8,128)S(1)}, bf16[32,8192]{1,0:T(8,128)(2,1)S(1)}) custom-call(s32[1]{0:T(128)} %bitcast.1.rank.refs_0_, f32[136,512]{1,0:T(8,128)S(1)} %get-tuple-element.20.kept, bf16[144,512]{1,0:T(8,128)(2,1)S(1)} %collective-permute-done.15.got_a, bf16[144,512]{1,0:T(8,128)(2,1)S(1)} %collective-permute-done.16.got_b, ...), custom_call_target="tpu_custom_call" | custom-call | flops 1073741824 | bytes 18874368 | tf_op jit(solution)/shard_map/project/project/pallas_call | solution.py:562
  65.6 1.9 %collective-permute-done.18 = bf16[32,8192]{1,0:T(8,128)(2,1)S(1)} collective-permute-done((bf16[32,8192]{1,0:T(8,128)(2,1)S(1)}, bf16[32,8192]{1,0:T(8,128)(2,1)S(1)}, u32[]{:S(2)}, u32[]{:S(2)}) %collective-permute-start.18) | collective-permute-done | bytes 524320 | tf_op jit(solution)/shard_map/reduce_cores/ppermute | solution.py:182
  67.6 0.7 collective-permute-start.19
  68.4 1.5 %collective-permute-start.21 = (bf16[8,8192]{1,0:T(8,128)(2,1)S(1)}, bf16[8,8192]{1,0:T(8,128)(2,1)S(1)}, u32[]{:S(2)}, u32[]{:S(2)}) collective-permute-start(bf16[8,8192]{1,0:T(8,128)(2,1)S(1)} %get-tuple-element.32), channel_id=1, source_target_pairs={{0,6},{1,7},{2,4},{3,5},{4,2},{5,3},{6,0},{7,1},{8,14},{9,15},{10,... | collective-permute-start | bytes 393224 | tf_op jit(solution)/shard_map/reduce_chips/ppermute | solution.py:182
  69.8 1.4 %collective-permute-start.20 = (bf16[8,8192]{1,0:T(8,128)(2,1)S(1)}, bf16[8,8192]{1,0:T(8,128)(2,1)S(1)}, u32[]{:S(2)}, u32[]{:S(2)}) collective-permute-start(bf16[8,8192]{1,0:T(8,128)(2,1)S(1)} %get-tuple-element.33), channel_id=1, source_target_pairs={{0,4},{1,5},{2,6},{3,7},{4,0},{5,1},{6,2},{7,3},{8,12},{9,13},{10,... | collective-permute-start | bytes 393224 | tf_op jit(solution)/shard_map/reduce_chips/ppermute | solution.py:182
  71.2 2.9 %collective-permute-done.19 = bf16[8,8192]{1,0:T(8,128)(2,1)S(1)} collective-permute-done((bf16[8,8192]{1,0:T(8,128)(2,1)S(1)}, bf16[8,8192]{1,0:T(8,128)(2,1)S(1)}, u32[]{:S(2)}, u32[]{:S(2)}) %collective-permute-start.19) | collective-permute-done | bytes 131104 | tf_op jit(solution)/shard_map/reduce_chips/ppermute | solution.py:182
  74.0 2.2 %collective-permute-done.21 = bf16[8,8192]{1,0:T(8,128)(2,1)S(1)} collective-permute-done((bf16[8,8192]{1,0:T(8,128)(2,1)S(1)}, bf16[8,8192]{1,0:T(8,128)(2,1)S(1)}, u32[]{:S(2)}, u32[]{:S(2)}) %collective-permute-start.21) | collective-permute-done | bytes 131104 | tf_op jit(solution)/shard_map/reduce_chips/ppermute | solution.py:182
  76.2 1.4 %collective-permute-done.20 = bf16[8,8192]{1,0:T(8,128)(2,1)S(1)} collective-permute-done((bf16[8,8192]{1,0:T(8,128)(2,1)S(1)}, bf16[8,8192]{1,0:T(8,128)(2,1)S(1)}, u32[]{:S(2)}, u32[]{:S(2)}) %collective-permute-start.20) | collective-permute-done | bytes 131104 | tf_op jit(solution)/shard_map/reduce_chips/ppermute | solution.py:182
  77.7 1.8 %collective-permute-start.22 = (bf16[8,8192]{1,0:T(8,128)(2,1)S(1)}, bf16[8,8192]{1,0:T(8,128)(2,1)S(1)}, u32[]{:S(2)}, u32[]{:S(2)}) collective-permute-start(bf16[8,8192]{1,0:T(8,128)(2,1)S(1)} %fusion.3), channel_id=1, source_target_pairs={{24,0},{0,8},{8,16},{16,24},{25,1},{1,9},{9,17},{17,25},{26,2},{2,... | collective-permute-start | bytes 393224 | tf_op jit(solution)/shard_map/hand_on/ppermute | solution.py:20
  79.5 5.1 %collective-permute-done.22 = bf16[8,8192]{1,0:T(8,128)(2,1)S(1)} collective-permute-done((bf16[8,8192]{1,0:T(8,128)(2,1)S(1)}, bf16[8,8192]{1,0:T(8,128)(2,1)S(1)}, u32[]{:S(2)}, u32[]{:S(2)}) %collective-permute-start.22) | collective-permute-done | bytes 131104 | tf_op jit(solution)/shard_map/hand_on/ppermute | solution.py:20
  84.5 0.7 copy.13
  (56 shorter events, 4.8 us)
Async XLA Ops:
  0.0 8.1 %collective-permute-start.5 = (bf16[8,8192]{1,0:T(8,128)(2,1)}, bf16[8,8192]{1,0:T(8,128)(2,1)S(1)}, u32[]{:S(2)}, u32[]{:S(2)}) collective-permute-start(bf16[8,8192]{1,0:T(8,128)(2,1)} %bitcast.20), channel_id=1, source_target_pairs={{0,6},{1,7},{2,4},{3,5},{4,2},{5,3},{6,0},{7,1},{8,14},{9,15},{10,... | collective-permute-start | bytes 393224 | tf_op jit(solution)/shard_map/gather_tokens/ppermute | solution.py:182
  3.9 6.5 %collective-permute-start.3 = (bf16[8,8192]{1,0:T(8,128)(2,1)}, bf16[8,8192]{1,0:T(8,128)(2,1)S(1)}, u32[]{:S(2)}, u32[]{:S(2)}) collective-permute-start(bf16[8,8192]{1,0:T(8,128)(2,1)} %bitcast.21), channel_id=1, source_target_pairs={{0,4},{1,5},{2,6},{3,7},{4,0},{5,1},{6,2},{7,3},{8,12},{9,13},{10,... | collective-permute-start | bytes 393224 | tf_op jit(solution)/shard_map/gather_tokens/ppermute | solution.py:182
  4.4 6.3 %collective-permute-start.1 = (bf16[8,8192]{1,0:T(8,128)(2,1)}, bf16[8,8192]{1,0:T(8,128)(2,1)S(1)}, u32[]{:S(2)}, u32[]{:S(2)}) collective-permute-start(bf16[8,8192]{1,0:T(8,128)(2,1)} %bitcast.22), channel_id=1, source_target_pairs={{0,2},{1,3},{2,0},{3,1},{4,6},{5,7},{6,4},{7,5},{8,10},{9,11},{10,... | collective-permute-start | bytes 393224 | tf_op jit(solution)/shard_map/gather_tokens/ppermute | solution.py:182
  4.5 6.8 %collective-permute-start = (bf16[8,8192]{1,0:T(8,128)(2,1)}, bf16[8,8192]{1,0:T(8,128)(2,1)S(1)}, u32[]{:S(2)}, u32[]{:S(2)}) collective-permute-start(bf16[8,8192]{1,0:T(8,128)(2,1)} %bitcast.23), channel_id=1, source_target_pairs={{0,1},{1,0},{2,3},{3,2},{4,5},{5,4},{6,7},{7,6},{8,9},{9,8},{10,11... | collective-permute-start | bytes 393224 | tf_op jit(solution)/shard_map/gather_tokens/ppermute | solution.py:182
  8.1 3.1 %collective-permute-start.6 = (bf16[8,8192]{1,0:T(8,128)(2,1)S(1)}, bf16[8,8192]{1,0:T(8,128)(2,1)S(1)}, u32[]{:S(2)}, u32[]{:S(2)}) collective-permute-start(bf16[8,8192]{1,0:T(8,128)(2,1)S(1)} %collective-permute-done.5.refs_6_), channel_id=1, source_target_pairs={{0,1},{1,0},{2,3},{3,2},{4,5},{5,4},{6,7},{7,6},{8,9},{9,8},{10,11... | collective-permute-start | bytes 393224 | tf_op jit(solution)/shard_map/gather_tokens/ppermute | solution.py:182
  10.4 1.3 %collective-permute-start.4 = (bf16[8,8192]{1,0:T(8,128)(2,1)S(1)}, bf16[8,8192]{1,0:T(8,128)(2,1)S(1)}, u32[]{:S(2)}, u32[]{:S(2)}) collective-permute-start(bf16[8,8192]{1,0:T(8,128)(2,1)S(1)} %collective-permute-done.3.refs_4_), channel_id=1, source_target_pairs={{0,1},{1,0},{2,3},{3,2},{4,5},{5,4},{6,7},{7,6},{8,9},{9,8},{10,11... | collective-permute-start | bytes 393224 | tf_op jit(solution)/shard_map/gather_tokens/ppermute | solution.py:182
  10.7 1.3 %collective-permute-start.2 = (bf16[8,8192]{1,0:T(8,128)(2,1)S(1)}, bf16[8,8192]{1,0:T(8,128)(2,1)S(1)}, u32[]{:S(2)}, u32[]{:S(2)}) collective-permute-start(bf16[8,8192]{1,0:T(8,128)(2,1)S(1)} %collective-permute-done.1.refs_2_), channel_id=1, source_target_pairs={{0,1},{1,0},{2,3},{3,2},{4,5},{5,4},{6,7},{7,6},{8,9},{9,8},{10,11... | collective-permute-start | bytes 393224 | tf_op jit(solution)/shard_map/gather_tokens/ppermute | solution.py:182
  19.4 7.0 %copy-start.1 = (bf16[1,2048,8,128]{3,2,1,0:T(8,128)(2,1)S(1)}, bf16[1,2048,8,128]{3,2,1,0:T(8,128)(2,1)}, u32[]{:S(2)}) copy-start(bf16[1,2048,8,128]{3,2,1,0:T(8,128)(2,1)} %param.16) | copy-start | bytes 12582916
  19.4 7.0 %copy-start.2 = (bf16[1,2048,8,128]{3,2,1,0:T(8,128)(2,1)S(1)}, bf16[1,2048,8,128]{3,2,1,0:T(8,128)(2,1)}, u32[]{:S(2)}) copy-start(bf16[1,2048,8,128]{3,2,1,0:T(8,128)(2,1)} %param.17) | copy-start | bytes 12582916
  23.0 6.3 %collective-permute-start.13 = (bf16[64,1024]{1,0:T(8,128)(2,1)S(1)}, bf16[64,1024]{1,0:T(8,128)(2,1)S(1)}, u32[]{:S(2)}, u32[]{:S(2)}) collective-permute-start(bf16[64,1024]{1,0:T(8,128)(2,1)S(1)} %get-tuple-element.17.refs_2_.refs_0_), channel_id=1, source_target_pairs={{0,1},{1,0},{2,3},{3,2},{4,5},{5,4},{6,7},{7,6},{8,9},{9,8},{10,11... | collective-permute-start | bytes 393224 | tf_op jit(solution)/shard_map/gather_queries/ppermute | solution.py:182
  23.4 6.4 %collective-permute-start.11 = (bf16[64,1024]{1,0:T(8,128)(2,1)S(1)}, bf16[64,1024]{1,0:T(8,128)(2,1)S(1)}, u32[]{:S(2)}, u32[]{:S(2)}) collective-permute-start(bf16[64,1024]{1,0:T(8,128)(2,1)S(1)} %get-tuple-element.17.refs_2_.refs_0_), channel_id=1, source_target_pairs={{0,7},{1,6},{2,5},{3,4},{4,3},{5,2},{6,1},{7,0},{8,15},{9,14},{10,... | collective-permute-start | bytes 393224 | tf_op jit(solution)/shard_map/gather_queries/ppermute | solution.py:182
  24.9 7.9 %collective-permute-start.9 = (bf16[64,1024]{1,0:T(8,128)(2,1)S(1)}, bf16[64,1024]{1,0:T(8,128)(2,1)S(1)}, u32[]{:S(2)}, u32[]{:S(2)}) collective-permute-start(bf16[64,1024]{1,0:T(8,128)(2,1)S(1)} %get-tuple-element.17.refs_2_.refs_0_), channel_id=1, source_target_pairs={{0,5},{1,4},{2,7},{3,6},{4,1},{5,0},{6,3},{7,2},{8,13},{9,12},{10,... | collective-permute-start | bytes 393224 | tf_op jit(solution)/shard_map/gather_queries/ppermute | solution.py:182
  26.2 6.7 %collective-permute-start.7 = (bf16[64,1024]{1,0:T(8,128)(2,1)S(1)}, bf16[64,1024]{1,0:T(8,128)(2,1)S(1)}, u32[]{:S(2)}, u32[]{:S(2)}) collective-permute-start(bf16[64,1024]{1,0:T(8,128)(2,1)S(1)} %get-tuple-element.17.refs_2_.refs_0_), channel_id=1, source_target_pairs={{0,3},{1,2},{2,1},{3,0},{4,7},{5,6},{6,5},{7,4},{8,11},{9,10},{10,... | collective-permute-start | bytes 393224 | tf_op jit(solution)/shard_map/gather_queries/ppermute | solution.py:182
  26.4 35.8 %slice-start = ((s8[16777216]{0:T(1024)(128)(4,1)}), s8[4194304]{0:T(1024)(128)(4,1)S(1)}, s32[]{:S(2)}) async-start(s8[16777216]{0:T(1024)(128)(4,1)} %bitcast.13), calls=%async_computation | async-start | bytes 8388608
  32.9 29.3 %slice-start.1 = ((s8[16777216]{0:T(1024)(128)(4,1)}), s8[4194304]{0:T(1024)(128)(4,1)S(1)}, s32[]{:S(2)}) async-start(s8[16777216]{0:T(1024)(128)(4,1)} %bitcast.13), calls=%async_computation.1 | async-start | bytes 8388608
  32.9 29.3 %slice-start.2 = ((s8[16777216]{0:T(1024)(128)(4,1)}), s8[4194304]{0:T(1024)(128)(4,1)S(1)}, s32[]{:S(2)}) async-start(s8[16777216]{0:T(1024)(128)(4,1)} %bitcast.13), calls=%async_computation.2 | async-start | bytes 8388608
  40.9 14.7 %copy-start.3 = (bf16[1,8192,128]{2,1,0:T(8,128)(2,1)S(1)}, bf16[1,8192,128]{2,1,0:T(8,128)(2,1)}, u32[]{:S(2)}) copy-start(bf16[1,8192,128]{2,1,0:T(8,128)(2,1)} %param.13) | copy-start | bytes 6291460
  40.9 14.7 %copy-start.4 = (bf16[1,8192,128]{2,1,0:T(8,128)(2,1)S(1)}, bf16[1,8192,128]{2,1,0:T(8,128)(2,1)}, u32[]{:S(2)}) copy-start(bf16[1,8192,128]{2,1,0:T(8,128)(2,1)} %param.14) | copy-start | bytes 6291460
  40.9 21.3 %slice-start.3 = ((s8[16777216]{0:T(1024)(128)(4,1)}), s8[4194304]{0:T(1024)(128)(4,1)S(1)}, s32[]{:S(2)}) async-start(s8[16777216]{0:T(1024)(128)(4,1)} %bitcast.13), calls=%async_computation.3 | async-start | bytes 8388608
  40.9 10.8 %collective-permute-start.14 = (bf16[4,144,512]{2,1,0:T(8,128)(2,1)S(1)}, bf16[4,144,512]{2,1,0:T(8,128)(2,1)S(1)}, u32[]{:S(2)}, u32[]{:S(2)}) collective-permute-start(bf16[4,144,512]{2,1,0:T(8,128)(2,1)S(1)} %cache_odd.1), channel_id=1, source_target_pairs={{0,1},{1,0},{2,3},{3,2},{4,5},{5,4},{6,7},{7,6},{8,9},{9,8},{10,11... | collective-permute-start | bytes 1769480 | tf_op jit(solution)/shard_map/swap_odd/ppermute | solution.py:182
  41.1 2.1 %collective-permute-start.12 = (bf16[64,1024]{1,0:T(8,128)(2,1)S(1)}, bf16[64,1024]{1,0:T(8,128)(2,1)S(1)}, u32[]{:S(2)}, u32[]{:S(2)}) collective-permute-start(bf16[64,1024]{1,0:T(8,128)(2,1)S(1)} %collective-permute-done.11.refs_5_), channel_id=1, source_target_pairs={{0,1},{1,0},{2,3},{3,2},{4,5},{5,4},{6,7},{7,6},{8,9},{9,8},{10,11... | collective-permute-start | bytes 393224 | tf_op jit(solution)/shard_map/gather_queries/ppermute | solution.py:182
  41.5 1.9 %collective-permute-start.10 = (bf16[64,1024]{1,0:T(8,128)(2,1)S(1)}, bf16[64,1024]{1,0:T(8,128)(2,1)S(1)}, u32[]{:S(2)}, u32[]{:S(2)}) collective-permute-start(bf16[64,1024]{1,0:T(8,128)(2,1)S(1)} %collective-permute-done.9.refs_4_), channel_id=1, source_target_pairs={{0,1},{1,0},{2,3},{3,2},{4,5},{5,4},{6,7},{7,6},{8,9},{9,8},{10,11... | collective-permute-start | bytes 393224 | tf_op jit(solution)/shard_map/gather_queries/ppermute | solution.py:182
  41.6 1.9 %collective-permute-start.8 = (bf16[64,1024]{1,0:T(8,128)(2,1)S(1)}, bf16[64,1024]{1,0:T(8,128)(2,1)S(1)}, u32[]{:S(2)}, u32[]{:S(2)}) collective-permute-start(bf16[64,1024]{1,0:T(8,128)(2,1)S(1)} %collective-permute-done.7.refs_3_), channel_id=1, source_target_pairs={{0,1},{1,0},{2,3},{3,2},{4,5},{5,4},{6,7},{7,6},{8,9},{9,8},{10,11... | collective-permute-start | bytes 393224 | tf_op jit(solution)/shard_map/gather_queries/ppermute | solution.py:182
  52.0 6.8 %collective-permute-start.15 = (bf16[144,512]{1,0:T(8,128)(2,1)S(1)}, bf16[144,512]{1,0:T(8,128)(2,1)S(1)}, u32[]{:S(2)}, u32[]{:S(2)}) collective-permute-start(bf16[144,512]{1,0:T(8,128)(2,1)S(1)} %get-tuple-element.21), channel_id=1, source_target_pairs={{0,2},{1,3},{2,0},{3,1},{4,6},{5,7},{6,4},{7,5},{8,10},{9,11},{10,... | collective-permute-start | bytes 442376 | tf_op jit(solution)/shard_map/exchange_parts/ppermute | solution.py:182
  52.1 8.3 %collective-permute-start.16 = (bf16[144,512]{1,0:T(8,128)(2,1)S(1)}, bf16[144,512]{1,0:T(8,128)(2,1)S(1)}, u32[]{:S(2)}, u32[]{:S(2)}) collective-permute-start(bf16[144,512]{1,0:T(8,128)(2,1)S(1)} %get-tuple-element.22), channel_id=1, source_target_pairs={{0,4},{1,5},{2,6},{3,7},{4,0},{5,1},{6,2},{7,3},{8,12},{9,13},{10,... | collective-permute-start | bytes 442376 | tf_op jit(solution)/shard_map/exchange_parts/ppermute | solution.py:182
  53.8 8.4 %collective-permute-start.17 = (bf16[144,512]{1,0:T(8,128)(2,1)S(1)}, bf16[144,512]{1,0:T(8,128)(2,1)S(1)}, u32[]{:S(2)}, u32[]{:S(2)}) collective-permute-start(bf16[144,512]{1,0:T(8,128)(2,1)S(1)} %get-tuple-element.23), channel_id=1, source_target_pairs={{0,6},{1,7},{2,4},{3,5},{4,2},{5,3},{6,0},{7,1},{8,14},{9,15},{10,... | collective-permute-start | bytes 442376 | tf_op jit(solution)/shard_map/exchange_parts/ppermute | solution.py:182
  62.2 15.4 %copy-start.6 = (bf16[1,8,8192]{2,1,0:T(8,128)(2,1)S(1)}, bf16[1,8,8192]{2,1,0:T(8,128)(2,1)}, u32[]{:S(2)}) copy-start(bf16[1,8,8192]{2,1,0:T(8,128)(2,1)} %param.10) | copy-start | bytes 393220
  65.5 2.0 %collective-permute-start.18 = (bf16[32,8192]{1,0:T(8,128)(2,1)S(1)}, bf16[32,8192]{1,0:T(8,128)(2,1)S(1)}, u32[]{:S(2)}, u32[]{:S(2)}) collective-permute-start(bf16[32,8192]{1,0:T(8,128)(2,1)S(1)} %get-tuple-element.28), channel_id=1, source_target_pairs={{0,1},{1,0},{2,3},{3,2},{4,5},{5,4},{6,7},{7,6},{8,9},{9,8},{10,11... | collective-permute-start | bytes 1572872 | tf_op jit(solution)/shard_map/reduce_cores/ppermute | solution.py:182
  67.6 6.4 %collective-permute-start.19 = (bf16[8,8192]{1,0:T(8,128)(2,1)S(1)}, bf16[8,8192]{1,0:T(8,128)(2,1)S(1)}, u32[]{:S(2)}, u32[]{:S(2)}) collective-permute-start(bf16[8,8192]{1,0:T(8,128)(2,1)S(1)} %get-tuple-element.31), channel_id=1, source_target_pairs={{0,2},{1,3},{2,0},{3,1},{4,6},{5,7},{6,4},{7,5},{8,10},{9,11},{10,... | collective-permute-start | bytes 393224 | tf_op jit(solution)/shard_map/reduce_chips/ppermute | solution.py:182
  68.4 7.9 %collective-permute-start.21 = (bf16[8,8192]{1,0:T(8,128)(2,1)S(1)}, bf16[8,8192]{1,0:T(8,128)(2,1)S(1)}, u32[]{:S(2)}, u32[]{:S(2)}) collective-permute-start(bf16[8,8192]{1,0:T(8,128)(2,1)S(1)} %get-tuple-element.32), channel_id=1, source_target_pairs={{0,6},{1,7},{2,4},{3,5},{4,2},{5,3},{6,0},{7,1},{8,14},{9,15},{10,... | collective-permute-start | bytes 393224 | tf_op jit(solution)/shard_map/reduce_chips/ppermute | solution.py:182
  69.8 7.8 %collective-permute-start.20 = (bf16[8,8192]{1,0:T(8,128)(2,1)S(1)}, bf16[8,8192]{1,0:T(8,128)(2,1)S(1)}, u32[]{:S(2)}, u32[]{:S(2)}) collective-permute-start(bf16[8,8192]{1,0:T(8,128)(2,1)S(1)} %get-tuple-element.33), channel_id=1, source_target_pairs={{0,4},{1,5},{2,6},{3,7},{4,0},{5,1},{6,2},{7,3},{8,12},{9,13},{10,... | collective-permute-start | bytes 393224 | tf_op jit(solution)/shard_map/reduce_chips/ppermute | solution.py:182
  77.7 6.8 %collective-permute-start.22 = (bf16[8,8192]{1,0:T(8,128)(2,1)S(1)}, bf16[8,8192]{1,0:T(8,128)(2,1)S(1)}, u32[]{:S(2)}, u32[]{:S(2)}) collective-permute-start(bf16[8,8192]{1,0:T(8,128)(2,1)S(1)} %fusion.3), channel_id=1, source_target_pairs={{24,0},{0,8},{8,16},{16,24},{25,1},{1,9},{9,17},{17,25},{26,2},{2,... | collective-permute-start | bytes 393224 | tf_op jit(solution)/shard_map/hand_on/ppermute | solution.py:20
  (4 other events, 13.9 us)

commit v2 on v1

--- a/solution.py
+++ b/solution.py
@@ -182,7 +182,7 @@
     return lax.ppermute(block, "seq", [(i, i ^ bits) for i in range(n)])
 
 
-def call(kernel, name, out_shape, in_specs, flops=0, nbytes=0, scratch=(), vmem=16, **grid):
+def call(kernel, name, out_shape, in_specs, flops=0, nbytes=0, scratch=(), vmem=6, **grid):
     out_specs = grid.pop("out_specs", jax.tree.map(lambda _: IN_VMEM, out_shape))
     return pl.pallas_call(
         kernel,
@@ -201,32 +201,21 @@
     return pltpu.with_memory_space_constraint(array, pltpu.VMEM)
 
 
-def by_head_kernel(keys, values, keys_out, values_out):
-    keys_out[...] = jnp.swapaxes(keys[...], 0, 1)
-    turned = jnp.swapaxes(values[...], 0, 1)
-    for g in range(turned.shape[0]):
-        values_out[g] = turned[g].T
-
-
-def cache_by_head(keys, values):
-    ctx, heads, dim = keys.shape
-    block = 256
-    source = pl.BlockSpec((block, heads, dim), lambda i: (i, 0, 0))
+def join_kernel(count, *refs):
+    for i in range(count):
+        refs[-1][i] = refs[i][...]
+
+
+def joined_after(blocks, done, name):
+    count = len(blocks)
     return call(
-        by_head_kernel,
-        "cache_by_head",
-        [
-            jax.ShapeDtypeStruct((heads, ctx, dim), jnp.bfloat16),
-            jax.ShapeDtypeStruct((heads, dim, ctx), jnp.bfloat16),
-        ],
-        [source, source],
-        nbytes=4 * ctx * heads * dim * 2,
-        grid=(ctx // block,),
-        out_specs=[
-            pl.BlockSpec((heads, block, dim), lambda i: (0, i, 0)),
-            pl.BlockSpec((heads, dim, block), lambda i: (0, 0, i)),
-        ],
-    )(keys, values)
+        lambda *refs: join_kernel(count, *refs),
+        name,
+        jax.ShapeDtypeStruct((count, *blocks[0].shape), blocks[0].dtype),
+        [IN_VMEM] * count + [pl.BlockSpec(memory_space=pl.ANY)] * len(done),
+        nbytes=MIB,
+        vmem=2,
+    )(*blocks, *done)
 
 
 def rotated(heads, cosine, sine):
@@ -235,10 +224,11 @@
 
 
 def query_kernel(rank, *refs):
-    blocks = refs[:8]
-    gain, cosine, sine, weights, query, normed, rows = refs[8:]
+    mine, near, far, far_near = refs[:4]
+    gain, cosine, sine, weights, query, normed, rows = refs[4:]
     width = rows.shape[1]
-    count = blocks[0].shape[0]
+    count = mine.shape[0]
+    blocks = [mine, near] + [part.at[i] for i in range(3) for part in (far, far_near)]
     step = 1024
     for bits in range(8):
         at = pl.multiple_of((rank[0] ^ bits) * count, count)
@@ -273,7 +263,57 @@
     return lax.dot_general(a, b, (((1,), (1,)), ((), ())), preferred_element_type=jnp.float32)
 
 
-def new_kernel(scale, query, normed, w_key, w_value, cosine, sine, summed, stats):
+def keys_kernel(rank, keys, keys_out, done):
+    keys_out[...] = jnp.swapaxes(keys[...], 0, 1)
+    done[...] = jnp.zeros_like(done)
+
+
+def keys_by_head(rank, keys):
+    ctx, heads, dim = keys.shape
+    block = 256
+    return call(
+        keys_kernel,
+        "keys_by_head",
+        [
+            jax.ShapeDtypeStruct((heads, ctx, dim), jnp.bfloat16),
+            jax.ShapeDtypeStruct((8, 128), jnp.float32),
+        ],
+        [IN_SMEM, pl.BlockSpec((block, heads, dim), lambda i: (i, 0, 0))],
+        flops=10**10,
+        nbytes=2 * ctx * heads * dim * 2,
+        grid=(ctx // block,),
+        out_specs=[
+            pl.BlockSpec((heads, block, dim), lambda i: (0, i, 0)),
+            pl.BlockSpec((8, 128), lambda i: (0, 0)),
+        ],
+    )(rank, pltpu.with_memory_space_constraint(keys, pltpu.HBM))
+
+
+def values_by_head(values, values_out):
+    block = 256
+
+    @pl.loop(0, values.shape[0] // block)
+    def _(i):
+        at = pl.ds(pl.multiple_of(i * block, block), block)
+        turned = jnp.swapaxes(values[at], 0, 1)
+        for g in range(turned.shape[0]):
+            values_out[g, :, at] = turned[g].T
+
+
+def new_kernel(
+    scale,
+    query,
+    normed,
+    w_key,
+    w_value,
+    cosine,
+    sine,
+    cached_values,
+    values_out,
+    summed,
+    stats,
+):
+    values_by_head(cached_values, values_out)
     tok, dim = cosine.shape
     heads = query.shape[1] // dim
     raw = jnp.dot(normed[...], w_key[...], preferred_element_type=jnp.float32)
@@ -313,99 +353,118 @@
 
 
 def cache_kernel(scale, order, rank, mask, *refs):
-    queries = refs[:4]
-    keys, values, out, q_rows, summed, visible = refs[4:]
+    n = len(order)
+    given = 1 if len(refs[0].shape) == 3 else n
+    queries, (keys, values), outs = refs[:given], refs[given : given + 2], refs[given + 2 : -3]
+    if given < n:
+        queries = [queries[0].at[i] for i in range(n)]
+    q_rows, summed, visible = refs[-3:]
     dim = keys.shape[2]
     heads = queries[0].shape[1] // dim
     cols = heads * QB
-    tail = out.shape[1] - dim
     groups = [rank[0] ^ bits for bits in order]
+    own = [bits for bits in order if bits in EVEN]
     for q_block in range(mask.shape[0]):
         count = jnp.int32(0)
         for b in range(mask.shape[1]):
             visible[count] = b
             count = count + (mask[q_block, b] > 0).astype(jnp.int32)
         visible[count] = 0
-        for i in range(4):
+        for i in range(n):
             q_rows[i] = query_rows(queries[i], q_block, heads, dim)
             summed[i] = jnp.zeros((dim, cols), jnp.float32)
 
         def step(pair, carry):
-            at_first = pl.multiple_of(visible[2 * pair] * KB, KB)
-            at_second = pl.multiple_of(visible[2 * pair + 1] * KB, KB)
+            at = [pl.multiple_of(visible[2 * pair + e] * KB, KB) for e in range(2)]
             hidden = jnp.where(2 * pair + 1 < count, jnp.float32(0.0), jnp.float32(neg_fill))
-            after = []
-            for i in range(4):
+            scores = [
+                matmul_nt(
+                    jnp.concatenate([keys[g, pl.ds(a, KB), :] for a in at], axis=0), q_rows[i]
+                )
+                for i, g in enumerate(groups)
+            ]
+            levels, scaled = [], []
+            for i in range(n):
                 top, total = carry[2 * i], carry[2 * i + 1]
-                g = groups[i]
-                first = matmul_nt(keys[g, pl.ds(at_first, KB), :], q_rows[i]) * scale
-                second = matmul_nt(keys[g, pl.ds(at_second, KB), :], q_rows[i]) * scale + hidden
+                first = scores[i][:KB] * scale
+                second = scores[i][KB:] * scale + hidden
                 new_top = jnp.maximum(
-                    top,
-                    jnp.maximum(
-                        jnp.max(first, axis=0, keepdims=True),
-                        jnp.max(second, axis=0, keepdims=True),
-                    ),
+                    top, jnp.max(jnp.maximum(first, second), axis=0, keepdims=True)
                 )
                 first = jnp.exp2(first - new_top)
                 second = jnp.exp2(second - new_top)
                 factor = jnp.exp2(top - new_top)
-                total = (
-                    total * factor
-                    + jnp.sum(first, axis=0, keepdims=True)
-                    + jnp.sum(second, axis=0, keepdims=True)
+                total = total * factor + jnp.sum(first + second, axis=0, keepdims=True)
+                levels += [new_top, total]
+                weights = jnp.concatenate(
+                    [first.astype(jnp.bfloat16), second.astype(jnp.bfloat16)], axis=0
                 )
-                weights = jnp.concatenate([first, second], axis=0).astype(jnp.bfloat16)
-                block = jnp.concatenate(
-                    [values[g, :, pl.ds(at_first, KB)], values[g, :, pl.ds(at_second, KB)]], axis=1
+                scaled.append((factor, weights))
+            products = [
+                jnp.dot(
+                    jnp.concatenate([values[g, :, pl.ds(a, KB)] for a in at], axis=1),
+                    scaled[i][1],
+                    preferred_element_type=jnp.float32,
                 )
-                summed[i] = summed[i] * factor + jnp.dot(
-                    block, weights, preferred_element_type=jnp.float32
-                )
-                after += [new_top, total]
-            return tuple(after)
-
-        start = (jnp.full((1, cols), neg_fill, jnp.float32), jnp.zeros((1, cols), jnp.float32)) * 4
+                for i, g in enumerate(groups)
+            ]
+            for i in range(n):
+                summed[i] = summed[i] * scaled[i][0] + products[i]
+            return tuple(levels)
+
+        start = (jnp.full((1, cols), neg_fill, jnp.float32), jnp.zeros((1, cols), jnp.float32)) * n
         ended = lax.fori_loop(0, (count + 1) // 2, step, start)
         at = slice(q_block * cols, (q_block + 1) * cols)
-        for i in range(4):
+        for i, bits in enumerate(order):
             top, total = ended[2 * i], ended[2 * i + 1]
             seen = total > 0.0
             safe = jnp.where(seen, total, 1.0)
             level = jnp.where(seen, top + jnp.log2(safe), neg_fill)
-            out[i, 0:dim, at] = (summed[i] / safe).astype(out.dtype)
-            out[i, dim:, at] = split_rows(level, tail).astype(out.dtype)
-
-
-def cache_part(scale, order, rank, mask, queries, keys, values, dtype, name):
+            if bits in EVEN:
+                out, place = outs[0], own.index(bits)
+            else:
+                out, place = outs[-1], i - len(own)
+            out[place, 0:dim, at] = (summed[i] / safe).astype(out.dtype)
+            out[place, dim:, at] = split_rows(level, out.shape[1] - dim).astype(out.dtype)
+
+
+def cache_part(scale, order, rank, mask, queries, keys, values, name):
     heads, ctx, dim = keys.shape
-    cols = (queries[0].shape[1] // dim) * QB
-    tail = 16 if dtype == jnp.bfloat16 else 8
+    cols = (queries[0].shape[-1] // dim) * QB
+    n = len(order)
+    own = len([bits for bits in order if bits in EVEN])
+    outs = []
+    if own:
+        outs.append(jax.ShapeDtypeStruct((own, dim + 8, mask.shape[0] * cols), jnp.float32))
+    if n > own:
+        outs.append(jax.ShapeDtypeStruct((n - own, dim + 16, mask.shape[0] * cols), jnp.bfloat16))
     return call(
         lambda *refs: cache_kernel(scale, order, *refs),
         name,
-        jax.ShapeDtypeStruct((4, dim + tail, mask.shape[0] * cols), dtype),
-        [IN_SMEM, IN_SMEM] + [IN_VMEM] * 6,
-        flops=4 * 4 * queries[0].shape[0] * heads * ctx * dim // 4,
-        nbytes=4 * MIB,
+        outs,
+        [IN_SMEM, IN_SMEM] + [IN_VMEM] * (len(queries) + 2),
+        flops=(2 if own else 10) * n * queries[0].shape[-2] * heads * ctx * dim,
+        nbytes=n * MIB,
         scratch=[
-            pltpu.VMEM((4, cols, dim), jnp.bfloat16),
-            pltpu.VMEM((4, dim, cols), jnp.float32),
+            pltpu.VMEM((n, cols, dim), jnp.bfloat16),
+            pltpu.VMEM((n, dim, cols), jnp.float32),
             pltpu.SMEM((mask.shape[1] + 2,), jnp.int32),
         ],
     )(rank, mask, *queries, held(keys), held(values))
 
 
-def merge_kernel(own, got, kept, *sent):
-    dim = own.shape[1] - 8
+def merge_kernel(own_first, own_rest, got_first, got_rest, kept, *sent):
+    dim = own_first.shape[1] - 8
     for i in range(4):
-        mine, other = level_of(own[i, dim:, :]), level_of(got[i, dim:, :])
+        own = own_first.at[0] if i == 0 else own_rest.at[i - 1]
+        got = got_first.at[0] if i == 0 else got_rest.at[i - 1]
+        mine, other = level_of(own[dim:, :]), level_of(got[dim:, :])
         top = jnp.maximum(mine, other)
         mine, other = jnp.exp2(mine - top), jnp.exp2(other - top)
         total = mine + other
         level = top + jnp.log2(total)
         mine, other = mine / total, other / total
-        joined = own[i, :dim, :] * mine + got[i, :dim, :].astype(jnp.float32) * other
+        joined = own[:dim, :] * mine + got[:dim, :].astype(jnp.float32) * other
         target = kept if i == 0 else sent[i - 1]
         target[:dim, :] = joined.astype(target.dtype)
         target[dim:, :] = split_rows(level, target.shape[0] - dim).astype(target.dtype)
@@ -474,13 +533,15 @@
     scale = dim ** (-0.5) * log2e
     mask = cache_mask[0]
 
+    with jax.named_scope("cache_layout"):
+        keys, layout_done = keys_by_head(rank, key_cache[0])
     with jax.named_scope("gather_tokens"):
         blocks = {0: tokens[0]}
         blocks[1] = swapped(tokens[0], 1)
         for bits in SAME_CORE:
             blocks[bits] = swapped(tokens[0], bits)
-        for bits in SAME_CORE:
-            blocks[bits ^ 1] = swapped(blocks[bits], 1)
+        far = joined_after([blocks[bits] for bits in SAME_CORE], [layout_done], "join_tokens")
+        far_near = swapped(far, 1)
 
     with jax.named_scope("tables"):
         positions = span_offset[0].astype(jnp.float32) + jnp.arange(tok, dtype=jnp.int32).astype(
@@ -491,9 +552,6 @@
         cosine, sine = jnp.cos(angles), jnp.sin(angles)
         cosine = jnp.concatenate([cosine, cosine], axis=1)
         sine = jnp.concatenate([-sine, sine], axis=1)
-
-    with jax.named_scope("cache_layout"):
-        keys, values = cache_by_head(key_cache[0], cached_value_rows[0])
 
     with jax.named_scope("queries"):
         query, normed = call(
@@ -503,13 +561,16 @@
                 jax.ShapeDtypeStruct((tok, own_cols), jnp.bfloat16),
                 jax.ShapeDtypeStruct((tok, width), jnp.bfloat16),
             ],
-            [IN_SMEM] + [IN_VMEM] * 12,
-            flops=2 * tok * width * own_cols,
+            [IN_SMEM] + [IN_VMEM] * 8,
+            flops=8 * tok * width * own_cols // 2,
             nbytes=16 * MIB,
             scratch=[pltpu.VMEM((tok, width), jnp.float32)],
         )(
             rank,
-            *[blocks[bits] for bits in range(8)],
+            blocks[0],
+            blocks[1],
+            far,
+            far_near,
             norm_gain,
             cosine,
             sine,
@@ -520,32 +581,42 @@
         queries = {0: query}
         for bits in ODD:
             queries[bits] = swapped(query, bits)
-        for bits in SAME_CORE:
-            queries[bits] = swapped(queries[bits ^ 1], 1)
-
     with jax.named_scope("new_tokens"):
-        summed, stats = call(
+        heads, ctx = key_cache.shape[2], key_cache.shape[1]
+        values, summed, stats = call(
             lambda *refs: new_kernel(scale, *refs),
             "new_tokens",
             [
+                jax.ShapeDtypeStruct((heads, dim, ctx), jnp.bfloat16),
                 jax.ShapeDtypeStruct((dim, tok * own_cols // dim), jnp.float32),
                 jax.ShapeDtypeStruct((8, tok * own_cols // dim), jnp.float32),
             ],
-            [IN_VMEM] * 6,
-            flops=4 * tok * width * dim,
-            nbytes=5 * MIB,
-        )(query, normed, held(key_projection[0]), held(value_projection[0]), cosine, sine)
-
+            [IN_VMEM] * 7,
+            flops=64 * tok * width * dim,
+            nbytes=13 * MIB,
+        )(
+            query,
+            normed,
+            held(key_projection[0]),
+            held(value_projection[0]),
+            cosine,
+            sine,
+            held(cached_value_rows[0]),
+        )
+
+    with jax.named_scope("cache_near"):
+        near_own, near_sent = cache_part(
+            scale, (0, 1), rank, mask, [queries[0], queries[1]], keys, values, "cache_near"
+        )
+        near_got = swapped(near_sent, 1)
+    with jax.named_scope("gather_queries"):
+        far_odd = joined_after([queries[bits] for bits in ODD[1:]], [near_own], "join_queries")
+        far_even = swapped(far_odd, 1)
     with jax.named_scope("cache_odd"):
-        odd = cache_part(
-            scale, ODD, rank, mask, [queries[b] for b in ODD], keys, values, jnp.bfloat16, "cache_odd"
-        )
-    with jax.named_scope("swap_odd"):
-        got = swapped(odd, 1)
+        (odd,) = cache_part(scale, ODD[1:], rank, mask, [far_odd], keys, values, "cache_odd")
+        odd_got = swapped(odd, 1)
     with jax.named_scope("cache_even"):
-        even = cache_part(
-            scale, EVEN, rank, mask, [queries[b] for b in EVEN], keys, values, jnp.float32, "cache_even"
-        )
+        (even,) = cache_part(scale, EVEN[1:], rank, mask, [far_even], keys, values, "cache_even")
     with jax.named_scope("merge_cores"):
         cols = even.shape[2]
         kept, *sent = call(
@@ -553,9 +624,9 @@
             "merge_cores",
             [jax.ShapeDtypeStruct((dim + 8, cols), jnp.float32)]
             + [jax.ShapeDtypeStruct((dim + 16, cols), jnp.bfloat16)] * 3,
-            [IN_VMEM] * 2,
+            [IN_VMEM] * 4,
             nbytes=2 * MIB,
-        )(even, got)
+        )(near_own, even, near_got, odd_got)
     with jax.named_scope("exchange_parts"):
         parts = [swapped(block, bits) for block, bits in zip(sent, SAME_CORE)]
     with jax.named_scope("project"):
@@ -567,7 +638,7 @@
                 jax.ShapeDtypeStruct((tok // 2, width), jnp.bfloat16),
             ],
             [IN_SMEM] + [IN_VMEM] * 7,
-            flops=2 * tok * width * own_cols,
+            flops=8 * tok * width * own_cols // 2,
             nbytes=18 * MIB,
             scratch=[
                 pltpu.VMEM((tok, own_cols), jnp.float32),

time: 85.7 us -> 72.1 us (0.84); the launches traced: 85.2 us -> 73 us
  waiting for transfers between devices: 30.2 us -> 21.7 us
  local copies, waits for them, and re-layouts: 8.16 us -> 0.76 us
  Pallas kernels: 27.3 us -> 30.5 us
    ppermute x22 -> x19, waiting for transfers between devices: 25.2 us -> 15.2 us  [swapped(): return lax.ppermute(block, 'seq', [(i, i ^ bits) for i in range(n)])]
    unnamed x27 -> x29, local copies, waits for them, and re-layouts: 8.13 us -> 0.73 us
    pallas_call x1, Pallas kernels: 1.15 us -> 3.07 us  [on_device_owned(): call(lambda *refs: new_kernel(scale, *refs), 'new_tokens', [jax.ShapeDtyp...]
    ppermute x1, waiting for transfers between devices: 5.06 us -> 6.58 us  [passed_along(): return lax.ppermute(block, axis, route)]
    pallas_call x3 -> x6, Pallas kernels: 19.1 us -> 20.4 us  [the longest x3 13.2 us: cache_part(): call(lambda *refs: cache_kernel(scale, order, *refs), name, outs, [IN_SME...]
    ppermute x22 -> x19, starting transfers between devices: 16.4 us -> 16.6 us  [swapped(): return lax.ppermute(block, 'seq', [(i, i ^ bits) for i in range(n)])]
  transfers between devices with their start and end apart: 23 -> 20, of which waited for: 19 -> 8; matrix products, arithmetic and copies ran while one was open for 0% -> 0% of each run, Pallas kernels for 14% -> 32%
where the time goes in v2:
time: 72.1 us; the launch traced here: 73 us
  Pallas kernels  30.5 us (42%)
  waiting for transfers between devices  21.7 us (30%)
  starting transfers between devices  18.4 us (26%)
  between operations  1.03 us (1%)
  local copies, waits for them, and re-layouts  0.76 us (1%)
    ppermute x19, starting transfers between devices, swapped(): return lax.ppermute(block, 'seq', [(i, i ^ bits) for i in range(n)])  16.6 us
    ppermute x19, waiting for transfers between devices, swapped(): return lax.ppermute(block, 'seq', [(i, i ^ bits) for i in range(n)])  15.2 us
    pallas_call x3, Pallas kernels, cache_part(): call(lambda *refs: cache_kernel(scale, order, *refs), name, outs, [IN_SME...  13.2 us
    pallas_call x1, Pallas kernels, keys_by_head(): call(keys_kernel, 'keys_by_head', [jax.ShapeDtypeStruct((heads, ctx, dim)...  7.13 us
    ppermute x1, waiting for transfers between devices, passed_along(): return lax.ppermute(block, axis, route)  6.58 us
    pallas_call x1, Pallas kernels, on_device_owned(): call(query_kernel, 'queries', [jax.ShapeDtypeStruct((tok, own_cols), jnp....  3.59 us
    pallas_call x1, Pallas kernels, on_device_owned(): call(output_kernel, 'project', [jax.ShapeDtypeStruct((tok // 2, width), j...  3.24 us
    pallas_call x1, Pallas kernels, on_device_owned(): call(lambda *refs: new_kernel(scale, *refs), 'new_tokens', [jax.ShapeDtyp...  3.07 us
  transfers between devices with their start and end apart: 20, of which 8 were waited for; matrix products, arithmetic and copies ran while one was open for 0% of the time, Pallas kernels for 32%

profile of v2, /device:TPU:0, one launch (start us, length us, event | category | flops | bytes accessed | tf_op | source)
XLA Modules:
  0.0 73.0 jit_solution(7821151155764139942)
XLA Ops:
  0.0 3.9 %collective-permute-start.3 = (bf16[8,8192]{1,0:T(8,128)(2,1)}, bf16[8,8192]{1,0:T(8,128)(2,1)S(1)}, u32[]{:S(2)}, u32[]{:S(2)}) collective-permute-start(bf16[8,8192]{1,0:T(8,128)(2,1)} %bitcast.18), channel_id=1, source_target_pairs={{0,6},{1,7},{2,4},{3,5},{4,2},{5,3},{6,0},{7,1},{8,14},{9,15},{10,... | collective-permute-start | bytes 393224 | tf_op jit(solution)/shard_map/gather_tokens/ppermute | solution.py:182
  3.9 0.5 collective-permute-start.2
  4.5 7.1 %keys_by_head.1 = (bf16[8,2048,128]{2,1,0:T(8,128)(2,1)S(1)}, f32[8,128]{1,0:T(8,128)S(1)}) custom-call(s32[1]{0:T(128)} %bitcast.1.rank.refs_0_, bf16[2048,8,128]{2,1,0:T(8,128)(2,1)} %bitcast.30), custom_call_target="tpu_custom_call" | custom-call | flops 10000000000 | bytes 8388608 | tf_op jit(solution)/shard_map/cache_layout/keys_by_head/pallas_call | solution.py:274
  12.4 0.6 collective-permute-start.4
  13.0 0.2 fusion.4
  13.3 1.0 %collective-permute-done.4.refs_3_ = bf16[3,8,8192]{2,1,0:T(8,128)(2,1)S(1)} collective-permute-done((bf16[3,8,8192]{2,1,0:T(8,128)(2,1)S(1)}, bf16[3,8,8192]{2,1,0:T(8,128)(2,1)S(1)}, u32[]{:S(2)}, u32[]{:S(2)}) %collective-permute-start.4) | collective-permute-done | bytes 393248 | tf_op jit(solution)/shard_map/gather_tokens/ppermute | solution.py:182
  14.4 3.6 %queries.1 = (bf16[64,1024]{1,0:T(8,128)(2,1)S(1)}, bf16[64,8192]{1,0:T(8,128)(2,1)S(1)}) custom-call(s32[1]{0:T(128)} %bitcast.1.rank.refs_0_, bf16[8,8192]{1,0:T(8,128)(2,1)S(1)} %bitcast.22, bf16[8,8192]{1,0:T(8,128)(2,1)S(1)} %collective-permute-done.refs_1_, bf16[3,8,8192]{2,1,0:T(8,128)(2,1)S(1)} %join_tokens.1.refs_2_, ...), custom_call_target="tpu_custom_call" | custom-call | flops 2147483648 | bytes 16777216 | tf_op jit(solution)/shard_map/queries/queries/pallas_call | solution.py:557
  18.0 3.0 %collective-permute-start.8 = (bf16[64,1024]{1,0:T(8,128)(2,1)S(1)}, bf16[64,1024]{1,0:T(8,128)(2,1)S(1)}, u32[]{:S(2)}, u32[]{:S(2)}) collective-permute-start(bf16[64,1024]{1,0:T(8,128)(2,1)S(1)} %get-tuple-element.21.refs_0_.refs_2_), channel_id=1, source_target_pairs={{0,7},{1,6},{2,5},{3,4},{4,3},{5,2},{6,1},{7,0},{8,15},{9,14},{10,... | collective-permute-start | bytes 393224 | tf_op jit(solution)/shard_map/gather_queries/ppermute | solution.py:182
  20.9 0.3 collective-permute-start.7
  21.2 0.1 collective-permute-start.6
  21.3 0.4 collective-permute-start.5
  21.7 3.1 %new_tokens.1 = (bf16[8,128,2048]{2,1,0:T(8,128)(2,1)S(1)}, f32[128,512]{1,0:T(8,128)S(1)}, f32[8,512]{1,0:T(8,128)S(1)}) custom-call(bf16[64,1024]{1,0:T(8,128)(2,1)S(1)} %get-tuple-element.21.refs_0_.refs_2_, bf16[64,8192]{1,0:T(8,128)(2,1)S(1)} %get-tuple-element.23.refs_1_, bf16[8192,128]{1,0:T(8,128)(2,1)S(1)} %bitcast.27, ...), custom_call_target="tpu_custom_call" | custom-call | flops 4294967296 | bytes 13631488 | tf_op jit(solution)/shard_map/new_tokens/new_tokens/pallas_call | solution.py:586
  24.8 4.1 %cache_near.1 = (f32[1,136,512]{2,1,0:T(8,128)S(1)}, bf16[1,144,512]{2,1,0:T(8,128)(2,1)S(1)}) custom-call(s32[1]{0:T(128)} %bitcast.1.rank.refs_0_, s32[2,16]{1,0:T(2,128)S(1)} %bitcast.23, bf16[64,1024]{1,0:T(8,128)(2,1)S(1)} %get-tuple-element.21.refs_0_.refs_2_, bf16[64,1024]{1,0:T(8,128)(2,1)S(1)} %collective-permute-done.5.refs_3_, ...), custom_call_target="tpu_custom_call" | custom-call | flops 536870912 | bytes 2097152 | tf_op jit(solution)/shard_map/cache_near/cache_near/pallas_call | solution.py:441
  29.1 4.5 %cache_odd.1 = bf16[3,144,512]{2,1,0:T(8,128)(2,1)S(1)} custom-call(s32[1]{0:T(128)} %bitcast.1.rank.refs_0_, s32[2,16]{1,0:T(2,128)S(1)} %bitcast.24, bf16[3,64,1024]{2,1,0:T(8,128)(2,1)S(1)} %join_queries.1.refs_2_, bf16[8,2048,128]{2,1,0:T(8,128)(2,1)S(1)} %get-tuple-element.22.refs_4_.refs_3_, bf16[8,128,2048]{2,1,0:T(8,128)(2,1)S(1)} %get-tuple-element.24.refs_5_.refs_4_), custom_call_target="tpu_custom_call" | custom-call | flops 4026531840 | bytes 3145728 | tf_op jit(solution)/shard_map/cache_odd/cache_odd/pallas_call | solution.py:441
  33.8 0.5 collective-permute-start.10
  34.2 4.5 %cache_even.1.own_rest = f32[3,136,512]{2,1,0:T(8,128)S(1)} custom-call(s32[1]{0:T(128)} %bitcast.1.rank.refs_0_, s32[2,16]{1,0:T(2,128)S(1)} %bitcast.25, bf16[3,64,1024]{2,1,0:T(8,128)(2,1)S(1)} %collective-permute-done.9.refs_2_, bf16[8,2048,128]{2,1,0:T(8,128)(2,1)S(1)} %get-tuple-element.22.refs_4_.refs_3_, ...), custom_call_target="tpu_custom_call" | custom-call | flops 805306368 | bytes 3145728 | tf_op jit(solution)/shard_map/cache_even/cache_even/pallas_call | solution.py:441
  38.8 0.3 merge_cores.1
  39.1 1.6 %collective-permute-start.13 = (bf16[144,512]{1,0:T(8,128)(2,1)S(1)}, bf16[144,512]{1,0:T(8,128)(2,1)S(1)}, u32[]{:S(2)}, u32[]{:S(2)}) collective-permute-start(bf16[144,512]{1,0:T(8,128)(2,1)S(1)} %get-tuple-element.29), channel_id=1, source_target_pairs={{0,4},{1,5},{2,6},{3,7},{4,0},{5,1},{6,2},{7,3},{8,12},{9,13},{10,... | collective-permute-start | bytes 442376 | tf_op jit(solution)/shard_map/exchange_parts/ppermute | solution.py:182
  40.8 1.9 %collective-permute-start.14 = (bf16[144,512]{1,0:T(8,128)(2,1)S(1)}, bf16[144,512]{1,0:T(8,128)(2,1)S(1)}, u32[]{:S(2)}, u32[]{:S(2)}) collective-permute-start(bf16[144,512]{1,0:T(8,128)(2,1)S(1)} %get-tuple-element.30), channel_id=1, source_target_pairs={{0,6},{1,7},{2,4},{3,5},{4,2},{5,3},{6,0},{7,1},{8,14},{9,15},{10,... | collective-permute-start | bytes 442376 | tf_op jit(solution)/shard_map/exchange_parts/ppermute | solution.py:182
  42.6 3.2 %collective-permute-done.12.got_a = bf16[144,512]{1,0:T(8,128)(2,1)S(1)} collective-permute-done((bf16[144,512]{1,0:T(8,128)(2,1)S(1)}, bf16[144,512]{1,0:T(8,128)(2,1)S(1)}, u32[]{:S(2)}, u32[]{:S(2)}) %collective-permute-start.12) | collective-permute-done | bytes 147488 | tf_op jit(solution)/shard_map/exchange_parts/ppermute | solution.py:182
  45.8 2.4 %collective-permute-done.13.got_b = bf16[144,512]{1,0:T(8,128)(2,1)S(1)} collective-permute-done((bf16[144,512]{1,0:T(8,128)(2,1)S(1)}, bf16[144,512]{1,0:T(8,128)(2,1)S(1)}, u32[]{:S(2)}, u32[]{:S(2)}) %collective-permute-start.13) | collective-permute-done | bytes 147488 | tf_op jit(solution)/shard_map/exchange_parts/ppermute | solution.py:182
  48.2 3.2 %project.1 = (f32[32,8192]{1,0:T(8,128)S(1)}, bf16[32,8192]{1,0:T(8,128)(2,1)S(1)}) custom-call(s32[1]{0:T(128)} %bitcast.1.rank.refs_0_, f32[136,512]{1,0:T(8,128)S(1)} %get-tuple-element.27.kept, bf16[144,512]{1,0:T(8,128)(2,1)S(1)} %collective-permute-done.12.got_a, bf16[144,512]{1,0:T(8,128)(2,1)S(1)} %collective-permute-done.13.got_b, ...), custom_call_target="tpu_custom_call" | custom-call | flops 2147483648 | bytes 18874368 | tf_op jit(solution)/shard_map/project/project/pallas_call | solution.py:633
  51.6 1.9 %collective-permute-done.15 = bf16[32,8192]{1,0:T(8,128)(2,1)S(1)} collective-permute-done((bf16[32,8192]{1,0:T(8,128)(2,1)S(1)}, bf16[32,8192]{1,0:T(8,128)(2,1)S(1)}, u32[]{:S(2)}, u32[]{:S(2)}) %collective-permute-start.15) | collective-permute-done | bytes 524320 | tf_op jit(solution)/shard_map/reduce_cores/ppermute | solution.py:182
  53.6 1.2 %collective-permute-start.16 = (bf16[8,8192]{1,0:T(8,128)(2,1)S(1)}, bf16[8,8192]{1,0:T(8,128)(2,1)S(1)}, u32[]{:S(2)}, u32[]{:S(2)}) collective-permute-start(bf16[8,8192]{1,0:T(8,128)(2,1)S(1)} %get-tuple-element.37), channel_id=1, source_target_pairs={{0,2},{1,3},{2,0},{3,1},{4,6},{5,7},{6,4},{7,5},{8,10},{9,11},{10,... | collective-permute-start | bytes 393224 | tf_op jit(solution)/shard_map/reduce_chips/ppermute | solution.py:182
  54.8 1.2 %collective-permute-start.18 = (bf16[8,8192]{1,0:T(8,128)(2,1)S(1)}, bf16[8,8192]{1,0:T(8,128)(2,1)S(1)}, u32[]{:S(2)}, u32[]{:S(2)}) collective-permute-start(bf16[8,8192]{1,0:T(8,128)(2,1)S(1)} %get-tuple-element.38), channel_id=1, source_target_pairs={{0,6},{1,7},{2,4},{3,5},{4,2},{5,3},{6,0},{7,1},{8,14},{9,15},{10,... | collective-permute-start | bytes 393224 | tf_op jit(solution)/shard_map/reduce_chips/ppermute | solution.py:182
  56.0 1.2 %collective-permute-start.17 = (bf16[8,8192]{1,0:T(8,128)(2,1)S(1)}, bf16[8,8192]{1,0:T(8,128)(2,1)S(1)}, u32[]{:S(2)}, u32[]{:S(2)}) collective-permute-start(bf16[8,8192]{1,0:T(8,128)(2,1)S(1)} %get-tuple-element.39), channel_id=1, source_target_pairs={{0,4},{1,5},{2,6},{3,7},{4,0},{5,1},{6,2},{7,3},{8,12},{9,13},{10,... | collective-permute-start | bytes 393224 | tf_op jit(solution)/shard_map/reduce_chips/ppermute | solution.py:182
  57.2 2.9 %collective-permute-done.16 = bf16[8,8192]{1,0:T(8,128)(2,1)S(1)} collective-permute-done((bf16[8,8192]{1,0:T(8,128)(2,1)S(1)}, bf16[8,8192]{1,0:T(8,128)(2,1)S(1)}, u32[]{:S(2)}, u32[]{:S(2)}) %collective-permute-start.16) | collective-permute-done | bytes 131104 | tf_op jit(solution)/shard_map/reduce_chips/ppermute | solution.py:182
  60.0 2.4 %collective-permute-done.18 = bf16[8,8192]{1,0:T(8,128)(2,1)S(1)} collective-permute-done((bf16[8,8192]{1,0:T(8,128)(2,1)S(1)}, bf16[8,8192]{1,0:T(8,128)(2,1)S(1)}, u32[]{:S(2)}, u32[]{:S(2)}) %collective-permute-start.18) | collective-permute-done | bytes 131104 | tf_op jit(solution)/shard_map/reduce_chips/ppermute | solution.py:182
  62.4 1.4 %collective-permute-done.17 = bf16[8,8192]{1,0:T(8,128)(2,1)S(1)} collective-permute-done((bf16[8,8192]{1,0:T(8,128)(2,1)S(1)}, bf16[8,8192]{1,0:T(8,128)(2,1)S(1)}, u32[]{:S(2)}, u32[]{:S(2)}) %collective-permute-start.17) | collective-permute-done | bytes 131104 | tf_op jit(solution)/shard_map/reduce_chips/ppermute | solution.py:182
  63.9 1.8 %collective-permute-start.19 = (bf16[8,8192]{1,0:T(8,128)(2,1)S(1)}, bf16[8,8192]{1,0:T(8,128)(2,1)S(1)}, u32[]{:S(2)}, u32[]{:S(2)}) collective-permute-start(bf16[8,8192]{1,0:T(8,128)(2,1)S(1)} %fusion.3), channel_id=1, source_target_pairs={{24,0},{0,8},{8,16},{16,24},{25,1},{1,9},{9,17},{17,25},{26,2},{2,... | collective-permute-start | bytes 393224 | tf_op jit(solution)/shard_map/hand_on/ppermute | solution.py:20
  65.7 6.6 %collective-permute-done.19 = bf16[8,8192]{1,0:T(8,128)(2,1)S(1)} collective-permute-done((bf16[8,8192]{1,0:T(8,128)(2,1)S(1)}, bf16[8,8192]{1,0:T(8,128)(2,1)S(1)}, u32[]{:S(2)}, u32[]{:S(2)}) %collective-permute-start.19) | collective-permute-done | bytes 131104 | tf_op jit(solution)/shard_map/hand_on/ppermute | solution.py:20
  72.3 0.7 copy.13
  (56 shorter events, 0.9 us)
Async XLA Ops:
  0.0 12.3 %collective-permute-start.3 = (bf16[8,8192]{1,0:T(8,128)(2,1)}, bf16[8,8192]{1,0:T(8,128)(2,1)S(1)}, u32[]{:S(2)}, u32[]{:S(2)}) collective-permute-start(bf16[8,8192]{1,0:T(8,128)(2,1)} %bitcast.18), channel_id=1, source_target_pairs={{0,6},{1,7},{2,4},{3,5},{4,2},{5,3},{6,0},{7,1},{8,14},{9,15},{10,... | collective-permute-start | bytes 393224 | tf_op jit(solution)/shard_map/gather_tokens/ppermute | solution.py:182
  3.9 8.4 %collective-permute-start.2 = (bf16[8,8192]{1,0:T(8,128)(2,1)}, bf16[8,8192]{1,0:T(8,128)(2,1)S(1)}, u32[]{:S(2)}, u32[]{:S(2)}) collective-permute-start(bf16[8,8192]{1,0:T(8,128)(2,1)} %bitcast.19), channel_id=1, source_target_pairs={{0,4},{1,5},{2,6},{3,7},{4,0},{5,1},{6,2},{7,3},{8,12},{9,13},{10,... | collective-permute-start | bytes 393224 | tf_op jit(solution)/shard_map/gather_tokens/ppermute | solution.py:182
  4.4 7.9 %collective-permute-start.1 = (bf16[8,8192]{1,0:T(8,128)(2,1)}, bf16[8,8192]{1,0:T(8,128)(2,1)S(1)}, u32[]{:S(2)}, u32[]{:S(2)}) collective-permute-start(bf16[8,8192]{1,0:T(8,128)(2,1)} %bitcast.20), channel_id=1, source_target_pairs={{0,2},{1,3},{2,0},{3,1},{4,6},{5,7},{6,4},{7,5},{8,10},{9,11},{10,... | collective-permute-start | bytes 393224 | tf_op jit(solution)/shard_map/gather_tokens/ppermute | solution.py:182
  4.5 8.8 %collective-permute-start = (bf16[8,8192]{1,0:T(8,128)(2,1)}, bf16[8,8192]{1,0:T(8,128)(2,1)S(1)}, u32[]{:S(2)}, u32[]{:S(2)}) collective-permute-start(bf16[8,8192]{1,0:T(8,128)(2,1)} %bitcast.21), channel_id=1, source_target_pairs={{0,1},{1,0},{2,3},{3,2},{4,5},{5,4},{6,7},{7,6},{8,9},{9,8},{10,11... | collective-permute-start | bytes 393224 | tf_op jit(solution)/shard_map/gather_tokens/ppermute | solution.py:182
  4.5 9.8 %slice-start = ((s8[16777216]{0:T(1024)(128)(4,1)}), s8[4194304]{0:T(1024)(128)(4,1)S(1)}, s32[]{:S(2)}) async-start(s8[16777216]{0:T(1024)(128)(4,1)} %bitcast.12), calls=%async_computation | async-start | bytes 8388608
  4.5 9.8 %slice-start.1 = ((s8[16777216]{0:T(1024)(128)(4,1)}), s8[4194304]{0:T(1024)(128)(4,1)S(1)}, s32[]{:S(2)}) async-start(s8[16777216]{0:T(1024)(128)(4,1)} %bitcast.12), calls=%async_computation.1 | async-start | bytes 8388608
  4.5 9.8 %slice-start.2 = ((s8[16777216]{0:T(1024)(128)(4,1)}), s8[4194304]{0:T(1024)(128)(4,1)S(1)}, s32[]{:S(2)}) async-start(s8[16777216]{0:T(1024)(128)(4,1)} %bitcast.12), calls=%async_computation.2 | async-start | bytes 8388608
  4.5 9.8 %slice-start.3 = ((s8[16777216]{0:T(1024)(128)(4,1)}), s8[4194304]{0:T(1024)(128)(4,1)S(1)}, s32[]{:S(2)}) async-start(s8[16777216]{0:T(1024)(128)(4,1)} %bitcast.12), calls=%async_computation.3 | async-start | bytes 8388608
  4.5 9.8 %copy-start = (bf16[1,8,8192]{2,1,0:T(8,128)(2,1)S(1)}, bf16[1,8,8192]{2,1,0:T(8,128)(2,1)}, u32[]{:S(2)}) copy-start(bf16[1,8,8192]{2,1,0:T(8,128)(2,1)} %param.10) | copy-start | bytes 393220
  4.5 9.8 %copy-start.1 = (bf16[1,8192]{1,0:T(2,128)(2,1)S(1)}, bf16[1,8192]{1,0:T(2,128)(2,1)}, u32[]{:S(2)}) copy-start(bf16[1,8192]{1,0:T(2,128)(2,1)} %refs_4_.1) | copy-start | bytes 49156
  12.4 1.9 %collective-permute-start.4 = (bf16[3,8,8192]{2,1,0:T(8,128)(2,1)S(1)}, bf16[3,8,8192]{2,1,0:T(8,128)(2,1)S(1)}, u32[]{:S(2)}, u32[]{:S(2)}) collective-permute-start(bf16[3,8,8192]{2,1,0:T(8,128)(2,1)S(1)} %join_tokens.1.refs_2_), channel_id=1, source_target_pairs={{0,1},{1,0},{2,3},{3,2},{4,5},{5,4},{6,7},{7,6},{8,9},{9,8},{10,11... | collective-permute-start | bytes 1179656 | tf_op jit(solution)/shard_map/gather_tokens/ppermute | solution.py:182
  14.3 7.4 %copy-start.3 = (bf16[1,2048,8,128]{3,2,1,0:T(8,128)(2,1)S(1)}, bf16[1,2048,8,128]{3,2,1,0:T(8,128)(2,1)}, u32[]{:S(2)}) copy-start(bf16[1,2048,8,128]{3,2,1,0:T(8,128)(2,1)} %param.17) | copy-start | bytes 12582916
  14.4 7.4 %copy-start.4 = (bf16[1,8192,128]{2,1,0:T(8,128)(2,1)S(1)}, bf16[1,8192,128]{2,1,0:T(8,128)(2,1)}, u32[]{:S(2)}) copy-start(bf16[1,8192,128]{2,1,0:T(8,128)(2,1)} %param.13) | copy-start | bytes 6291460
  18.0 11.0 %collective-permute-start.8 = (bf16[64,1024]{1,0:T(8,128)(2,1)S(1)}, bf16[64,1024]{1,0:T(8,128)(2,1)S(1)}, u32[]{:S(2)}, u32[]{:S(2)}) collective-permute-start(bf16[64,1024]{1,0:T(8,128)(2,1)S(1)} %get-tuple-element.21.refs_0_.refs_2_), channel_id=1, source_target_pairs={{0,7},{1,6},{2,5},{3,4},{4,3},{5,2},{6,1},{7,0},{8,15},{9,14},{10,... | collective-permute-start | bytes 393224 | tf_op jit(solution)/shard_map/gather_queries/ppermute | solution.py:182
  20.9 8.0 %collective-permute-start.7 = (bf16[64,1024]{1,0:T(8,128)(2,1)S(1)}, bf16[64,1024]{1,0:T(8,128)(2,1)S(1)}, u32[]{:S(2)}, u32[]{:S(2)}) collective-permute-start(bf16[64,1024]{1,0:T(8,128)(2,1)S(1)} %get-tuple-element.21.refs_0_.refs_2_), channel_id=1, source_target_pairs={{0,5},{1,4},{2,7},{3,6},{4,1},{5,0},{6,3},{7,2},{8,13},{9,12},{10,... | collective-permute-start | bytes 393224 | tf_op jit(solution)/shard_map/gather_queries/ppermute | solution.py:182
  21.2 7.8 %collective-permute-start.6 = (bf16[64,1024]{1,0:T(8,128)(2,1)S(1)}, bf16[64,1024]{1,0:T(8,128)(2,1)S(1)}, u32[]{:S(2)}, u32[]{:S(2)}) collective-permute-start(bf16[64,1024]{1,0:T(8,128)(2,1)S(1)} %get-tuple-element.21.refs_0_.refs_2_), channel_id=1, source_target_pairs={{0,3},{1,2},{2,1},{3,0},{4,7},{5,6},{6,5},{7,4},{8,11},{9,10},{10,... | collective-permute-start | bytes 393224 | tf_op jit(solution)/shard_map/gather_queries/ppermute | solution.py:182
  21.3 3.5 %collective-permute-start.5 = (bf16[64,1024]{1,0:T(8,128)(2,1)S(1)}, bf16[64,1024]{1,0:T(8,128)(2,1)S(1)}, u32[]{:S(2)}, u32[]{:S(2)}) collective-permute-start(bf16[64,1024]{1,0:T(8,128)(2,1)S(1)} %get-tuple-element.21.refs_0_.refs_2_), channel_id=1, source_target_pairs={{0,1},{1,0},{2,3},{3,2},{4,5},{5,4},{6,7},{7,6},{8,9},{9,8},{10,11... | collective-permute-start | bytes 393224 | tf_op jit(solution)/shard_map/gather_queries/ppermute | solution.py:182
  24.8 23.4 %slice-start.4 = ((s8[16777216]{0:T(1024)(128)(4,1)}), s8[4194304]{0:T(1024)(128)(4,1)S(1)}, s32[]{:S(2)}) async-start(s8[16777216]{0:T(1024)(128)(4,1)} %bitcast.15), calls=%async_computation.4 | async-start | bytes 8388608
  29.0 19.2 %slice-start.5 = ((s8[16777216]{0:T(1024)(128)(4,1)}), s8[4194304]{0:T(1024)(128)(4,1)S(1)}, s32[]{:S(2)}) async-start(s8[16777216]{0:T(1024)(128)(4,1)} %bitcast.15), calls=%async_computation.5 | async-start | bytes 8388608
  29.0 19.2 %slice-start.6 = ((s8[16777216]{0:T(1024)(128)(4,1)}), s8[4194304]{0:T(1024)(128)(4,1)S(1)}, s32[]{:S(2)}) async-start(s8[16777216]{0:T(1024)(128)(4,1)} %bitcast.15), calls=%async_computation.6 | async-start | bytes 8388608
  29.0 5.2 %collective-permute-start.9 = (bf16[3,64,1024]{2,1,0:T(8,128)(2,1)S(1)}, bf16[3,64,1024]{2,1,0:T(8,128)(2,1)S(1)}, u32[]{:S(2)}, u32[]{:S(2)}) collective-permute-start(bf16[3,64,1024]{2,1,0:T(8,128)(2,1)S(1)} %join_queries.1.refs_2_), channel_id=1, source_target_pairs={{0,1},{1,0},{2,3},{3,2},{4,5},{5,4},{6,7},{7,6},{8,9},{9,8},{10,11... | collective-permute-start | bytes 1179656 | tf_op jit(solution)/shard_map/gather_queries/ppermute | solution.py:182
  33.7 5.1 %collective-permute-start.11 = (bf16[3,144,512]{2,1,0:T(8,128)(2,1)S(1)}, bf16[3,144,512]{2,1,0:T(8,128)(2,1)S(1)}, u32[]{:S(2)}, u32[]{:S(2)}) collective-permute-start(bf16[3,144,512]{2,1,0:T(8,128)(2,1)S(1)} %cache_odd.1), channel_id=1, source_target_pairs={{0,1},{1,0},{2,3},{3,2},{4,5},{5,4},{6,7},{7,6},{8,9},{9,8},{10,11... | collective-permute-start | bytes 1327112 | tf_op jit(solution)/shard_map/cache_odd/ppermute | solution.py:182
  33.7 14.5 %slice-start.7 = ((s8[16777216]{0:T(1024)(128)(4,1)}), s8[4194304]{0:T(1024)(128)(4,1)S(1)}, s32[]{:S(2)}) async-start(s8[16777216]{0:T(1024)(128)(4,1)} %bitcast.15), calls=%async_computation.7 | async-start | bytes 8388608
  33.8 5.0 %collective-permute-start.10 = (bf16[1,144,512]{2,1,0:T(8,128)(2,1)S(1)}, bf16[1,144,512]{2,1,0:T(8,128)(2,1)S(1)}, u32[]{:S(2)}, u32[]{:S(2)}) collective-permute-start(bf16[1,144,512]{2,1,0:T(8,128)(2,1)S(1)} %get-tuple-element.26), channel_id=1, source_target_pairs={{0,1},{1,0},{2,3},{3,2},{4,5},{5,4},{6,7},{7,6},{8,9},{9,8},{10,11... | collective-permute-start | bytes 442376 | tf_op jit(solution)/shard_map/cache_near/ppermute | solution.py:182
  39.1 6.7 %collective-permute-start.12 = (bf16[144,512]{1,0:T(8,128)(2,1)S(1)}, bf16[144,512]{1,0:T(8,128)(2,1)S(1)}, u32[]{:S(2)}, u32[]{:S(2)}) collective-permute-start(bf16[144,512]{1,0:T(8,128)(2,1)S(1)} %get-tuple-element.28), channel_id=1, source_target_pairs={{0,2},{1,3},{2,0},{3,1},{4,6},{5,7},{6,4},{7,5},{8,10},{9,11},{10,... | collective-permute-start | bytes 442376 | tf_op jit(solution)/shard_map/exchange_parts/ppermute | solution.py:182
  39.1 9.1 %collective-permute-start.13 = (bf16[144,512]{1,0:T(8,128)(2,1)S(1)}, bf16[144,512]{1,0:T(8,128)(2,1)S(1)}, u32[]{:S(2)}, u32[]{:S(2)}) collective-permute-start(bf16[144,512]{1,0:T(8,128)(2,1)S(1)} %get-tuple-element.29), channel_id=1, source_target_pairs={{0,4},{1,5},{2,6},{3,7},{4,0},{5,1},{6,2},{7,3},{8,12},{9,13},{10,... | collective-permute-start | bytes 442376 | tf_op jit(solution)/shard_map/exchange_parts/ppermute | solution.py:182
  40.8 7.5 %collective-permute-start.14 = (bf16[144,512]{1,0:T(8,128)(2,1)S(1)}, bf16[144,512]{1,0:T(8,128)(2,1)S(1)}, u32[]{:S(2)}, u32[]{:S(2)}) collective-permute-start(bf16[144,512]{1,0:T(8,128)(2,1)S(1)} %get-tuple-element.30), channel_id=1, source_target_pairs={{0,6},{1,7},{2,4},{3,5},{4,2},{5,3},{6,0},{7,1},{8,14},{9,15},{10,... | collective-permute-start | bytes 442376 | tf_op jit(solution)/shard_map/exchange_parts/ppermute | solution.py:182
  51.5 2.0 %collective-permute-start.15 = (bf16[32,8192]{1,0:T(8,128)(2,1)S(1)}, bf16[32,8192]{1,0:T(8,128)(2,1)S(1)}, u32[]{:S(2)}, u32[]{:S(2)}) collective-permute-start(bf16[32,8192]{1,0:T(8,128)(2,1)S(1)} %get-tuple-element.34), channel_id=1, source_target_pairs={{0,1},{1,0},{2,3},{3,2},{4,5},{5,4},{6,7},{7,6},{8,9},{9,8},{10,11... | collective-permute-start | bytes 1572872 | tf_op jit(solution)/shard_map/reduce_cores/ppermute | solution.py:182
  53.6 6.4 %collective-permute-start.16 = (bf16[8,8192]{1,0:T(8,128)(2,1)S(1)}, bf16[8,8192]{1,0:T(8,128)(2,1)S(1)}, u32[]{:S(2)}, u32[]{:S(2)}) collective-permute-start(bf16[8,8192]{1,0:T(8,128)(2,1)S(1)} %get-tuple-element.37), channel_id=1, source_target_pairs={{0,2},{1,3},{2,0},{3,1},{4,6},{5,7},{6,4},{7,5},{8,10},{9,11},{10,... | collective-permute-start | bytes 393224 | tf_op jit(solution)/shard_map/reduce_chips/ppermute | solution.py:182
  54.8 7.6 %collective-permute-start.18 = (bf16[8,8192]{1,0:T(8,128)(2,1)S(1)}, bf16[8,8192]{1,0:T(8,128)(2,1)S(1)}, u32[]{:S(2)}, u32[]{:S(2)}) collective-permute-start(bf16[8,8192]{1,0:T(8,128)(2,1)S(1)} %get-tuple-element.38), channel_id=1, source_target_pairs={{0,6},{1,7},{2,4},{3,5},{4,2},{5,3},{6,0},{7,1},{8,14},{9,15},{10,... | collective-permute-start | bytes 393224 | tf_op jit(solution)/shard_map/reduce_chips/ppermute | solution.py:182
  56.0 7.8 %collective-permute-start.17 = (bf16[8,8192]{1,0:T(8,128)(2,1)S(1)}, bf16[8,8192]{1,0:T(8,128)(2,1)S(1)}, u32[]{:S(2)}, u32[]{:S(2)}) collective-permute-start(bf16[8,8192]{1,0:T(8,128)(2,1)S(1)} %get-tuple-element.39), channel_id=1, source_target_pairs={{0,4},{1,5},{2,6},{3,7},{4,0},{5,1},{6,2},{7,3},{8,12},{9,13},{10,... | collective-permute-start | bytes 393224 | tf_op jit(solution)/shard_map/reduce_chips/ppermute | solution.py:182
  63.9 8.4 %collective-permute-start.19 = (bf16[8,8192]{1,0:T(8,128)(2,1)S(1)}, bf16[8,8192]{1,0:T(8,128)(2,1)S(1)}, u32[]{:S(2)}, u32[]{:S(2)}) collective-permute-start(bf16[8,8192]{1,0:T(8,128)(2,1)S(1)} %fusion.3), channel_id=1, source_target_pairs={{24,0},{0,8},{8,16},{16,24},{25,1},{1,9},{9,17},{17,25},{26,2},{2,... | collective-permute-start | bytes 393224 | tf_op jit(solution)/shard_map/hand_on/ppermute | solution.py:20
  (2 other events, 10.4 us)

commit v3 on v2

--- a/solution.py
+++ b/solution.py
@@ -182,6 +182,14 @@
     return lax.ppermute(block, "seq", [(i, i ^ bits) for i in range(n)])
 
 
+def onward(block, bits):
+    sections, n = lax.axis_size("section"), lax.axis_size("seq")
+    route = [
+        (s * n + i, (s + 1) % sections * n + (i ^ bits)) for s in range(sections) for i in range(n)
+    ]
+    return lax.ppermute(block, ("section", "seq"), route)
+
+
 def call(kernel, name, out_shape, in_specs, flops=0, nbytes=0, scratch=(), vmem=6, **grid):
     out_specs = grid.pop("out_specs", jax.tree.map(lambda _: IN_VMEM, out_shape))
     return pl.pallas_call(
@@ -224,11 +232,10 @@
 
 
 def query_kernel(rank, *refs):
-    mine, near, far, far_near = refs[:4]
-    gain, cosine, sine, weights, query, normed, rows = refs[4:]
+    same_core, other_core, gain, cosine, sine, weights, query, normed, rows = refs
     width = rows.shape[1]
-    count = mine.shape[0]
-    blocks = [mine, near] + [part.at[i] for i in range(3) for part in (far, far_near)]
+    count = same_core.shape[1]
+    blocks = [part.at[i] for i in range(4) for part in (same_core, other_core)]
     step = 1024
     for bits in range(8):
         at = pl.multiple_of((rank[0] ^ bits) * count, count)
@@ -263,41 +270,57 @@
     return lax.dot_general(a, b, (((1,), (1,)), ((), ())), preferred_element_type=jnp.float32)
 
 
-def keys_kernel(rank, keys, keys_out, done):
-    keys_out[...] = jnp.swapaxes(keys[...], 0, 1)
+def by_head_kernel(rank, keys, values, keys_out, values_out, done, keys_in, values_in, sems):
+    block = keys.shape[0] // sems.shape[1]
+    copies = []
+    for i in range(sems.shape[1]):
+        at = pl.ds(i * block, block)
+        copies.append(
+            [
+                pltpu.make_async_copy(source.at[at], target.at[at], sems.at[which, i])
+                for which, (source, target) in enumerate([(keys, keys_in), (values, values_in)])
+            ]
+        )
+    for pair in copies:
+        for copy in pair:
+            copy.start()
     done[...] = jnp.zeros_like(done)
-
-
-def keys_by_head(rank, keys):
+    for i, pair in enumerate(copies):
+        at = pl.ds(i * block, block)
+        pair[0].wait()
+        keys_out[:, at, :] = jnp.swapaxes(keys_in[at], 0, 1)
+        pair[1].wait()
+        turned = jnp.swapaxes(values_in[at], 0, 1)
+        for g in range(turned.shape[0]):
+            values_out[g, :, at] = turned[g].T
+
+
+def cache_by_head(rank, keys, values):
     ctx, heads, dim = keys.shape
-    block = 256
+    blocks = 8
+    in_hbm = pl.BlockSpec(memory_space=pltpu.HBM)
     return call(
-        keys_kernel,
-        "keys_by_head",
+        by_head_kernel,
+        "cache_by_head",
         [
             jax.ShapeDtypeStruct((heads, ctx, dim), jnp.bfloat16),
+            jax.ShapeDtypeStruct((heads, dim, ctx), jnp.bfloat16),
             jax.ShapeDtypeStruct((8, 128), jnp.float32),
         ],
-        [IN_SMEM, pl.BlockSpec((block, heads, dim), lambda i: (i, 0, 0))],
+        [IN_SMEM, in_hbm, in_hbm],
         flops=10**10,
-        nbytes=2 * ctx * heads * dim * 2,
-        grid=(ctx // block,),
-        out_specs=[
-            pl.BlockSpec((heads, block, dim), lambda i: (0, i, 0)),
-            pl.BlockSpec((8, 128), lambda i: (0, 0)),
+        nbytes=ctx * heads * dim * 2,
+        scratch=[
+            pltpu.VMEM(keys.shape, jnp.bfloat16),
+            pltpu.VMEM(values.shape, jnp.bfloat16),
+            pltpu.SemaphoreType.DMA((2, blocks)),
         ],
-    )(rank, pltpu.with_memory_space_constraint(keys, pltpu.HBM))
-
-
-def values_by_head(values, values_out):
-    block = 256
-
-    @pl.loop(0, values.shape[0] // block)
-    def _(i):
-        at = pl.ds(pl.multiple_of(i * block, block), block)
-        turned = jnp.swapaxes(values[at], 0, 1)
-        for g in range(turned.shape[0]):
-            values_out[g, :, at] = turned[g].T
+        vmem=14,
+    )(
+        rank,
+        pltpu.with_memory_space_constraint(keys, pltpu.HBM),
+        pltpu.with_memory_space_constraint(values, pltpu.HBM),
+    )
 
 
 def new_kernel(
@@ -308,12 +331,9 @@
     w_value,
     cosine,
     sine,
-    cached_values,
-    values_out,
     summed,
     stats,
 ):
-    values_by_head(cached_values, values_out)
     tok, dim = cosine.shape
     heads = query.shape[1] // dim
     raw = jnp.dot(normed[...], w_key[...], preferred_element_type=jnp.float32)
@@ -355,10 +375,10 @@
 def cache_kernel(scale, order, rank, mask, *refs):
     n = len(order)
     given = 1 if len(refs[0].shape) == 3 else n
-    queries, (keys, values), outs = refs[:given], refs[given : given + 2], refs[given + 2 : -3]
+    queries, (keys, values), outs = refs[:given], refs[given : given + 2], refs[given + 2 : -4]
     if given < n:
         queries = [queries[0].at[i] for i in range(n)]
-    q_rows, summed, visible = refs[-3:]
+    q_rows, summed, visible, scores = refs[-4:]
     dim = keys.shape[2]
     heads = queries[0].shape[1] // dim
     cols = heads * QB
@@ -369,37 +389,44 @@
         for b in range(mask.shape[1]):
             visible[count] = b
             count = count + (mask[q_block, b] > 0).astype(jnp.int32)
-        visible[count] = 0
+        for e in range(4):
+            visible[count + e] = 0
         for i in range(n):
             q_rows[i] = query_rows(queries[i], q_block, heads, dim)
             summed[i] = jnp.zeros((dim, cols), jnp.float32)
 
-        def step(pair, carry):
-            at = [pl.multiple_of(visible[2 * pair + e] * KB, KB) for e in range(2)]
+        def places(pair):
+            return [pl.multiple_of(visible[2 * pair + e] * KB, KB) for e in range(2)]
+
+        def score(pair):
+            at = places(pair)
             hidden = jnp.where(2 * pair + 1 < count, jnp.float32(0.0), jnp.float32(neg_fill))
-            scores = [
+            products = [
                 matmul_nt(
                     jnp.concatenate([keys[g, pl.ds(a, KB), :] for a in at], axis=0), q_rows[i]
                 )
                 for i, g in enumerate(groups)
             ]
+            tops = []
+            for i in range(n):
+                first = products[i][:KB] * scale
+                second = products[i][KB:] * scale + hidden
+                scores[i, :KB] = first
+                scores[i, KB:] = second
+                tops.append(jnp.max(jnp.maximum(first, second), axis=0, keepdims=True))
+            return tops
+
+        def step(pair, carry):
             levels, scaled = [], []
             for i in range(n):
-                top, total = carry[2 * i], carry[2 * i + 1]
-                first = scores[i][:KB] * scale
-                second = scores[i][KB:] * scale + hidden
-                new_top = jnp.maximum(
-                    top, jnp.max(jnp.maximum(first, second), axis=0, keepdims=True)
-                )
-                first = jnp.exp2(first - new_top)
-                second = jnp.exp2(second - new_top)
+                top, total, pair_top = carry[3 * i : 3 * i + 3]
+                new_top = jnp.maximum(top, pair_top)
+                weights = jnp.exp2(scores[i] - new_top)
                 factor = jnp.exp2(top - new_top)
-                total = total * factor + jnp.sum(first + second, axis=0, keepdims=True)
+                total = total * factor + jnp.sum(weights, axis=0, keepdims=True)
                 levels += [new_top, total]
-                weights = jnp.concatenate(
-                    [first.astype(jnp.bfloat16), second.astype(jnp.bfloat16)], axis=0
-                )
-                scaled.append((factor, weights))
+                scaled.append((factor, weights.astype(jnp.bfloat16)))
+            at = places(pair)
             products = [
                 jnp.dot(
                     jnp.concatenate([values[g, :, pl.ds(a, KB)] for a in at], axis=1),
@@ -408,15 +435,24 @@
                 )
                 for i, g in enumerate(groups)
             ]
+            tops = score(pair + 1)
+            after = []
             for i in range(n):
                 summed[i] = summed[i] * scaled[i][0] + products[i]
-            return tuple(levels)
-
-        start = (jnp.full((1, cols), neg_fill, jnp.float32), jnp.zeros((1, cols), jnp.float32)) * n
-        ended = lax.fori_loop(0, (count + 1) // 2, step, start)
+                after += [levels[2 * i], levels[2 * i + 1], tops[i]]
+            return tuple(after)
+
+        start = []
+        for top in score(0):
+            start += [
+                jnp.full((1, cols), neg_fill, jnp.float32),
+                jnp.zeros((1, cols), jnp.float32),
+                top,
+            ]
+        ended = lax.fori_loop(0, (count + 1) // 2, step, tuple(start))
         at = slice(q_block * cols, (q_block + 1) * cols)
         for i, bits in enumerate(order):
-            top, total = ended[2 * i], ended[2 * i + 1]
+            top, total = ended[3 * i], ended[3 * i + 1]
             seen = total > 0.0
             safe = jnp.where(seen, total, 1.0)
             level = jnp.where(seen, top + jnp.log2(safe), neg_fill)
@@ -424,7 +460,7 @@
                 out, place = outs[0], own.index(bits)
             else:
                 out, place = outs[-1], i - len(own)
-            out[place, 0:dim, at] = (summed[i] / safe).astype(out.dtype)
+            out[place, 0:dim, at] = (summed[i] * (1.0 / safe)).astype(out.dtype)
             out[place, dim:, at] = split_rows(level, out.shape[1] - dim).astype(out.dtype)
 
 
@@ -448,7 +484,8 @@
         scratch=[
             pltpu.VMEM((n, cols, dim), jnp.bfloat16),
             pltpu.VMEM((n, dim, cols), jnp.float32),
-            pltpu.SMEM((mask.shape[1] + 2,), jnp.int32),
+            pltpu.SMEM((mask.shape[1] + 4,), jnp.int32),
+            pltpu.VMEM((n, 2 * KB, cols), jnp.float32),
         ],
     )(rank, mask, *queries, held(keys), held(values))
 
@@ -470,7 +507,20 @@
         target[dim:, :] = split_rows(level, target.shape[0] - dim).astype(target.dtype)
 
 
-def output_kernel(rank, kept, got_a, got_b, got_c, summed, stats, weights, own, sent, rows, sorted_rows):
+def output_kernel(
+    rank,
+    kept,
+    got_a,
+    got_b,
+    got_c,
+    summed,
+    stats,
+    weights,
+    own,
+    sent,
+    rows,
+    sorted_rows,
+):
     dim = summed.shape[0]
     levels = [level_of(part[dim:, :]) for part in (kept, got_a, got_b, got_c)]
     top = stats[0:1, :]
@@ -483,7 +533,7 @@
         factor = jnp.exp2(level - top)
         total = total + factor
         joined = joined + part[:dim, :].astype(jnp.float32) * factor
-    joined = joined / total
+    joined = joined * (1.0 / total)
     heads = rows.shape[1] // dim
     cols = heads * QB
     for q_block in range(rows.shape[0] // QB):
@@ -534,14 +584,13 @@
     mask = cache_mask[0]
 
     with jax.named_scope("cache_layout"):
-        keys, layout_done = keys_by_head(rank, key_cache[0])
+        keys, values, layout_done = cache_by_head(rank, key_cache[0], cached_value_rows[0])
     with jax.named_scope("gather_tokens"):
         blocks = {0: tokens[0]}
-        blocks[1] = swapped(tokens[0], 1)
         for bits in SAME_CORE:
-            blocks[bits] = swapped(tokens[0], bits)
-        far = joined_after([blocks[bits] for bits in SAME_CORE], [layout_done], "join_tokens")
-        far_near = swapped(far, 1)
+            blocks[bits] = swapped(blocks[0], bits)
+        same_core = joined_after([blocks[bits] for bits in EVEN], [layout_done], "join_tokens")
+        other_core = swapped(same_core, 1)
 
     with jax.named_scope("tables"):
         positions = span_offset[0].astype(jnp.float32) + jnp.arange(tok, dtype=jnp.int32).astype(
@@ -561,16 +610,14 @@
                 jax.ShapeDtypeStruct((tok, own_cols), jnp.bfloat16),
                 jax.ShapeDtypeStruct((tok, width), jnp.bfloat16),
             ],
-            [IN_SMEM] + [IN_VMEM] * 8,
+            [IN_SMEM] + [IN_VMEM] * 6,
             flops=8 * tok * width * own_cols // 2,
             nbytes=16 * MIB,
             scratch=[pltpu.VMEM((tok, width), jnp.float32)],
         )(
             rank,
-            blocks[0],
-            blocks[1],
-            far,
-            far_near,
+            same_core,
+            other_core,
             norm_gain,
             cosine,
             sine,
@@ -582,18 +629,16 @@
         for bits in ODD:
             queries[bits] = swapped(query, bits)
     with jax.named_scope("new_tokens"):
-        heads, ctx = key_cache.shape[2], key_cache.shape[1]
-        values, summed, stats = call(
+        summed, stats = call(
             lambda *refs: new_kernel(scale, *refs),
             "new_tokens",
             [
-                jax.ShapeDtypeStruct((heads, dim, ctx), jnp.bfloat16),
                 jax.ShapeDtypeStruct((dim, tok * own_cols // dim), jnp.float32),
                 jax.ShapeDtypeStruct((8, tok * own_cols // dim), jnp.float32),
             ],
-            [IN_VMEM] * 7,
-            flops=64 * tok * width * dim,
-            nbytes=13 * MIB,
+            [IN_VMEM] * 6,
+            flops=16 * tok * width * dim,
+            nbytes=5 * MIB,
         )(
             query,
             normed,
@@ -601,7 +646,6 @@
             held(value_projection[0]),
             cosine,
             sine,
-            held(cached_value_rows[0]),
         )
 
     with jax.named_scope("cache_near"):
@@ -647,14 +691,14 @@
         )(rank, kept, *parts, summed, stats, held(w_out[0]))
     with jax.named_scope("reduce_cores"):
         pair = own + swapped(other, 1).astype(jnp.float32)
-    with jax.named_scope("reduce_chips"):
-        total = tokens[0].astype(jnp.float32) + pair[:count]
-        for i, bits in enumerate(SAME_CORE):
-            block = pair[(i + 1) * count : (i + 2) * count].astype(jnp.bfloat16)
-            total = total + swapped(block, bits).astype(jnp.float32)
-        layer_out = total.astype(jnp.bfloat16)
-    with jax.named_scope("hand_on"):
-        handed = passed_along(layer_out, "section", 1)
+    with jax.named_scope("reduce_on_next_section"):
+        total = 0.0
+        for i, bits in enumerate(EVEN):
+            block = pair[i * count : (i + 1) * count]
+            if bits == 0:
+                block = tokens[0].astype(jnp.float32) + block
+            total = total + onward(block.astype(jnp.bfloat16), bits).astype(jnp.float32)
+        handed = total.astype(jnp.bfloat16)
     return handed[None]
 
 

time: 72.1 us -> 67.8 us (0.940); the launches traced: 73 us -> 67.5 us
  Pallas kernels: 30.5 us -> 21.2 us
  starting transfers between devices: 18.4 us -> 20.3 us
  waiting for transfers between devices: 21.7 us -> 23 us
    ppermute x1 -> x4, starting transfers between devices: 1.84 us -> 7.14 us  [onward(): return lax.ppermute(block, ('section', 'seq'), route)]
    pallas_call x3, Pallas kernels: 13.2 us -> 8.26 us  [cache_part(): call(lambda *refs: cache_kernel(scale, order, *refs), name, outs, [IN_SME...]
    ppermute x19 -> x15, starting transfers between devices: 16.6 us -> 13.1 us  [swapped(): return lax.ppermute(block, 'seq', [(i, i ^ bits) for i in range(n)])]
    ppermute x1 -> x4, waiting for transfers between devices: 6.58 us -> 9.84 us  [onward(): return lax.ppermute(block, ('section', 'seq'), route)]
    pallas_call x1, Pallas kernels: 7.13 us -> 4.65 us  [cache_by_head(): call(by_head_kernel, 'cache_by_head', [jax.ShapeDtypeStruct((heads, ctx,...]
    ppermute x19 -> x15, waiting for transfers between devices: 15.2 us -> 13.1 us  [swapped(): return lax.ppermute(block, 'seq', [(i, i ^ bits) for i in range(n)])]
    pallas_call x1, Pallas kernels: 3.07 us -> 1.15 us  [on_device_owned(): call(lambda *refs: new_kernel(scale, *refs), 'new_tokens', [jax.ShapeDtyp...]
    broadcast_in_dim x0 -> x1, other arithmetic: none -> 0.72 us  [on_device_owned(): return handed[None]]
  transfers between devices with their start and end apart: 20 -> 19, of which waited for: 8 -> 10; matrix products, arithmetic and copies ran while one was open for 0% -> 0% of each run, Pallas kernels for 32% -> 21%
where the time goes in v3:
time: 67.8 us; the launch traced here: 67.5 us
  waiting for transfers between devices  23 us (34%)
  Pallas kernels  21.2 us (31%)
  starting transfers between devices  20.3 us (30%)
  between operations  1.69 us (2%)
  other arithmetic  1.18 us (2%)
    ppermute x15, waiting for transfers between devices, swapped(): return lax.ppermute(block, 'seq', [(i, i ^ bits) for i in range(n)])  13.1 us
    ppermute x15, starting transfers between devices, swapped(): return lax.ppermute(block, 'seq', [(i, i ^ bits) for i in range(n)])  13.1 us
    ppermute x4, waiting for transfers between devices, onward(): return lax.ppermute(block, ('section', 'seq'), route)  9.84 us
    pallas_call x3, Pallas kernels, cache_part(): call(lambda *refs: cache_kernel(scale, order, *refs), name, outs, [IN_SME...  8.26 us
    ppermute x4, starting transfers between devices, onward(): return lax.ppermute(block, ('section', 'seq'), route)  7.14 us
    pallas_call x1, Pallas kernels, cache_by_head(): call(by_head_kernel, 'cache_by_head', [jax.ShapeDtypeStruct((heads, ctx,...  4.65 us
    pallas_call x1, Pallas kernels, on_device_owned(): call(query_kernel, 'queries', [jax.ShapeDtypeStruct((tok, own_cols), jnp....  3.57 us
    pallas_call x1, Pallas kernels, on_device_owned(): call(output_kernel, 'project', [jax.ShapeDtypeStruct((tok // 2, width), j...  3.25 us
  transfers between devices with their start and end apart: 19, of which 10 were waited for; matrix products, arithmetic and copies ran while one was open for 0% of the time, Pallas kernels for 21%

profile of v3, /device:TPU:0, one launch (start us, length us, event | category | flops | bytes accessed | tf_op | source)
XLA Modules:
  0.0 67.5 jit_solution(1230903120516090234)
XLA Ops:
  0.0 3.9 %collective-permute-start.2 = (bf16[8,8192]{1,0:T(8,128)(2,1)}, bf16[8,8192]{1,0:T(8,128)(2,1)S(1)}, u32[]{:S(2)}, u32[]{:S(2)}) collective-permute-start(bf16[8,8192]{1,0:T(8,128)(2,1)} %bitcast.21), channel_id=1, source_target_pairs={{0,6},{1,7},{2,4},{3,5},{4,2},{5,3},{6,0},{7,1},{8,14},{9,15},{10,... | collective-permute-start | bytes 393224 | tf_op jit(solution)/shard_map/gather_tokens/ppermute | solution.py:182
  3.9 0.5 collective-permute-start.1
  4.5 4.7 %cache_by_head.1 = (bf16[8,2048,128]{2,1,0:T(8,128)(2,1)S(1)}, bf16[8,128,2048]{2,1,0:T(8,128)(2,1)S(1)}, f32[8,128]{1,0:T(8,128)S(1)}) custom-call(s32[1]{0:T(128)} %bitcast.1.rank.refs_0_, bf16[2048,8,128]{2,1,0:T(8,128)(2,1)} %bitcast.28, bf16[2048,8,128]{2,1,0:T(8,128)(2,1)} %bitcast.29), custom_call_target="tpu_custom_call" | custom-call | flops 10000000000 | bytes 4194304 | tf_op jit(solution)/shard_map/cache_layout/cache_by_head/pallas_call | solution.py:302
  10.8 0.2 fusion.2
  11.1 1.6 %collective-permute-done.3.refs_1_ = bf16[4,8,8192]{2,1,0:T(8,128)(2,1)S(1)} collective-permute-done((bf16[4,8,8192]{2,1,0:T(8,128)(2,1)S(1)}, bf16[4,8,8192]{2,1,0:T(8,128)(2,1)S(1)}, u32[]{:S(2)}, u32[]{:S(2)}) %collective-permute-start.3) | collective-permute-done | bytes 524320 | tf_op jit(solution)/shard_map/gather_tokens/ppermute | solution.py:182
  12.9 3.6 %queries.1 = (bf16[64,1024]{1,0:T(8,128)(2,1)S(1)}, bf16[64,8192]{1,0:T(8,128)(2,1)S(1)}) custom-call(s32[1]{0:T(128)} %bitcast.1.rank.refs_0_, bf16[4,8,8192]{2,1,0:T(8,128)(2,1)S(1)} %join_tokens.1.refs_0_, bf16[4,8,8192]{2,1,0:T(8,128)(2,1)S(1)} %collective-permute-done.3.refs_1_, bf16[1,8192]{1,0:T(2,128)(2,1)S(1)} %copy-done.3, ...), custom_call_target="tpu_custom_call" | custom-call | flops 2147483648 | bytes 16777216 | tf_op jit(solution)/shard_map/queries/queries/pallas_call | solution.py:606
  16.5 3.0 %collective-permute-start.7 = (bf16[64,1024]{1,0:T(8,128)(2,1)S(1)}, bf16[64,1024]{1,0:T(8,128)(2,1)S(1)}, u32[]{:S(2)}, u32[]{:S(2)}) collective-permute-start(bf16[64,1024]{1,0:T(8,128)(2,1)S(1)} %get-tuple-element.21.refs_2_.refs_0_), channel_id=1, source_target_pairs={{0,7},{1,6},{2,5},{3,4},{4,3},{5,2},{6,1},{7,0},{8,15},{9,14},{10,... | collective-permute-start | bytes 393224 | tf_op jit(solution)/shard_map/gather_queries/ppermute | solution.py:182
  19.9 2.4 %cache_near.1 = (f32[1,136,512]{2,1,0:T(8,128)S(1)}, bf16[1,144,512]{2,1,0:T(8,128)(2,1)S(1)}) custom-call(s32[1]{0:T(128)} %bitcast.1.rank.refs_0_, s32[2,16]{1,0:T(2,128)S(1)} %bitcast.25, bf16[64,1024]{1,0:T(8,128)(2,1)S(1)} %get-tuple-element.21.refs_2_.refs_0_, bf16[64,1024]{1,0:T(8,128)(2,1)S(1)} %collective-permute-done.4.refs_3_, ...), custom_call_target="tpu_custom_call" | custom-call | flops 536870912 | bytes 2097152 | tf_op jit(solution)/shard_map/cache_near/cache_near/pallas_call | solution.py:477
  22.3 1.1 %collective-permute-done.7.refs_2_ = bf16[64,1024]{1,0:T(8,128)(2,1)S(1)} collective-permute-done((bf16[64,1024]{1,0:T(8,128)(2,1)S(1)}, bf16[64,1024]{1,0:T(8,128)(2,1)S(1)}, u32[]{:S(2)}, u32[]{:S(2)}) %collective-permute-start.7) | collective-permute-done | bytes 131104 | tf_op jit(solution)/shard_map/gather_queries/ppermute | solution.py:182
  23.4 2.9 %collective-permute-done.6.refs_1_ = bf16[64,1024]{1,0:T(8,128)(2,1)S(1)} collective-permute-done((bf16[64,1024]{1,0:T(8,128)(2,1)S(1)}, bf16[64,1024]{1,0:T(8,128)(2,1)S(1)}, u32[]{:S(2)}, u32[]{:S(2)}) %collective-permute-start.6) | collective-permute-done | bytes 131104 | tf_op jit(solution)/shard_map/gather_queries/ppermute | solution.py:182
  26.4 0.2 collective-permute-start.8
  26.6 2.8 %cache_odd.1 = bf16[3,144,512]{2,1,0:T(8,128)(2,1)S(1)} custom-call(s32[1]{0:T(128)} %bitcast.1.rank.refs_0_, s32[2,16]{1,0:T(2,128)S(1)} %bitcast.26, bf16[3,64,1024]{2,1,0:T(8,128)(2,1)S(1)} %join_queries.1.refs_2_, bf16[8,2048,128]{2,1,0:T(8,128)(2,1)S(1)} %get-tuple-element.22.refs_4_.refs_3_, bf16[8,128,2048]{2,1,0:T(8,128)(2,1)S(1)} %get-tuple-element.23.refs_5_.refs_4_), custom_call_target="tpu_custom_call" | custom-call | flops 4026531840 | bytes 3145728 | tf_op jit(solution)/shard_map/cache_odd/cache_odd/pallas_call | solution.py:477
  29.4 1.3 %collective-permute-start.10 = (bf16[3,144,512]{2,1,0:T(8,128)(2,1)S(1)}, bf16[3,144,512]{2,1,0:T(8,128)(2,1)S(1)}, u32[]{:S(2)}, u32[]{:S(2)}) collective-permute-start(bf16[3,144,512]{2,1,0:T(8,128)(2,1)S(1)} %cache_odd.1), channel_id=1, source_target_pairs={{0,1},{1,0},{2,3},{3,2},{4,5},{5,4},{6,7},{7,6},{8,9},{9,8},{10,11... | collective-permute-start | bytes 1327112 | tf_op jit(solution)/shard_map/cache_odd/ppermute | solution.py:182
  30.8 3.0 %cache_even.1.own_rest = f32[3,136,512]{2,1,0:T(8,128)S(1)} custom-call(s32[1]{0:T(128)} %bitcast.1.rank.refs_0_, s32[2,16]{1,0:T(2,128)S(1)} %bitcast.27, bf16[3,64,1024]{2,1,0:T(8,128)(2,1)S(1)} %collective-permute-done.8.refs_2_, bf16[8,2048,128]{2,1,0:T(8,128)(2,1)S(1)} %get-tuple-element.22.refs_4_.refs_3_, ...), custom_call_target="tpu_custom_call" | custom-call | flops 805306368 | bytes 3145728 | tf_op jit(solution)/shard_map/cache_even/cache_even/pallas_call | solution.py:477
  33.8 0.3 merge_cores.1
  34.1 1.7 %collective-permute-start.11 = (bf16[144,512]{1,0:T(8,128)(2,1)S(1)}, bf16[144,512]{1,0:T(8,128)(2,1)S(1)}, u32[]{:S(2)}, u32[]{:S(2)}) collective-permute-start(bf16[144,512]{1,0:T(8,128)(2,1)S(1)} %get-tuple-element.27), channel_id=1, source_target_pairs={{0,2},{1,3},{2,0},{3,1},{4,6},{5,7},{6,4},{7,5},{8,10},{9,11},{10,... | collective-permute-start | bytes 442376 | tf_op jit(solution)/shard_map/exchange_parts/ppermute | solution.py:182
  35.8 0.4 collective-permute-start.12
  36.2 1.4 %collective-permute-start.13 = (bf16[144,512]{1,0:T(8,128)(2,1)S(1)}, bf16[144,512]{1,0:T(8,128)(2,1)S(1)}, u32[]{:S(2)}, u32[]{:S(2)}) collective-permute-start(bf16[144,512]{1,0:T(8,128)(2,1)S(1)} %get-tuple-element.29), channel_id=1, source_target_pairs={{0,6},{1,7},{2,4},{3,5},{4,2},{5,3},{6,0},{7,1},{8,14},{9,15},{10,... | collective-permute-start | bytes 442376 | tf_op jit(solution)/shard_map/exchange_parts/ppermute | solution.py:182
  37.7 1.1 %new_tokens.1 = (f32[128,512]{1,0:T(8,128)S(1)}, f32[8,512]{1,0:T(8,128)S(1)}) custom-call(bf16[64,1024]{1,0:T(8,128)(2,1)S(1)} %get-tuple-element.21.refs_2_.refs_0_, bf16[64,8192]{1,0:T(8,128)(2,1)S(1)} %get-tuple-element.30.refs_1_, bf16[8192,128]{1,0:T(8,128)(2,1)S(1)} %bitcast.19, bf16[8192,128]{1,0:T(8,128)(2,1)S(1)} %bitcast.20, ...), custom_call_target="tpu_custom_call" | custom-call | flops 1073741824 | bytes 5242880 | tf_op jit(solution)/shard_map/new_tokens/new_tokens/pallas_call | solution.py:632
  38.8 1.8 %collective-permute-done.11.got_a = bf16[144,512]{1,0:T(8,128)(2,1)S(1)} collective-permute-done((bf16[144,512]{1,0:T(8,128)(2,1)S(1)}, bf16[144,512]{1,0:T(8,128)(2,1)S(1)}, u32[]{:S(2)}, u32[]{:S(2)}) %collective-permute-start.11) | collective-permute-done | bytes 147488 | tf_op jit(solution)/shard_map/exchange_parts/ppermute | solution.py:182
  40.7 3.7 %collective-permute-done.12.got_b = bf16[144,512]{1,0:T(8,128)(2,1)S(1)} collective-permute-done((bf16[144,512]{1,0:T(8,128)(2,1)S(1)}, bf16[144,512]{1,0:T(8,128)(2,1)S(1)}, u32[]{:S(2)}, u32[]{:S(2)}) %collective-permute-start.12) | collective-permute-done | bytes 147488 | tf_op jit(solution)/shard_map/exchange_parts/ppermute | solution.py:182
  44.4 3.2 %project.1 = (f32[32,8192]{1,0:T(8,128)S(1)}, bf16[32,8192]{1,0:T(8,128)(2,1)S(1)}) custom-call(s32[1]{0:T(128)} %bitcast.1.rank.refs_0_, f32[136,512]{1,0:T(8,128)S(1)} %get-tuple-element.26.kept, bf16[144,512]{1,0:T(8,128)(2,1)S(1)} %collective-permute-done.11.got_a, bf16[144,512]{1,0:T(8,128)(2,1)S(1)} %collective-permute-done.12.got_b, ...), custom_call_target="tpu_custom_call" | custom-call | flops 2147483648 | bytes 18874368 | tf_op jit(solution)/shard_map/project/project/pallas_call | solution.py:677
  47.7 1.9 %collective-permute-done.14 = bf16[32,8192]{1,0:T(8,128)(2,1)S(1)} collective-permute-done((bf16[32,8192]{1,0:T(8,128)(2,1)S(1)}, bf16[32,8192]{1,0:T(8,128)(2,1)S(1)}, u32[]{:S(2)}, u32[]{:S(2)}) %collective-permute-start.14) | collective-permute-done | bytes 524320 | tf_op jit(solution)/shard_map/reduce_cores/ppermute | solution.py:182
  49.8 1.0 %collective-permute-start.15 = (bf16[8,8192]{1,0:T(8,128)(2,1)S(1)}, bf16[8,8192]{1,0:T(8,128)(2,1)S(1)}, u32[]{:S(2)}, u32[]{:S(2)}) collective-permute-start(bf16[8,8192]{1,0:T(8,128)(2,1)S(1)} %fusion), channel_id=1, source_target_pairs={{0,8},{1,9},{2,10},{3,11},{4,12},{5,13},{6,14},{7,15},{8,16},{9,17... | collective-permute-start | bytes 393224 | tf_op jit(solution)/shard_map/reduce_on_next_section/ppermute | solution.py:190
  50.8 3.5 %collective-permute-start.16 = (bf16[8,8192]{1,0:T(8,128)(2,1)S(1)}, bf16[8,8192]{1,0:T(8,128)(2,1)S(1)}, u32[]{:S(2)}, u32[]{:S(2)}) collective-permute-start(bf16[8,8192]{1,0:T(8,128)(2,1)S(1)} %get-tuple-element.37), channel_id=1, source_target_pairs={{0,10},{1,11},{2,8},{3,9},{4,14},{5,15},{6,12},{7,13},{8,18},{9,19... | collective-permute-start | bytes 393224 | tf_op jit(solution)/shard_map/reduce_on_next_section/ppermute | solution.py:190
  54.3 1.4 %collective-permute-start.18 = (bf16[8,8192]{1,0:T(8,128)(2,1)S(1)}, bf16[8,8192]{1,0:T(8,128)(2,1)S(1)}, u32[]{:S(2)}, u32[]{:S(2)}) collective-permute-start(bf16[8,8192]{1,0:T(8,128)(2,1)S(1)} %get-tuple-element.38), channel_id=1, source_target_pairs={{0,14},{1,15},{2,12},{3,13},{4,10},{5,11},{6,8},{7,9},{8,22},{9,23... | collective-permute-start | bytes 393224 | tf_op jit(solution)/shard_map/reduce_on_next_section/ppermute | solution.py:190
  55.7 1.3 %collective-permute-start.17 = (bf16[8,8192]{1,0:T(8,128)(2,1)S(1)}, bf16[8,8192]{1,0:T(8,128)(2,1)S(1)}, u32[]{:S(2)}, u32[]{:S(2)}) collective-permute-start(bf16[8,8192]{1,0:T(8,128)(2,1)S(1)} %get-tuple-element.39), channel_id=1, source_target_pairs={{0,12},{1,13},{2,14},{3,15},{4,8},{5,9},{6,10},{7,11},{8,20},{9,21... | collective-permute-start | bytes 393224 | tf_op jit(solution)/shard_map/reduce_on_next_section/ppermute | solution.py:190
  57.0 1.3 %collective-permute-done.15 = bf16[8,8192]{1,0:T(8,128)(2,1)S(1)} collective-permute-done((bf16[8,8192]{1,0:T(8,128)(2,1)S(1)}, bf16[8,8192]{1,0:T(8,128)(2,1)S(1)}, u32[]{:S(2)}, u32[]{:S(2)}) %collective-permute-start.15) | collective-permute-done | bytes 131104 | tf_op jit(solution)/shard_map/reduce_on_next_section/ppermute | solution.py:190
  58.3 3.7 %collective-permute-done.16 = bf16[8,8192]{1,0:T(8,128)(2,1)S(1)} collective-permute-done((bf16[8,8192]{1,0:T(8,128)(2,1)S(1)}, bf16[8,8192]{1,0:T(8,128)(2,1)S(1)}, u32[]{:S(2)}, u32[]{:S(2)}) %collective-permute-start.16) | collective-permute-done | bytes 131104 | tf_op jit(solution)/shard_map/reduce_on_next_section/ppermute | solution.py:190
  61.9 3.1 %collective-permute-done.18 = bf16[8,8192]{1,0:T(8,128)(2,1)S(1)} collective-permute-done((bf16[8,8192]{1,0:T(8,128)(2,1)S(1)}, bf16[8,8192]{1,0:T(8,128)(2,1)S(1)}, u32[]{:S(2)}, u32[]{:S(2)}) %collective-permute-start.18) | collective-permute-done | bytes 131104 | tf_op jit(solution)/shard_map/reduce_on_next_section/ppermute | solution.py:190
  65.1 1.7 %collective-permute-done.17 = bf16[8,8192]{1,0:T(8,128)(2,1)S(1)} collective-permute-done((bf16[8,8192]{1,0:T(8,128)(2,1)S(1)}, bf16[8,8192]{1,0:T(8,128)(2,1)S(1)}, u32[]{:S(2)}, u32[]{:S(2)}) %collective-permute-start.17) | collective-permute-done | bytes 131104 | tf_op jit(solution)/shard_map/reduce_on_next_section/ppermute | solution.py:190
  66.8 0.7 %fusion.1 = bf16[1,8,8192]{2,1,0:T(8,128)(2,1)} fusion(bf16[8,8192]{1,0:T(8,128)(2,1)S(1)} %collective-permute-done.18, bf16[8,8192]{1,0:T(8,128)(2,1)S(1)} %collective-permute-done.17, bf16[8,8192]{1,0:T(8,128)(2,1)S(1)} %collective-permute-done.16, bf16[8,8192]{1,0:T(8,128)(2,1)S(1)} %collective-permute-done.15), kind=kLoop, calls=%fused_computation.4 | loop fusion | flops 524288 | bytes 655360 | tf_op jit(solution)/shard_map/broadcast_in_dim | solution.py:702
  (52 shorter events, 1.3 us)
Async XLA Ops:
  0.0 10.6 %collective-permute-start.2 = (bf16[8,8192]{1,0:T(8,128)(2,1)}, bf16[8,8192]{1,0:T(8,128)(2,1)S(1)}, u32[]{:S(2)}, u32[]{:S(2)}) collective-permute-start(bf16[8,8192]{1,0:T(8,128)(2,1)} %bitcast.21), channel_id=1, source_target_pairs={{0,6},{1,7},{2,4},{3,5},{4,2},{5,3},{6,0},{7,1},{8,14},{9,15},{10,... | collective-permute-start | bytes 393224 | tf_op jit(solution)/shard_map/gather_tokens/ppermute | solution.py:182
  3.9 6.7 %collective-permute-start.1 = (bf16[8,8192]{1,0:T(8,128)(2,1)}, bf16[8,8192]{1,0:T(8,128)(2,1)S(1)}, u32[]{:S(2)}, u32[]{:S(2)}) collective-permute-start(bf16[8,8192]{1,0:T(8,128)(2,1)} %bitcast.22), channel_id=1, source_target_pairs={{0,4},{1,5},{2,6},{3,7},{4,0},{5,1},{6,2},{7,3},{8,12},{9,13},{10,... | collective-permute-start | bytes 393224 | tf_op jit(solution)/shard_map/gather_tokens/ppermute | solution.py:182
  4.4 6.3 %collective-permute-start = (bf16[8,8192]{1,0:T(8,128)(2,1)}, bf16[8,8192]{1,0:T(8,128)(2,1)S(1)}, u32[]{:S(2)}, u32[]{:S(2)}) collective-permute-start(bf16[8,8192]{1,0:T(8,128)(2,1)} %bitcast.23), channel_id=1, source_target_pairs={{0,2},{1,3},{2,0},{3,1},{4,6},{5,7},{6,4},{7,5},{8,10},{9,11},{10,... | collective-permute-start | bytes 393224 | tf_op jit(solution)/shard_map/gather_tokens/ppermute | solution.py:182
  4.5 8.2 %slice-start = ((s8[16777216]{0:T(1024)(128)(4,1)}), s8[4194304]{0:T(1024)(128)(4,1)S(1)}, s32[]{:S(2)}) async-start(s8[16777216]{0:T(1024)(128)(4,1)} %bitcast.13), calls=%async_computation | async-start | bytes 8388608
  4.5 6.2 %copy-start.2 = (bf16[1,8,8192]{2,1,0:T(8,128)(2,1)S(1)}, bf16[1,8,8192]{2,1,0:T(8,128)(2,1)}, u32[]{:S(2)}) copy-start(bf16[1,8,8192]{2,1,0:T(8,128)(2,1)} %param.10) | copy-start | bytes 393220
  4.5 8.2 %slice-start.1 = ((s8[16777216]{0:T(1024)(128)(4,1)}), s8[4194304]{0:T(1024)(128)(4,1)S(1)}, s32[]{:S(2)}) async-start(s8[16777216]{0:T(1024)(128)(4,1)} %bitcast.13), calls=%async_computation.1 | async-start | bytes 8388608
  4.5 8.2 %slice-start.2 = ((s8[16777216]{0:T(1024)(128)(4,1)}), s8[4194304]{0:T(1024)(128)(4,1)S(1)}, s32[]{:S(2)}) async-start(s8[16777216]{0:T(1024)(128)(4,1)} %bitcast.13), calls=%async_computation.2 | async-start | bytes 8388608
  4.5 8.4 %slice-start.3 = ((s8[16777216]{0:T(1024)(128)(4,1)}), s8[4194304]{0:T(1024)(128)(4,1)S(1)}, s32[]{:S(2)}) async-start(s8[16777216]{0:T(1024)(128)(4,1)} %bitcast.13), calls=%async_computation.3 | async-start | bytes 8388608
  4.5 8.4 %copy-start.3 = (bf16[1,8192]{1,0:T(2,128)(2,1)S(1)}, bf16[1,8192]{1,0:T(2,128)(2,1)}, u32[]{:S(2)}) copy-start(bf16[1,8192]{1,0:T(2,128)(2,1)} %refs_2_.1) | copy-start | bytes 49156
  10.7 2.0 %collective-permute-start.3 = (bf16[4,8,8192]{2,1,0:T(8,128)(2,1)S(1)}, bf16[4,8,8192]{2,1,0:T(8,128)(2,1)S(1)}, u32[]{:S(2)}, u32[]{:S(2)}) collective-permute-start(bf16[4,8,8192]{2,1,0:T(8,128)(2,1)S(1)} %join_tokens.1.refs_0_), channel_id=1, source_target_pairs={{0,1},{1,0},{2,3},{3,2},{4,5},{5,4},{6,7},{7,6},{8,9},{9,8},{10,11... | collective-permute-start | bytes 1572872 | tf_op jit(solution)/shard_map/gather_tokens/ppermute | solution.py:182
  12.9 7.0 %copy-start.4 = (s32[1,2,16]{2,1,0:T(2,128)S(1)}, s32[1,2,16]{2,1,0:T(2,128)}, u32[]{:S(2)}) copy-start(s32[1,2,16]{2,1,0:T(2,128)} %param.18) | copy-start | bytes 388
  16.4 3.4 %collective-permute-start.4 = (bf16[64,1024]{1,0:T(8,128)(2,1)S(1)}, bf16[64,1024]{1,0:T(8,128)(2,1)S(1)}, u32[]{:S(2)}, u32[]{:S(2)}) collective-permute-start(bf16[64,1024]{1,0:T(8,128)(2,1)S(1)} %get-tuple-element.21.refs_2_.refs_0_), channel_id=1, source_target_pairs={{0,1},{1,0},{2,3},{3,2},{4,5},{5,4},{6,7},{7,6},{8,9},{9,8},{10,11... | collective-permute-start | bytes 393224 | tf_op jit(solution)/shard_map/gather_queries/ppermute | solution.py:182
  16.5 6.9 %collective-permute-start.7 = (bf16[64,1024]{1,0:T(8,128)(2,1)S(1)}, bf16[64,1024]{1,0:T(8,128)(2,1)S(1)}, u32[]{:S(2)}, u32[]{:S(2)}) collective-permute-start(bf16[64,1024]{1,0:T(8,128)(2,1)S(1)} %get-tuple-element.21.refs_2_.refs_0_), channel_id=1, source_target_pairs={{0,7},{1,6},{2,5},{3,4},{4,3},{5,2},{6,1},{7,0},{8,15},{9,14},{10,... | collective-permute-start | bytes 393224 | tf_op jit(solution)/shard_map/gather_queries/ppermute | solution.py:182
  19.6 6.8 %collective-permute-start.6 = (bf16[64,1024]{1,0:T(8,128)(2,1)S(1)}, bf16[64,1024]{1,0:T(8,128)(2,1)S(1)}, u32[]{:S(2)}, u32[]{:S(2)}) collective-permute-start(bf16[64,1024]{1,0:T(8,128)(2,1)S(1)} %get-tuple-element.21.refs_2_.refs_0_), channel_id=1, source_target_pairs={{0,5},{1,4},{2,7},{3,6},{4,1},{5,0},{6,3},{7,2},{8,13},{9,12},{10,... | collective-permute-start | bytes 393224 | tf_op jit(solution)/shard_map/gather_queries/ppermute | solution.py:182
  19.7 6.7 %collective-permute-start.5 = (bf16[64,1024]{1,0:T(8,128)(2,1)S(1)}, bf16[64,1024]{1,0:T(8,128)(2,1)S(1)}, u32[]{:S(2)}, u32[]{:S(2)}) collective-permute-start(bf16[64,1024]{1,0:T(8,128)(2,1)S(1)} %get-tuple-element.21.refs_2_.refs_0_), channel_id=1, source_target_pairs={{0,3},{1,2},{2,1},{3,0},{4,7},{5,6},{6,5},{7,4},{8,11},{9,10},{10,... | collective-permute-start | bytes 393224 | tf_op jit(solution)/shard_map/gather_queries/ppermute | solution.py:182
  26.4 4.4 %collective-permute-start.8 = (bf16[3,64,1024]{2,1,0:T(8,128)(2,1)S(1)}, bf16[3,64,1024]{2,1,0:T(8,128)(2,1)S(1)}, u32[]{:S(2)}, u32[]{:S(2)}) collective-permute-start(bf16[3,64,1024]{2,1,0:T(8,128)(2,1)S(1)} %join_queries.1.refs_2_), channel_id=1, source_target_pairs={{0,1},{1,0},{2,3},{3,2},{4,5},{5,4},{6,7},{7,6},{8,9},{9,8},{10,11... | collective-permute-start | bytes 1179656 | tf_op jit(solution)/shard_map/gather_queries/ppermute | solution.py:182
  26.6 11.1 %copy-start.1 = (bf16[1,8192,128]{2,1,0:T(8,128)(2,1)S(1)}, bf16[1,8192,128]{2,1,0:T(8,128)(2,1)}, u32[]{:S(2)}) copy-start(bf16[1,8192,128]{2,1,0:T(8,128)(2,1)} %param.14) | copy-start | bytes 6291460
  26.6 17.8 %slice-start.4 = ((s8[16777216]{0:T(1024)(128)(4,1)}), s8[4194304]{0:T(1024)(128)(4,1)S(1)}, s32[]{:S(2)}) async-start(s8[16777216]{0:T(1024)(128)(4,1)} %bitcast.16), calls=%async_computation.4 | async-start | bytes 8388608
  26.6 17.8 %slice-start.5 = ((s8[16777216]{0:T(1024)(128)(4,1)}), s8[4194304]{0:T(1024)(128)(4,1)S(1)}, s32[]{:S(2)}) async-start(s8[16777216]{0:T(1024)(128)(4,1)} %bitcast.16), calls=%async_computation.5 | async-start | bytes 8388608
  29.4 4.4 %collective-permute-start.10 = (bf16[3,144,512]{2,1,0:T(8,128)(2,1)S(1)}, bf16[3,144,512]{2,1,0:T(8,128)(2,1)S(1)}, u32[]{:S(2)}, u32[]{:S(2)}) collective-permute-start(bf16[3,144,512]{2,1,0:T(8,128)(2,1)S(1)} %cache_odd.1), channel_id=1, source_target_pairs={{0,1},{1,0},{2,3},{3,2},{4,5},{5,4},{6,7},{7,6},{8,9},{9,8},{10,11... | collective-permute-start | bytes 1327112 | tf_op jit(solution)/shard_map/cache_odd/ppermute | solution.py:182
  30.7 7.0 %copy-start = (bf16[1,8192,128]{2,1,0:T(8,128)(2,1)S(1)}, bf16[1,8192,128]{2,1,0:T(8,128)(2,1)}, u32[]{:S(2)}) copy-start(bf16[1,8192,128]{2,1,0:T(8,128)(2,1)} %param.13) | copy-start | bytes 6291460
  30.7 13.7 %slice-start.6 = ((s8[16777216]{0:T(1024)(128)(4,1)}), s8[4194304]{0:T(1024)(128)(4,1)S(1)}, s32[]{:S(2)}) async-start(s8[16777216]{0:T(1024)(128)(4,1)} %bitcast.16), calls=%async_computation.6 | async-start | bytes 8388608
  30.7 13.7 %slice-start.7 = ((s8[16777216]{0:T(1024)(128)(4,1)}), s8[4194304]{0:T(1024)(128)(4,1)S(1)}, s32[]{:S(2)}) async-start(s8[16777216]{0:T(1024)(128)(4,1)} %bitcast.16), calls=%async_computation.7 | async-start | bytes 8388608
  30.7 3.1 %collective-permute-start.9 = (bf16[1,144,512]{2,1,0:T(8,128)(2,1)S(1)}, bf16[1,144,512]{2,1,0:T(8,128)(2,1)S(1)}, u32[]{:S(2)}, u32[]{:S(2)}) collective-permute-start(bf16[1,144,512]{2,1,0:T(8,128)(2,1)S(1)} %get-tuple-element.25), channel_id=1, source_target_pairs={{0,1},{1,0},{2,3},{3,2},{4,5},{5,4},{6,7},{7,6},{8,9},{9,8},{10,11... | collective-permute-start | bytes 442376 | tf_op jit(solution)/shard_map/cache_near/ppermute | solution.py:182
  34.1 6.6 %collective-permute-start.11 = (bf16[144,512]{1,0:T(8,128)(2,1)S(1)}, bf16[144,512]{1,0:T(8,128)(2,1)S(1)}, u32[]{:S(2)}, u32[]{:S(2)}) collective-permute-start(bf16[144,512]{1,0:T(8,128)(2,1)S(1)} %get-tuple-element.27), channel_id=1, source_target_pairs={{0,2},{1,3},{2,0},{3,1},{4,6},{5,7},{6,4},{7,5},{8,10},{9,11},{10,... | collective-permute-start | bytes 442376 | tf_op jit(solution)/shard_map/exchange_parts/ppermute | solution.py:182
  35.8 8.5 %collective-permute-start.12 = (bf16[144,512]{1,0:T(8,128)(2,1)S(1)}, bf16[144,512]{1,0:T(8,128)(2,1)S(1)}, u32[]{:S(2)}, u32[]{:S(2)}) collective-permute-start(bf16[144,512]{1,0:T(8,128)(2,1)S(1)} %get-tuple-element.28), channel_id=1, source_target_pairs={{0,4},{1,5},{2,6},{3,7},{4,0},{5,1},{6,2},{7,3},{8,12},{9,13},{10,... | collective-permute-start | bytes 442376 | tf_op jit(solution)/shard_map/exchange_parts/ppermute | solution.py:182
  36.2 8.1 %collective-permute-start.13 = (bf16[144,512]{1,0:T(8,128)(2,1)S(1)}, bf16[144,512]{1,0:T(8,128)(2,1)S(1)}, u32[]{:S(2)}, u32[]{:S(2)}) collective-permute-start(bf16[144,512]{1,0:T(8,128)(2,1)S(1)} %get-tuple-element.29), channel_id=1, source_target_pairs={{0,6},{1,7},{2,4},{3,5},{4,2},{5,3},{6,0},{7,1},{8,14},{9,15},{10,... | collective-permute-start | bytes 442376 | tf_op jit(solution)/shard_map/exchange_parts/ppermute | solution.py:182
  47.6 2.0 %collective-permute-start.14 = (bf16[32,8192]{1,0:T(8,128)(2,1)S(1)}, bf16[32,8192]{1,0:T(8,128)(2,1)S(1)}, u32[]{:S(2)}, u32[]{:S(2)}) collective-permute-start(bf16[32,8192]{1,0:T(8,128)(2,1)S(1)} %get-tuple-element.34), channel_id=1, source_target_pairs={{0,1},{1,0},{2,3},{3,2},{4,5},{5,4},{6,7},{7,6},{8,9},{9,8},{10,11... | collective-permute-start | bytes 1572872 | tf_op jit(solution)/shard_map/reduce_cores/ppermute | solution.py:182
  49.8 8.4 %collective-permute-start.15 = (bf16[8,8192]{1,0:T(8,128)(2,1)S(1)}, bf16[8,8192]{1,0:T(8,128)(2,1)S(1)}, u32[]{:S(2)}, u32[]{:S(2)}) collective-permute-start(bf16[8,8192]{1,0:T(8,128)(2,1)S(1)} %fusion), channel_id=1, source_target_pairs={{0,8},{1,9},{2,10},{3,11},{4,12},{5,13},{6,14},{7,15},{8,16},{9,17... | collective-permute-start | bytes 393224 | tf_op jit(solution)/shard_map/reduce_on_next_section/ppermute | solution.py:190
  50.8 11.1 %collective-permute-start.16 = (bf16[8,8192]{1,0:T(8,128)(2,1)S(1)}, bf16[8,8192]{1,0:T(8,128)(2,1)S(1)}, u32[]{:S(2)}, u32[]{:S(2)}) collective-permute-start(bf16[8,8192]{1,0:T(8,128)(2,1)S(1)} %get-tuple-element.37), channel_id=1, source_target_pairs={{0,10},{1,11},{2,8},{3,9},{4,14},{5,15},{6,12},{7,13},{8,18},{9,19... | collective-permute-start | bytes 393224 | tf_op jit(solution)/shard_map/reduce_on_next_section/ppermute | solution.py:190
  54.3 10.8 %collective-permute-start.18 = (bf16[8,8192]{1,0:T(8,128)(2,1)S(1)}, bf16[8,8192]{1,0:T(8,128)(2,1)S(1)}, u32[]{:S(2)}, u32[]{:S(2)}) collective-permute-start(bf16[8,8192]{1,0:T(8,128)(2,1)S(1)} %get-tuple-element.38), channel_id=1, source_target_pairs={{0,14},{1,15},{2,12},{3,13},{4,10},{5,11},{6,8},{7,9},{8,22},{9,23... | collective-permute-start | bytes 393224 | tf_op jit(solution)/shard_map/reduce_on_next_section/ppermute | solution.py:190
  55.7 11.1 %collective-permute-start.17 = (bf16[8,8192]{1,0:T(8,128)(2,1)S(1)}, bf16[8,8192]{1,0:T(8,128)(2,1)S(1)}, u32[]{:S(2)}, u32[]{:S(2)}) collective-permute-start(bf16[8,8192]{1,0:T(8,128)(2,1)S(1)} %get-tuple-element.39), channel_id=1, source_target_pairs={{0,12},{1,13},{2,14},{3,15},{4,8},{5,9},{6,10},{7,11},{8,20},{9,21... | collective-permute-start | bytes 393224 | tf_op jit(solution)/shard_map/reduce_on_next_section/ppermute | solution.py:190

commit v4 on v3

--- a/solution.py
+++ b/solution.py
@@ -1,3 +1,5 @@
+import functools
+
 import jax
 import jax.numpy as jnp
 from jax import lax
@@ -271,25 +273,29 @@
 
 
 def by_head_kernel(rank, keys, values, keys_out, values_out, done, keys_in, values_in, sems):
-    block = keys.shape[0] // sems.shape[1]
-    copies = []
-    for i in range(sems.shape[1]):
-        at = pl.ds(i * block, block)
-        copies.append(
-            [
-                pltpu.make_async_copy(source.at[at], target.at[at], sems.at[which, i])
-                for which, (source, target) in enumerate([(keys, keys_in), (values, values_in)])
-            ]
-        )
-    for pair in copies:
-        for copy in pair:
+    blocks = sems.shape[1]
+    block = keys.shape[0] // blocks
+
+    def copies(i):
+        at = pl.ds(pl.multiple_of(i * block, block), block)
+        return [
+            pltpu.make_async_copy(source.at[at], target.at[at], sems.at[which, i])
+            for which, (source, target) in enumerate([(keys, keys_in), (values, values_in)])
+        ]
+
+    @pl.loop(0, blocks)
+    def _(i):
+        for copy in copies(i):
             copy.start()
+
     done[...] = jnp.zeros_like(done)
-    for i, pair in enumerate(copies):
-        at = pl.ds(i * block, block)
-        pair[0].wait()
+
+    @pl.loop(0, blocks)
+    def _(i):
+        at = pl.ds(pl.multiple_of(i * block, block), block)
+        for copy in copies(i):
+            copy.wait()
         keys_out[:, at, :] = jnp.swapaxes(keys_in[at], 0, 1)
-        pair[1].wait()
         turned = jnp.swapaxes(values_in[at], 0, 1)
         for g in range(turned.shape[0]):
             values_out[g, :, at] = turned[g].T
@@ -375,84 +381,92 @@
 def cache_kernel(scale, order, rank, mask, *refs):
     n = len(order)
     given = 1 if len(refs[0].shape) == 3 else n
-    queries, (keys, values), outs = refs[:given], refs[given : given + 2], refs[given + 2 : -4]
+    queries, (keys, values), outs = refs[:given], refs[given : given + 2], refs[given + 2 : -5]
     if given < n:
         queries = [queries[0].at[i] for i in range(n)]
-    q_rows, summed, visible, scores = refs[-4:]
+    q_rows, summed, visible, scores, levels = refs[-5:]
     dim = keys.shape[2]
     heads = queries[0].shape[1] // dim
     cols = heads * QB
     groups = [rank[0] ^ bits for bits in order]
     own = [bits for bits in order if bits in EVEN]
-    for q_block in range(mask.shape[0]):
-        count = jnp.int32(0)
+    blocks = mask.shape[0]
+    place = jnp.int32(0)
+    ends, singles = [], []
+    for q_block in range(blocks):
         for b in range(mask.shape[1]):
-            visible[count] = b
-            count = count + (mask[q_block, b] > 0).astype(jnp.int32)
-        for e in range(4):
-            visible[count + e] = 0
+            visible[place] = b
+            place = place + (mask[q_block, b] > 0).astype(jnp.int32)
+        visible[place] = 0
+        odd = place % 2
+        place = place + odd
+        ends.append(place // 2)
+        singles.append(jnp.where(odd == 1, place // 2 - 1, -1))
         for i in range(n):
-            q_rows[i] = query_rows(queries[i], q_block, heads, dim)
-            summed[i] = jnp.zeros((dim, cols), jnp.float32)
-
-        def places(pair):
-            return [pl.multiple_of(visible[2 * pair + e] * KB, KB) for e in range(2)]
-
-        def score(pair):
-            at = places(pair)
-            hidden = jnp.where(2 * pair + 1 < count, jnp.float32(0.0), jnp.float32(neg_fill))
-            products = [
-                matmul_nt(
-                    jnp.concatenate([keys[g, pl.ds(a, KB), :] for a in at], axis=0), q_rows[i]
-                )
-                for i, g in enumerate(groups)
-            ]
-            tops = []
-            for i in range(n):
-                first = products[i][:KB] * scale
-                second = products[i][KB:] * scale + hidden
-                scores[i, :KB] = first
-                scores[i, KB:] = second
-                tops.append(jnp.max(jnp.maximum(first, second), axis=0, keepdims=True))
-            return tops
-
-        def step(pair, carry):
-            levels, scaled = [], []
-            for i in range(n):
-                top, total, pair_top = carry[3 * i : 3 * i + 3]
-                new_top = jnp.maximum(top, pair_top)
-                weights = jnp.exp2(scores[i] - new_top)
-                factor = jnp.exp2(top - new_top)
-                total = total * factor + jnp.sum(weights, axis=0, keepdims=True)
-                levels += [new_top, total]
-                scaled.append((factor, weights.astype(jnp.bfloat16)))
-            at = places(pair)
-            products = [
-                jnp.dot(
-                    jnp.concatenate([values[g, :, pl.ds(a, KB)] for a in at], axis=1),
-                    scaled[i][1],
-                    preferred_element_type=jnp.float32,
-                )
-                for i, g in enumerate(groups)
-            ]
-            tops = score(pair + 1)
-            after = []
-            for i in range(n):
-                summed[i] = summed[i] * scaled[i][0] + products[i]
-                after += [levels[2 * i], levels[2 * i + 1], tops[i]]
-            return tuple(after)
-
-        start = []
-        for top in score(0):
-            start += [
-                jnp.full((1, cols), neg_fill, jnp.float32),
-                jnp.zeros((1, cols), jnp.float32),
-                top,
-            ]
-        ended = lax.fori_loop(0, (count + 1) // 2, step, tuple(start))
+            q_rows[q_block, i] = query_rows(queries[i], q_block, heads, dim)
+            summed[q_block, i] = jnp.zeros((dim, cols), jnp.float32)
+            levels[q_block, i, 0:1] = jnp.full((1, cols), neg_fill, jnp.float32)
+            levels[q_block, i, 1:2] = jnp.zeros((1, cols), jnp.float32)
+    for e in range(2):
+        visible[place + e] = 0
+
+    def q_block_of(pair):
+        return sum((pair >= end).astype(jnp.int32) for end in ends[:-1])
+
+    def places(pair):
+        return [pl.multiple_of(visible[2 * pair + e] * KB, KB) for e in range(2)]
+
+    def score(pair):
+        at = places(pair)
+        q_block = q_block_of(pair)
+        single = functools.reduce(jnp.logical_or, [pair == one for one in singles])
+        hidden = jnp.where(single, jnp.float32(neg_fill), jnp.float32(0.0))
+        products = [
+            matmul_nt(
+                jnp.concatenate([keys[g, pl.ds(a, KB), :] for a in at], axis=0),
+                q_rows[q_block, i],
+            )
+            for i, g in enumerate(groups)
+        ]
+        tops = []
+        for i in range(n):
+            first = products[i][:KB] * scale
+            second = products[i][KB:] * scale + hidden
+            scores[i, :KB] = first
+            scores[i, KB:] = second
+            tops.append(jnp.max(jnp.maximum(first, second), axis=0, keepdims=True))
+        return tops
+
+    def step(pair, tops):
+        q_block = q_block_of(pair)
+        scaled = []
+        for i in range(n):
+            top, total = levels[q_block, i, 0:1], levels[q_block, i, 1:2]
+            new_top = jnp.maximum(top, tops[i])
+            weights = jnp.exp2(scores[i] - new_top)
+            factor = jnp.exp2(top - new_top)
+            levels[q_block, i, 0:1] = new_top
+            levels[q_block, i, 1:2] = total * factor + jnp.sum(weights, axis=0, keepdims=True)
+            scaled.append((factor, weights.astype(jnp.bfloat16)))
+        at = places(pair)
+        products = [
+            jnp.dot(
+                jnp.concatenate([values[g, :, pl.ds(a, KB)] for a in at], axis=1),
+                scaled[i][1],
+                preferred_element_type=jnp.float32,
+            )
+            for i, g in enumerate(groups)
+        ]
+        tops = score(pair + 1)
+        for i in range(n):
+            summed[q_block, i] = summed[q_block, i] * scaled[i][0] + products[i]
+        return tuple(tops)
+
+    lax.fori_loop(0, ends[-1], step, tuple(score(jnp.int32(0))))
+    for q_block in range(blocks):
         at = slice(q_block * cols, (q_block + 1) * cols)
         for i, bits in enumerate(order):
-            top, total = ended[3 * i], ended[3 * i + 1]
+            top, total = levels[q_block, i, 0:1], levels[q_block, i, 1:2]
             seen = total > 0.0
             safe = jnp.where(seen, total, 1.0)
             level = jnp.where(seen, top + jnp.log2(safe), neg_fill)
@@ -460,7 +474,7 @@
                 out, place = outs[0], own.index(bits)
             else:
                 out, place = outs[-1], i - len(own)
-            out[place, 0:dim, at] = (summed[i] * (1.0 / safe)).astype(out.dtype)
+            out[place, 0:dim, at] = (summed[q_block, i] * (1.0 / safe)).astype(out.dtype)
             out[place, dim:, at] = split_rows(level, out.shape[1] - dim).astype(out.dtype)
 
 
@@ -482,10 +496,11 @@
         flops=(2 if own else 10) * n * queries[0].shape[-2] * heads * ctx * dim,
         nbytes=n * MIB,
         scratch=[
-            pltpu.VMEM((n, cols, dim), jnp.bfloat16),
-            pltpu.VMEM((n, dim, cols), jnp.float32),
-            pltpu.SMEM((mask.shape[1] + 4,), jnp.int32),
+            pltpu.VMEM((mask.shape[0], n, cols, dim), jnp.bfloat16),
+            pltpu.VMEM((mask.shape[0], n, dim, cols), jnp.float32),
+            pltpu.SMEM((mask.size + 4,), jnp.int32),
             pltpu.VMEM((n, 2 * KB, cols), jnp.float32),
+            pltpu.VMEM((mask.shape[0], n, 8, cols), jnp.float32),
         ],
     )(rank, mask, *queries, held(keys), held(values))
 

time: 67.8 us -> 67.3 us (level)
    pallas_call x3, Pallas kernels: 8.26 us -> 7.56 us  [cache_part(): call(lambda *refs: cache_kernel(scale, order, *refs), name, outs, [IN_SME...]
  transfers between devices with their start and end apart: 19 -> 19, of which waited for: 10 -> 10; matrix products, arithmetic and copies ran while one was open for 0% -> 0% of each run, Pallas kernels for 21% -> 20%
where the time goes in v4:
time: 67.3 us; the launch traced here: 67.2 us
  waiting for transfers between devices  23.3 us (35%)
  Pallas kernels  20.6 us (31%)
  starting transfers between devices  20.3 us (30%)
  between operations  1.72 us (3%)
  other arithmetic  1.18 us (2%)
    ppermute x15, waiting for transfers between devices, swapped(): return lax.ppermute(block, 'seq', [(i, i ^ bits) for i in range(n)])  13.3 us
    ppermute x15, starting transfers between devices, swapped(): return lax.ppermute(block, 'seq', [(i, i ^ bits) for i in range(n)])  12.8 us
    ppermute x4, waiting for transfers between devices, onward(): return lax.ppermute(block, ('section', 'seq'), route)  10 us
    pallas_call x3, Pallas kernels, cache_part(): call(lambda *refs: cache_kernel(scale, order, *refs), name, outs, [IN_SME...  7.56 us
    ppermute x4, starting transfers between devices, onward(): return lax.ppermute(block, ('section', 'seq'), route)  7.44 us
    pallas_call x1, Pallas kernels, cache_by_head(): call(by_head_kernel, 'cache_by_head', [jax.ShapeDtypeStruct((heads, ctx,...  4.79 us
    pallas_call x1, Pallas kernels, on_device_owned(): call(query_kernel, 'queries', [jax.ShapeDtypeStruct((tok, own_cols), jnp....  3.57 us
    pallas_call x1, Pallas kernels, on_device_owned(): call(output_kernel, 'project', [jax.ShapeDtypeStruct((tok // 2, width), j...  3.25 us
  transfers between devices with their start and end apart: 19, of which 10 were waited for; matrix products, arithmetic and copies ran while one was open for 0% of the time, Pallas kernels for 20%

profile of v4, /device:TPU:0, one launch (start us, length us, event | category | flops | bytes accessed | tf_op | source)
XLA Modules:
  0.0 67.2 jit_solution(3223658222116267733)
XLA Ops:
  0.0 3.9 %collective-permute-start.2 = (bf16[8,8192]{1,0:T(8,128)(2,1)}, bf16[8,8192]{1,0:T(8,128)(2,1)S(1)}, u32[]{:S(2)}, u32[]{:S(2)}) collective-permute-start(bf16[8,8192]{1,0:T(8,128)(2,1)} %bitcast.21), channel_id=1, source_target_pairs={{0,6},{1,7},{2,4},{3,5},{4,2},{5,3},{6,0},{7,1},{8,14},{9,15},{10,... | collective-permute-start | bytes 393224 | tf_op jit(solution)/shard_map/gather_tokens/ppermute | solution.py:184
  3.9 0.5 collective-permute-start.1
  4.5 4.8 %cache_by_head.1 = (bf16[8,2048,128]{2,1,0:T(8,128)(2,1)S(1)}, bf16[8,128,2048]{2,1,0:T(8,128)(2,1)S(1)}, f32[8,128]{1,0:T(8,128)S(1)}) custom-call(s32[1]{0:T(128)} %bitcast.1.rank.refs_0_, bf16[2048,8,128]{2,1,0:T(8,128)(2,1)} %bitcast.28, bf16[2048,8,128]{2,1,0:T(8,128)(2,1)} %bitcast.29), custom_call_target="tpu_custom_call" | custom-call | flops 10000000000 | bytes 4194304 | tf_op jit(solution)/shard_map/cache_layout/cache_by_head/pallas_call | solution.py:308
  11.2 1.6 %collective-permute-done.3.refs_1_ = bf16[4,8,8192]{2,1,0:T(8,128)(2,1)S(1)} collective-permute-done((bf16[4,8,8192]{2,1,0:T(8,128)(2,1)S(1)}, bf16[4,8,8192]{2,1,0:T(8,128)(2,1)S(1)}, u32[]{:S(2)}, u32[]{:S(2)}) %collective-permute-start.3) | collective-permute-done | bytes 524320 | tf_op jit(solution)/shard_map/gather_tokens/ppermute | solution.py:184
  12.9 3.6 %queries.1 = (bf16[64,1024]{1,0:T(8,128)(2,1)S(1)}, bf16[64,8192]{1,0:T(8,128)(2,1)S(1)}) custom-call(s32[1]{0:T(128)} %bitcast.1.rank.refs_0_, bf16[4,8,8192]{2,1,0:T(8,128)(2,1)S(1)} %join_tokens.1.refs_0_, bf16[4,8,8192]{2,1,0:T(8,128)(2,1)S(1)} %collective-permute-done.3.refs_1_, bf16[1,8192]{1,0:T(2,128)(2,1)S(1)} %copy-done.3, ...), custom_call_target="tpu_custom_call" | custom-call | flops 2147483648 | bytes 16777216 | tf_op jit(solution)/shard_map/queries/queries/pallas_call | solution.py:621
  16.6 2.9 %collective-permute-start.7 = (bf16[64,1024]{1,0:T(8,128)(2,1)S(1)}, bf16[64,1024]{1,0:T(8,128)(2,1)S(1)}, u32[]{:S(2)}, u32[]{:S(2)}) collective-permute-start(bf16[64,1024]{1,0:T(8,128)(2,1)S(1)} %get-tuple-element.21.refs_2_.refs_0_), channel_id=1, source_target_pairs={{0,7},{1,6},{2,5},{3,4},{4,3},{5,2},{6,1},{7,0},{8,15},{9,14},{10,... | collective-permute-start | bytes 393224 | tf_op jit(solution)/shard_map/gather_queries/ppermute | solution.py:184
  19.5 0.3 collective-permute-start.6
  19.9 2.3 %cache_near.1 = (f32[1,136,512]{2,1,0:T(8,128)S(1)}, bf16[1,144,512]{2,1,0:T(8,128)(2,1)S(1)}) custom-call(s32[1]{0:T(128)} %bitcast.1.rank.refs_0_, s32[2,16]{1,0:T(2,128)S(1)} %bitcast.25, bf16[64,1024]{1,0:T(8,128)(2,1)S(1)} %get-tuple-element.21.refs_2_.refs_0_, bf16[64,1024]{1,0:T(8,128)(2,1)S(1)} %collective-permute-done.4.refs_3_, ...), custom_call_target="tpu_custom_call" | custom-call | flops 536870912 | bytes 2097152 | tf_op jit(solution)/shard_map/cache_near/cache_near/pallas_call | solution.py:491
  22.2 1.3 %collective-permute-done.7.refs_2_ = bf16[64,1024]{1,0:T(8,128)(2,1)S(1)} collective-permute-done((bf16[64,1024]{1,0:T(8,128)(2,1)S(1)}, bf16[64,1024]{1,0:T(8,128)(2,1)S(1)}, u32[]{:S(2)}, u32[]{:S(2)}) %collective-permute-start.7) | collective-permute-done | bytes 131104 | tf_op jit(solution)/shard_map/gather_queries/ppermute | solution.py:184
  23.4 3.0 %collective-permute-done.6.refs_1_ = bf16[64,1024]{1,0:T(8,128)(2,1)S(1)} collective-permute-done((bf16[64,1024]{1,0:T(8,128)(2,1)S(1)}, bf16[64,1024]{1,0:T(8,128)(2,1)S(1)}, u32[]{:S(2)}, u32[]{:S(2)}) %collective-permute-start.6) | collective-permute-done | bytes 131104 | tf_op jit(solution)/shard_map/gather_queries/ppermute | solution.py:184
  26.4 0.2 collective-permute-start.8
  26.7 2.6 %cache_odd.1 = bf16[3,144,512]{2,1,0:T(8,128)(2,1)S(1)} custom-call(s32[1]{0:T(128)} %bitcast.1.rank.refs_0_, s32[2,16]{1,0:T(2,128)S(1)} %bitcast.26, bf16[3,64,1024]{2,1,0:T(8,128)(2,1)S(1)} %join_queries.1.refs_2_, bf16[8,2048,128]{2,1,0:T(8,128)(2,1)S(1)} %get-tuple-element.22.refs_4_.refs_3_, bf16[8,128,2048]{2,1,0:T(8,128)(2,1)S(1)} %get-tuple-element.23.refs_5_.refs_4_), custom_call_target="tpu_custom_call" | custom-call | flops 4026531840 | bytes 3145728 | tf_op jit(solution)/shard_map/cache_odd/cache_odd/pallas_call | solution.py:491
  29.4 0.5 collective-permute-start.9
  29.9 2.6 %cache_even.1.own_rest = f32[3,136,512]{2,1,0:T(8,128)S(1)} custom-call(s32[1]{0:T(128)} %bitcast.1.rank.refs_0_, s32[2,16]{1,0:T(2,128)S(1)} %bitcast.27, bf16[3,64,1024]{2,1,0:T(8,128)(2,1)S(1)} %collective-permute-done.8.refs_2_, bf16[8,2048,128]{2,1,0:T(8,128)(2,1)S(1)} %get-tuple-element.22.refs_4_.refs_3_, ...), custom_call_target="tpu_custom_call" | custom-call | flops 805306368 | bytes 3145728 | tf_op jit(solution)/shard_map/cache_even/cache_even/pallas_call | solution.py:491
  32.5 0.3 merge_cores.1
  32.8 1.7 %collective-permute-start.11 = (bf16[144,512]{1,0:T(8,128)(2,1)S(1)}, bf16[144,512]{1,0:T(8,128)(2,1)S(1)}, u32[]{:S(2)}, u32[]{:S(2)}) collective-permute-start(bf16[144,512]{1,0:T(8,128)(2,1)S(1)} %get-tuple-element.27), channel_id=1, source_target_pairs={{0,2},{1,3},{2,0},{3,1},{4,6},{5,7},{6,4},{7,5},{8,10},{9,11},{10,... | collective-permute-start | bytes 442376 | tf_op jit(solution)/shard_map/exchange_parts/ppermute | solution.py:184
  34.6 1.1 %collective-permute-start.12 = (bf16[144,512]{1,0:T(8,128)(2,1)S(1)}, bf16[144,512]{1,0:T(8,128)(2,1)S(1)}, u32[]{:S(2)}, u32[]{:S(2)}) collective-permute-start(bf16[144,512]{1,0:T(8,128)(2,1)S(1)} %get-tuple-element.28), channel_id=1, source_target_pairs={{0,4},{1,5},{2,6},{3,7},{4,0},{5,1},{6,2},{7,3},{8,12},{9,13},{10,... | collective-permute-start | bytes 442376 | tf_op jit(solution)/shard_map/exchange_parts/ppermute | solution.py:184
  35.7 1.1 %collective-permute-start.13 = (bf16[144,512]{1,0:T(8,128)(2,1)S(1)}, bf16[144,512]{1,0:T(8,128)(2,1)S(1)}, u32[]{:S(2)}, u32[]{:S(2)}) collective-permute-start(bf16[144,512]{1,0:T(8,128)(2,1)S(1)} %get-tuple-element.29), channel_id=1, source_target_pairs={{0,6},{1,7},{2,4},{3,5},{4,2},{5,3},{6,0},{7,1},{8,14},{9,15},{10,... | collective-permute-start | bytes 442376 | tf_op jit(solution)/shard_map/exchange_parts/ppermute | solution.py:184
  36.8 1.1 %new_tokens.1 = (f32[128,512]{1,0:T(8,128)S(1)}, f32[8,512]{1,0:T(8,128)S(1)}) custom-call(bf16[64,1024]{1,0:T(8,128)(2,1)S(1)} %get-tuple-element.21.refs_2_.refs_0_, bf16[64,8192]{1,0:T(8,128)(2,1)S(1)} %get-tuple-element.30.refs_1_, bf16[8192,128]{1,0:T(8,128)(2,1)S(1)} %bitcast.19, bf16[8192,128]{1,0:T(8,128)(2,1)S(1)} %bitcast.20, ...), custom_call_target="tpu_custom_call" | custom-call | flops 1073741824 | bytes 5242880 | tf_op jit(solution)/shard_map/new_tokens/new_tokens/pallas_call | solution.py:647
  38.0 1.4 %collective-permute-done.11.got_a = bf16[144,512]{1,0:T(8,128)(2,1)S(1)} collective-permute-done((bf16[144,512]{1,0:T(8,128)(2,1)S(1)}, bf16[144,512]{1,0:T(8,128)(2,1)S(1)}, u32[]{:S(2)}, u32[]{:S(2)}) %collective-permute-start.11) | collective-permute-done | bytes 147488 | tf_op jit(solution)/shard_map/exchange_parts/ppermute | solution.py:184
  39.4 4.2 %collective-permute-done.12.got_b = bf16[144,512]{1,0:T(8,128)(2,1)S(1)} collective-permute-done((bf16[144,512]{1,0:T(8,128)(2,1)S(1)}, bf16[144,512]{1,0:T(8,128)(2,1)S(1)}, u32[]{:S(2)}, u32[]{:S(2)}) %collective-permute-start.12) | collective-permute-done | bytes 147488 | tf_op jit(solution)/shard_map/exchange_parts/ppermute | solution.py:184
  43.6 3.2 %project.1 = (f32[32,8192]{1,0:T(8,128)S(1)}, bf16[32,8192]{1,0:T(8,128)(2,1)S(1)}) custom-call(s32[1]{0:T(128)} %bitcast.1.rank.refs_0_, f32[136,512]{1,0:T(8,128)S(1)} %get-tuple-element.26.kept, bf16[144,512]{1,0:T(8,128)(2,1)S(1)} %collective-permute-done.11.got_a, bf16[144,512]{1,0:T(8,128)(2,1)S(1)} %collective-permute-done.12.got_b, ...), custom_call_target="tpu_custom_call" | custom-call | flops 2147483648 | bytes 18874368 | tf_op jit(solution)/shard_map/project/project/pallas_call | solution.py:692
  46.9 1.9 %collective-permute-done.14 = bf16[32,8192]{1,0:T(8,128)(2,1)S(1)} collective-permute-done((bf16[32,8192]{1,0:T(8,128)(2,1)S(1)}, bf16[32,8192]{1,0:T(8,128)(2,1)S(1)}, u32[]{:S(2)}, u32[]{:S(2)}) %collective-permute-start.14) | collective-permute-done | bytes 524320 | tf_op jit(solution)/shard_map/reduce_cores/ppermute | solution.py:184
  49.0 2.0 %collective-permute-start.15 = (bf16[8,8192]{1,0:T(8,128)(2,1)S(1)}, bf16[8,8192]{1,0:T(8,128)(2,1)S(1)}, u32[]{:S(2)}, u32[]{:S(2)}) collective-permute-start(bf16[8,8192]{1,0:T(8,128)(2,1)S(1)} %fusion), channel_id=1, source_target_pairs={{0,8},{1,9},{2,10},{3,11},{4,12},{5,13},{6,14},{7,15},{8,16},{9,17... | collective-permute-start | bytes 393224 | tf_op jit(solution)/shard_map/reduce_on_next_section/ppermute | solution.py:192
  51.1 2.5 %collective-permute-start.16 = (bf16[8,8192]{1,0:T(8,128)(2,1)S(1)}, bf16[8,8192]{1,0:T(8,128)(2,1)S(1)}, u32[]{:S(2)}, u32[]{:S(2)}) collective-permute-start(bf16[8,8192]{1,0:T(8,128)(2,1)S(1)} %get-tuple-element.37), channel_id=1, source_target_pairs={{0,10},{1,11},{2,8},{3,9},{4,14},{5,15},{6,12},{7,13},{8,18},{9,19... | collective-permute-start | bytes 393224 | tf_op jit(solution)/shard_map/reduce_on_next_section/ppermute | solution.py:192
  53.6 1.7 %collective-permute-start.18 = (bf16[8,8192]{1,0:T(8,128)(2,1)S(1)}, bf16[8,8192]{1,0:T(8,128)(2,1)S(1)}, u32[]{:S(2)}, u32[]{:S(2)}) collective-permute-start(bf16[8,8192]{1,0:T(8,128)(2,1)S(1)} %get-tuple-element.38), channel_id=1, source_target_pairs={{0,14},{1,15},{2,12},{3,13},{4,10},{5,11},{6,8},{7,9},{8,22},{9,23... | collective-permute-start | bytes 393224 | tf_op jit(solution)/shard_map/reduce_on_next_section/ppermute | solution.py:192
  55.3 1.1 %collective-permute-start.17 = (bf16[8,8192]{1,0:T(8,128)(2,1)S(1)}, bf16[8,8192]{1,0:T(8,128)(2,1)S(1)}, u32[]{:S(2)}, u32[]{:S(2)}) collective-permute-start(bf16[8,8192]{1,0:T(8,128)(2,1)S(1)} %get-tuple-element.39), channel_id=1, source_target_pairs={{0,12},{1,13},{2,14},{3,15},{4,8},{5,9},{6,10},{7,11},{8,20},{9,21... | collective-permute-start | bytes 393224 | tf_op jit(solution)/shard_map/reduce_on_next_section/ppermute | solution.py:192
  56.5 1.3 %collective-permute-done.15 = bf16[8,8192]{1,0:T(8,128)(2,1)S(1)} collective-permute-done((bf16[8,8192]{1,0:T(8,128)(2,1)S(1)}, bf16[8,8192]{1,0:T(8,128)(2,1)S(1)}, u32[]{:S(2)}, u32[]{:S(2)}) %collective-permute-start.15) | collective-permute-done | bytes 131104 | tf_op jit(solution)/shard_map/reduce_on_next_section/ppermute | solution.py:192
  57.8 2.6 %collective-permute-done.16 = bf16[8,8192]{1,0:T(8,128)(2,1)S(1)} collective-permute-done((bf16[8,8192]{1,0:T(8,128)(2,1)S(1)}, bf16[8,8192]{1,0:T(8,128)(2,1)S(1)}, u32[]{:S(2)}, u32[]{:S(2)}) %collective-permute-start.16) | collective-permute-done | bytes 131104 | tf_op jit(solution)/shard_map/reduce_on_next_section/ppermute | solution.py:192
  60.4 4.6 %collective-permute-done.18 = bf16[8,8192]{1,0:T(8,128)(2,1)S(1)} collective-permute-done((bf16[8,8192]{1,0:T(8,128)(2,1)S(1)}, bf16[8,8192]{1,0:T(8,128)(2,1)S(1)}, u32[]{:S(2)}, u32[]{:S(2)}) %collective-permute-start.18) | collective-permute-done | bytes 131104 | tf_op jit(solution)/shard_map/reduce_on_next_section/ppermute | solution.py:192
  64.9 1.6 %collective-permute-done.17 = bf16[8,8192]{1,0:T(8,128)(2,1)S(1)} collective-permute-done((bf16[8,8192]{1,0:T(8,128)(2,1)S(1)}, bf16[8,8192]{1,0:T(8,128)(2,1)S(1)}, u32[]{:S(2)}, u32[]{:S(2)}) %collective-permute-start.17) | collective-permute-done | bytes 131104 | tf_op jit(solution)/shard_map/reduce_on_next_section/ppermute | solution.py:192
  66.5 0.7 %fusion.1 = bf16[1,8,8192]{2,1,0:T(8,128)(2,1)} fusion(bf16[8,8192]{1,0:T(8,128)(2,1)S(1)} %collective-permute-done.18, bf16[8,8192]{1,0:T(8,128)(2,1)S(1)} %collective-permute-done.17, bf16[8,8192]{1,0:T(8,128)(2,1)S(1)} %collective-permute-done.16, bf16[8,8192]{1,0:T(8,128)(2,1)S(1)} %collective-permute-done.15), kind=kLoop, calls=%fused_computation.4 | loop fusion | flops 524288 | bytes 655360 | tf_op jit(solution)/shard_map/broadcast_in_dim | solution.py:717
  (52 shorter events, 1.2 us)
Async XLA Ops:
  0.0 10.7 %collective-permute-start.2 = (bf16[8,8192]{1,0:T(8,128)(2,1)}, bf16[8,8192]{1,0:T(8,128)(2,1)S(1)}, u32[]{:S(2)}, u32[]{:S(2)}) collective-permute-start(bf16[8,8192]{1,0:T(8,128)(2,1)} %bitcast.21), channel_id=1, source_target_pairs={{0,6},{1,7},{2,4},{3,5},{4,2},{5,3},{6,0},{7,1},{8,14},{9,15},{10,... | collective-permute-start | bytes 393224 | tf_op jit(solution)/shard_map/gather_tokens/ppermute | solution.py:184
  3.9 6.9 %collective-permute-start.1 = (bf16[8,8192]{1,0:T(8,128)(2,1)}, bf16[8,8192]{1,0:T(8,128)(2,1)S(1)}, u32[]{:S(2)}, u32[]{:S(2)}) collective-permute-start(bf16[8,8192]{1,0:T(8,128)(2,1)} %bitcast.22), channel_id=1, source_target_pairs={{0,4},{1,5},{2,6},{3,7},{4,0},{5,1},{6,2},{7,3},{8,12},{9,13},{10,... | collective-permute-start | bytes 393224 | tf_op jit(solution)/shard_map/gather_tokens/ppermute | solution.py:184
  4.4 6.4 %collective-permute-start = (bf16[8,8192]{1,0:T(8,128)(2,1)}, bf16[8,8192]{1,0:T(8,128)(2,1)S(1)}, u32[]{:S(2)}, u32[]{:S(2)}) collective-permute-start(bf16[8,8192]{1,0:T(8,128)(2,1)} %bitcast.23), channel_id=1, source_target_pairs={{0,2},{1,3},{2,0},{3,1},{4,6},{5,7},{6,4},{7,5},{8,10},{9,11},{10,... | collective-permute-start | bytes 393224 | tf_op jit(solution)/shard_map/gather_tokens/ppermute | solution.py:184
  4.5 8.3 %slice-start = ((s8[16777216]{0:T(1024)(128)(4,1)}), s8[4194304]{0:T(1024)(128)(4,1)S(1)}, s32[]{:S(2)}) async-start(s8[16777216]{0:T(1024)(128)(4,1)} %bitcast.13), calls=%async_computation | async-start | bytes 8388608
  4.5 6.3 %copy-start.2 = (bf16[1,8,8192]{2,1,0:T(8,128)(2,1)S(1)}, bf16[1,8,8192]{2,1,0:T(8,128)(2,1)}, u32[]{:S(2)}) copy-start(bf16[1,8,8192]{2,1,0:T(8,128)(2,1)} %param.10) | copy-start | bytes 393220
  4.5 8.3 %slice-start.1 = ((s8[16777216]{0:T(1024)(128)(4,1)}), s8[4194304]{0:T(1024)(128)(4,1)S(1)}, s32[]{:S(2)}) async-start(s8[16777216]{0:T(1024)(128)(4,1)} %bitcast.13), calls=%async_computation.1 | async-start | bytes 8388608
  4.5 8.3 %slice-start.2 = ((s8[16777216]{0:T(1024)(128)(4,1)}), s8[4194304]{0:T(1024)(128)(4,1)S(1)}, s32[]{:S(2)}) async-start(s8[16777216]{0:T(1024)(128)(4,1)} %bitcast.13), calls=%async_computation.2 | async-start | bytes 8388608
  4.5 8.4 %slice-start.3 = ((s8[16777216]{0:T(1024)(128)(4,1)}), s8[4194304]{0:T(1024)(128)(4,1)S(1)}, s32[]{:S(2)}) async-start(s8[16777216]{0:T(1024)(128)(4,1)} %bitcast.13), calls=%async_computation.3 | async-start | bytes 8388608
  4.5 8.4 %copy-start.3 = (bf16[1,8192]{1,0:T(2,128)(2,1)S(1)}, bf16[1,8192]{1,0:T(2,128)(2,1)}, u32[]{:S(2)}) copy-start(bf16[1,8192]{1,0:T(2,128)(2,1)} %refs_2_.1) | copy-start | bytes 49156
  10.8 2.0 %collective-permute-start.3 = (bf16[4,8,8192]{2,1,0:T(8,128)(2,1)S(1)}, bf16[4,8,8192]{2,1,0:T(8,128)(2,1)S(1)}, u32[]{:S(2)}, u32[]{:S(2)}) collective-permute-start(bf16[4,8,8192]{2,1,0:T(8,128)(2,1)S(1)} %join_tokens.1.refs_0_), channel_id=1, source_target_pairs={{0,1},{1,0},{2,3},{3,2},{4,5},{5,4},{6,7},{7,6},{8,9},{9,8},{10,11... | collective-permute-start | bytes 1572872 | tf_op jit(solution)/shard_map/gather_tokens/ppermute | solution.py:184
  12.9 7.0 %copy-start.4 = (s32[1,2,16]{2,1,0:T(2,128)S(1)}, s32[1,2,16]{2,1,0:T(2,128)}, u32[]{:S(2)}) copy-start(s32[1,2,16]{2,1,0:T(2,128)} %param.18) | copy-start | bytes 388
  16.4 3.4 %collective-permute-start.4 = (bf16[64,1024]{1,0:T(8,128)(2,1)S(1)}, bf16[64,1024]{1,0:T(8,128)(2,1)S(1)}, u32[]{:S(2)}, u32[]{:S(2)}) collective-permute-start(bf16[64,1024]{1,0:T(8,128)(2,1)S(1)} %get-tuple-element.21.refs_2_.refs_0_), channel_id=1, source_target_pairs={{0,1},{1,0},{2,3},{3,2},{4,5},{5,4},{6,7},{7,6},{8,9},{9,8},{10,11... | collective-permute-start | bytes 393224 | tf_op jit(solution)/shard_map/gather_queries/ppermute | solution.py:184
  16.6 6.8 %collective-permute-start.7 = (bf16[64,1024]{1,0:T(8,128)(2,1)S(1)}, bf16[64,1024]{1,0:T(8,128)(2,1)S(1)}, u32[]{:S(2)}, u32[]{:S(2)}) collective-permute-start(bf16[64,1024]{1,0:T(8,128)(2,1)S(1)} %get-tuple-element.21.refs_2_.refs_0_), channel_id=1, source_target_pairs={{0,7},{1,6},{2,5},{3,4},{4,3},{5,2},{6,1},{7,0},{8,15},{9,14},{10,... | collective-permute-start | bytes 393224 | tf_op jit(solution)/shard_map/gather_queries/ppermute | solution.py:184
  19.5 6.8 %collective-permute-start.6 = (bf16[64,1024]{1,0:T(8,128)(2,1)S(1)}, bf16[64,1024]{1,0:T(8,128)(2,1)S(1)}, u32[]{:S(2)}, u32[]{:S(2)}) collective-permute-start(bf16[64,1024]{1,0:T(8,128)(2,1)S(1)} %get-tuple-element.21.refs_2_.refs_0_), channel_id=1, source_target_pairs={{0,5},{1,4},{2,7},{3,6},{4,1},{5,0},{6,3},{7,2},{8,13},{9,12},{10,... | collective-permute-start | bytes 393224 | tf_op jit(solution)/shard_map/gather_queries/ppermute | solution.py:184
  19.8 6.6 %collective-permute-start.5 = (bf16[64,1024]{1,0:T(8,128)(2,1)S(1)}, bf16[64,1024]{1,0:T(8,128)(2,1)S(1)}, u32[]{:S(2)}, u32[]{:S(2)}) collective-permute-start(bf16[64,1024]{1,0:T(8,128)(2,1)S(1)} %get-tuple-element.21.refs_2_.refs_0_), channel_id=1, source_target_pairs={{0,3},{1,2},{2,1},{3,0},{4,7},{5,6},{6,5},{7,4},{8,11},{9,10},{10,... | collective-permute-start | bytes 393224 | tf_op jit(solution)/shard_map/gather_queries/ppermute | solution.py:184
  26.4 3.5 %collective-permute-start.8 = (bf16[3,64,1024]{2,1,0:T(8,128)(2,1)S(1)}, bf16[3,64,1024]{2,1,0:T(8,128)(2,1)S(1)}, u32[]{:S(2)}, u32[]{:S(2)}) collective-permute-start(bf16[3,64,1024]{2,1,0:T(8,128)(2,1)S(1)} %join_queries.1.refs_2_), channel_id=1, source_target_pairs={{0,1},{1,0},{2,3},{3,2},{4,5},{5,4},{6,7},{7,6},{8,9},{9,8},{10,11... | collective-permute-start | bytes 1179656 | tf_op jit(solution)/shard_map/gather_queries/ppermute | solution.py:184
  26.6 10.2 %copy-start.1 = (bf16[1,8192,128]{2,1,0:T(8,128)(2,1)S(1)}, bf16[1,8192,128]{2,1,0:T(8,128)(2,1)}, u32[]{:S(2)}) copy-start(bf16[1,8192,128]{2,1,0:T(8,128)(2,1)} %param.14) | copy-start | bytes 6291460
  26.6 16.9 %slice-start.4 = ((s8[16777216]{0:T(1024)(128)(4,1)}), s8[4194304]{0:T(1024)(128)(4,1)S(1)}, s32[]{:S(2)}) async-start(s8[16777216]{0:T(1024)(128)(4,1)} %bitcast.16), calls=%async_computation.4 | async-start | bytes 8388608
  26.6 16.9 %slice-start.5 = ((s8[16777216]{0:T(1024)(128)(4,1)}), s8[4194304]{0:T(1024)(128)(4,1)S(1)}, s32[]{:S(2)}) async-start(s8[16777216]{0:T(1024)(128)(4,1)} %bitcast.16), calls=%async_computation.5 | async-start | bytes 8388608
  29.3 3.2 %collective-permute-start.10 = (bf16[3,144,512]{2,1,0:T(8,128)(2,1)S(1)}, bf16[3,144,512]{2,1,0:T(8,128)(2,1)S(1)}, u32[]{:S(2)}, u32[]{:S(2)}) collective-permute-start(bf16[3,144,512]{2,1,0:T(8,128)(2,1)S(1)} %cache_odd.1), channel_id=1, source_target_pairs={{0,1},{1,0},{2,3},{3,2},{4,5},{5,4},{6,7},{7,6},{8,9},{9,8},{10,11... | collective-permute-start | bytes 1327112 | tf_op jit(solution)/shard_map/cache_odd/ppermute | solution.py:184
  29.4 7.5 %copy-start = (bf16[1,8192,128]{2,1,0:T(8,128)(2,1)S(1)}, bf16[1,8192,128]{2,1,0:T(8,128)(2,1)}, u32[]{:S(2)}) copy-start(bf16[1,8192,128]{2,1,0:T(8,128)(2,1)} %param.13) | copy-start | bytes 6291460
  29.4 14.2 %slice-start.6 = ((s8[16777216]{0:T(1024)(128)(4,1)}), s8[4194304]{0:T(1024)(128)(4,1)S(1)}, s32[]{:S(2)}) async-start(s8[16777216]{0:T(1024)(128)(4,1)} %bitcast.16), calls=%async_computation.6 | async-start | bytes 8388608
  29.4 14.2 %slice-start.7 = ((s8[16777216]{0:T(1024)(128)(4,1)}), s8[4194304]{0:T(1024)(128)(4,1)S(1)}, s32[]{:S(2)}) async-start(s8[16777216]{0:T(1024)(128)(4,1)} %bitcast.16), calls=%async_computation.7 | async-start | bytes 8388608
  29.4 3.1 %collective-permute-start.9 = (bf16[1,144,512]{2,1,0:T(8,128)(2,1)S(1)}, bf16[1,144,512]{2,1,0:T(8,128)(2,1)S(1)}, u32[]{:S(2)}, u32[]{:S(2)}) collective-permute-start(bf16[1,144,512]{2,1,0:T(8,128)(2,1)S(1)} %get-tuple-element.25), channel_id=1, source_target_pairs={{0,1},{1,0},{2,3},{3,2},{4,5},{5,4},{6,7},{7,6},{8,9},{9,8},{10,11... | collective-permute-start | bytes 442376 | tf_op jit(solution)/shard_map/cache_near/ppermute | solution.py:184
  32.8 6.6 %collective-permute-start.11 = (bf16[144,512]{1,0:T(8,128)(2,1)S(1)}, bf16[144,512]{1,0:T(8,128)(2,1)S(1)}, u32[]{:S(2)}, u32[]{:S(2)}) collective-permute-start(bf16[144,512]{1,0:T(8,128)(2,1)S(1)} %get-tuple-element.27), channel_id=1, source_target_pairs={{0,2},{1,3},{2,0},{3,1},{4,6},{5,7},{6,4},{7,5},{8,10},{9,11},{10,... | collective-permute-start | bytes 442376 | tf_op jit(solution)/shard_map/exchange_parts/ppermute | solution.py:184
  34.6 9.0 %collective-permute-start.12 = (bf16[144,512]{1,0:T(8,128)(2,1)S(1)}, bf16[144,512]{1,0:T(8,128)(2,1)S(1)}, u32[]{:S(2)}, u32[]{:S(2)}) collective-permute-start(bf16[144,512]{1,0:T(8,128)(2,1)S(1)} %get-tuple-element.28), channel_id=1, source_target_pairs={{0,4},{1,5},{2,6},{3,7},{4,0},{5,1},{6,2},{7,3},{8,12},{9,13},{10,... | collective-permute-start | bytes 442376 | tf_op jit(solution)/shard_map/exchange_parts/ppermute | solution.py:184
  35.7 7.9 %collective-permute-start.13 = (bf16[144,512]{1,0:T(8,128)(2,1)S(1)}, bf16[144,512]{1,0:T(8,128)(2,1)S(1)}, u32[]{:S(2)}, u32[]{:S(2)}) collective-permute-start(bf16[144,512]{1,0:T(8,128)(2,1)S(1)} %get-tuple-element.29), channel_id=1, source_target_pairs={{0,6},{1,7},{2,4},{3,5},{4,2},{5,3},{6,0},{7,1},{8,14},{9,15},{10,... | collective-permute-start | bytes 442376 | tf_op jit(solution)/shard_map/exchange_parts/ppermute | solution.py:184
  46.8 2.0 %collective-permute-start.14 = (bf16[32,8192]{1,0:T(8,128)(2,1)S(1)}, bf16[32,8192]{1,0:T(8,128)(2,1)S(1)}, u32[]{:S(2)}, u32[]{:S(2)}) collective-permute-start(bf16[32,8192]{1,0:T(8,128)(2,1)S(1)} %get-tuple-element.34), channel_id=1, source_target_pairs={{0,1},{1,0},{2,3},{3,2},{4,5},{5,4},{6,7},{7,6},{8,9},{9,8},{10,11... | collective-permute-start | bytes 1572872 | tf_op jit(solution)/shard_map/reduce_cores/ppermute | solution.py:184
  49.0 8.7 %collective-permute-start.15 = (bf16[8,8192]{1,0:T(8,128)(2,1)S(1)}, bf16[8,8192]{1,0:T(8,128)(2,1)S(1)}, u32[]{:S(2)}, u32[]{:S(2)}) collective-permute-start(bf16[8,8192]{1,0:T(8,128)(2,1)S(1)} %fusion), channel_id=1, source_target_pairs={{0,8},{1,9},{2,10},{3,11},{4,12},{5,13},{6,14},{7,15},{8,16},{9,17... | collective-permute-start | bytes 393224 | tf_op jit(solution)/shard_map/reduce_on_next_section/ppermute | solution.py:192
  51.1 9.3 %collective-permute-start.16 = (bf16[8,8192]{1,0:T(8,128)(2,1)S(1)}, bf16[8,8192]{1,0:T(8,128)(2,1)S(1)}, u32[]{:S(2)}, u32[]{:S(2)}) collective-permute-start(bf16[8,8192]{1,0:T(8,128)(2,1)S(1)} %get-tuple-element.37), channel_id=1, source_target_pairs={{0,10},{1,11},{2,8},{3,9},{4,14},{5,15},{6,12},{7,13},{8,18},{9,19... | collective-permute-start | bytes 393224 | tf_op jit(solution)/shard_map/reduce_on_next_section/ppermute | solution.py:192
  53.6 11.3 %collective-permute-start.18 = (bf16[8,8192]{1,0:T(8,128)(2,1)S(1)}, bf16[8,8192]{1,0:T(8,128)(2,1)S(1)}, u32[]{:S(2)}, u32[]{:S(2)}) collective-permute-start(bf16[8,8192]{1,0:T(8,128)(2,1)S(1)} %get-tuple-element.38), channel_id=1, source_target_pairs={{0,14},{1,15},{2,12},{3,13},{4,10},{5,11},{6,8},{7,9},{8,22},{9,23... | collective-permute-start | bytes 393224 | tf_op jit(solution)/shard_map/reduce_on_next_section/ppermute | solution.py:192
  55.3 11.2 %collective-permute-start.17 = (bf16[8,8192]{1,0:T(8,128)(2,1)S(1)}, bf16[8,8192]{1,0:T(8,128)(2,1)S(1)}, u32[]{:S(2)}, u32[]{:S(2)}) collective-permute-start(bf16[8,8192]{1,0:T(8,128)(2,1)S(1)} %get-tuple-element.39), channel_id=1, source_target_pairs={{0,12},{1,13},{2,14},{3,15},{4,8},{5,9},{6,10},{7,11},{8,20},{9,21... | collective-permute-start | bytes 393224 | tf_op jit(solution)/shard_map/reduce_on_next_section/ppermute | solution.py:192

commit v5 on v4

--- a/solution.py
+++ b/solution.py
@@ -576,6 +576,20 @@
         sent[:, c : c + step] = product[half:].astype(jnp.bfloat16)
 
 
+def pair_kernel(own, got, resid, *outs):
+    count = resid.shape[0]
+    for i, out in enumerate(outs):
+        rows = slice(i * count, (i + 1) * count)
+        block = own[rows] + got[...].astype(jnp.float32)[rows]
+        if i == 0:
+            block = resid[...].astype(jnp.float32) + block
+        out[...] = block.astype(out.dtype)
+
+
+def add_kernel(block, across, out):
+    out[...] = (block[...] + across[...].astype(jnp.float32)).astype(out.dtype)
+
+
 def on_device_owned(
     tokens,
     norm_gain,
@@ -705,14 +719,17 @@
             ],
         )(rank, kept, *parts, summed, stats, held(w_out[0]))
     with jax.named_scope("reduce_cores"):
-        pair = own + swapped(other, 1).astype(jnp.float32)
+        row = jax.ShapeDtypeStruct((count, width), jnp.bfloat16)
+        row_f32 = jax.ShapeDtypeStruct((count, width), jnp.float32)
+        at_own, at_x, at_y, to_x = call(
+            pair_kernel, "reduce_cores", [row, row, row_f32, row], [IN_VMEM] * 3, nbytes=2 * MIB
+        )(own, swapped(other, 1), tokens[0])
     with jax.named_scope("reduce_on_next_section"):
-        total = 0.0
-        for i, bits in enumerate(EVEN):
-            block = pair[i * count : (i + 1) * count]
-            if bits == 0:
-                block = tokens[0].astype(jnp.float32) + block
-            total = total + onward(block.astype(jnp.bfloat16), bits).astype(jnp.float32)
+        across = swapped(to_x, EVEN[1])
+        from_own, from_x = onward(at_own, EVEN[0]), onward(at_x, EVEN[1])
+        at_y = call(add_kernel, "add_across", row, [IN_VMEM] * 2)(at_y, across)
+        total = from_own.astype(jnp.float32) + from_x.astype(jnp.float32)
+        total = total + onward(at_y, EVEN[2]).astype(jnp.float32)
         handed = total.astype(jnp.bfloat16)
     return handed[None]
 

time: 67.3 us -> 65.5 us (0.973)
  starting transfers between devices: 20.3 us -> 17.6 us
  Pallas kernels: 20.6 us -> 23.1 us
  waiting for transfers between devices: 23.3 us -> 22.1 us
    ppermute x4 -> x3, starting transfers between devices: 7.44 us -> 3.8 us  [onward(): return lax.ppermute(block, ('section', 'seq'), route)]
    pallas_call x3, Pallas kernels: 7.56 us -> 9.84 us  [cache_part(): call(lambda *refs: cache_kernel(scale, order, *refs), name, outs, [IN_SME...]
    ppermute x4 -> x3, waiting for transfers between devices: 10 us -> 7.75 us  [onward(): return lax.ppermute(block, ('section', 'seq'), route)]
    ppermute x15 -> x16, waiting for transfers between devices: 13.3 us -> 14.4 us  [swapped(): return lax.ppermute(block, 'seq', [(i, i ^ bits) for i in range(n)])]
    ppermute x15 -> x16, starting transfers between devices: 12.8 us -> 13.8 us  [swapped(): return lax.ppermute(block, 'seq', [(i, i ^ bits) for i in range(n)])]
  transfers between devices with their start and end apart: 19 -> 19, of which waited for: 10 -> 11; matrix products, arithmetic and copies ran while one was open for 0% -> 0% of each run, Pallas kernels for 20% -> 24%
where the time goes in v5:
time: 65.5 us; the launch traced here: 65.6 us
  Pallas kernels  23.1 us (35%)
  waiting for transfers between devices  22.1 us (34%)
  starting transfers between devices  17.6 us (27%)
  between operations  1.69 us (3%)
  other arithmetic  1 us (2%)
    ppermute x16, waiting for transfers between devices, swapped(): return lax.ppermute(block, 'seq', [(i, i ^ bits) for i in range(n)])  14.4 us
    ppermute x16, starting transfers between devices, swapped(): return lax.ppermute(block, 'seq', [(i, i ^ bits) for i in range(n)])  13.8 us
    pallas_call x3, Pallas kernels, cache_part(): call(lambda *refs: cache_kernel(scale, order, *refs), name, outs, [IN_SME...  9.84 us
    ppermute x3, waiting for transfers between devices, onward(): return lax.ppermute(block, ('section', 'seq'), route)  7.75 us
    pallas_call x1, Pallas kernels, cache_by_head(): call(by_head_kernel, 'cache_by_head', [jax.ShapeDtypeStruct((heads, ctx,...  4.79 us
    ppermute x3, starting transfers between devices, onward(): return lax.ppermute(block, ('section', 'seq'), route)  3.8 us
    pallas_call x1, Pallas kernels, on_device_owned(): call(query_kernel, 'queries', [jax.ShapeDtypeStruct((tok, own_cols), jnp....  3.57 us
    pallas_call x1, Pallas kernels, on_device_owned(): call(output_kernel, 'project', [jax.ShapeDtypeStruct((tok // 2, width), j...  3.25 us
  transfers between devices with their start and end apart: 19, of which 11 were waited for; matrix products, arithmetic and copies ran while one was open for 0% of the time, Pallas kernels for 24%

profile of v5, /device:TPU:0, one launch (start us, length us, event | category | flops | bytes accessed | tf_op | source)
XLA Modules:
  0.0 65.6 jit_solution(3427014332212251603)
XLA Ops:
  0.0 3.9 %collective-permute-start.2 = (bf16[8,8192]{1,0:T(8,128)(2,1)}, bf16[8,8192]{1,0:T(8,128)(2,1)S(1)}, u32[]{:S(2)}, u32[]{:S(2)}) collective-permute-start(bf16[8,8192]{1,0:T(8,128)(2,1)} %bitcast.20), channel_id=1, source_target_pairs={{0,6},{1,7},{2,4},{3,5},{4,2},{5,3},{6,0},{7,1},{8,14},{9,15},{10,... | collective-permute-start | bytes 393224 | tf_op jit(solution)/shard_map/gather_tokens/ppermute | solution.py:184
  3.9 0.5 collective-permute-start.1
  4.5 4.8 %cache_by_head.1 = (bf16[8,2048,128]{2,1,0:T(8,128)(2,1)S(1)}, bf16[8,128,2048]{2,1,0:T(8,128)(2,1)S(1)}, f32[8,128]{1,0:T(8,128)S(1)}) custom-call(s32[1]{0:T(128)} %bitcast.rank.refs_0_, bf16[2048,8,128]{2,1,0:T(8,128)(2,1)} %bitcast.28, bf16[2048,8,128]{2,1,0:T(8,128)(2,1)} %bitcast.29), custom_call_target="tpu_custom_call" | custom-call | flops 10000000000 | bytes 4194304 | tf_op jit(solution)/shard_map/cache_layout/cache_by_head/pallas_call | solution.py:308
  11.2 1.6 %collective-permute-done.3.refs_1_ = bf16[4,8,8192]{2,1,0:T(8,128)(2,1)S(1)} collective-permute-done((bf16[4,8,8192]{2,1,0:T(8,128)(2,1)S(1)}, bf16[4,8,8192]{2,1,0:T(8,128)(2,1)S(1)}, u32[]{:S(2)}, u32[]{:S(2)}) %collective-permute-start.3) | collective-permute-done | bytes 524320 | tf_op jit(solution)/shard_map/gather_tokens/ppermute | solution.py:184
  12.9 3.6 %queries.1 = (bf16[64,1024]{1,0:T(8,128)(2,1)S(1)}, bf16[64,8192]{1,0:T(8,128)(2,1)S(1)}) custom-call(s32[1]{0:T(128)} %bitcast.rank.refs_0_, bf16[4,8,8192]{2,1,0:T(8,128)(2,1)S(1)} %join_tokens.1.refs_0_, bf16[4,8,8192]{2,1,0:T(8,128)(2,1)S(1)} %collective-permute-done.3.refs_1_, bf16[1,8192]{1,0:T(2,128)(2,1)S(1)} %copy-done.3, ...), custom_call_target="tpu_custom_call" | custom-call | flops 2147483648 | bytes 16777216 | tf_op jit(solution)/shard_map/queries/queries/pallas_call | solution.py:635
  16.6 2.9 %collective-permute-start.7 = (bf16[64,1024]{1,0:T(8,128)(2,1)S(1)}, bf16[64,1024]{1,0:T(8,128)(2,1)S(1)}, u32[]{:S(2)}, u32[]{:S(2)}) collective-permute-start(bf16[64,1024]{1,0:T(8,128)(2,1)S(1)} %get-tuple-element.25.refs_2_.refs_0_), channel_id=1, source_target_pairs={{0,7},{1,6},{2,5},{3,4},{4,3},{5,2},{6,1},{7,0},{8,15},{9,14},{10,... | collective-permute-start | bytes 393224 | tf_op jit(solution)/shard_map/gather_queries/ppermute | solution.py:184
  19.5 0.3 collective-permute-start.6
  19.9 3.0 %cache_near.1 = (f32[1,136,512]{2,1,0:T(8,128)S(1)}, bf16[1,144,512]{2,1,0:T(8,128)(2,1)S(1)}) custom-call(s32[1]{0:T(128)} %bitcast.rank.refs_0_, s32[2,16]{1,0:T(2,128)S(1)} %bitcast.25, bf16[64,1024]{1,0:T(8,128)(2,1)S(1)} %get-tuple-element.25.refs_2_.refs_0_, bf16[64,1024]{1,0:T(8,128)(2,1)S(1)} %collective-permute-done.4.refs_3_, ...), custom_call_target="tpu_custom_call" | custom-call | flops 536870912 | bytes 2097152 | tf_op jit(solution)/shard_map/cache_near/cache_near/pallas_call | solution.py:491
  22.8 0.6 collective-permute-done.7.refs_2_
  23.4 3.0 %collective-permute-done.6.refs_1_ = bf16[64,1024]{1,0:T(8,128)(2,1)S(1)} collective-permute-done((bf16[64,1024]{1,0:T(8,128)(2,1)S(1)}, bf16[64,1024]{1,0:T(8,128)(2,1)S(1)}, u32[]{:S(2)}, u32[]{:S(2)}) %collective-permute-start.6) | collective-permute-done | bytes 131104 | tf_op jit(solution)/shard_map/gather_queries/ppermute | solution.py:184
  26.4 0.2 collective-permute-start.8
  26.7 3.5 %cache_odd.1 = bf16[3,144,512]{2,1,0:T(8,128)(2,1)S(1)} custom-call(s32[1]{0:T(128)} %bitcast.rank.refs_0_, s32[2,16]{1,0:T(2,128)S(1)} %bitcast.26, bf16[3,64,1024]{2,1,0:T(8,128)(2,1)S(1)} %join_queries.1.refs_2_, bf16[8,2048,128]{2,1,0:T(8,128)(2,1)S(1)} %get-tuple-element.26.refs_4_.refs_3_, bf16[8,128,2048]{2,1,0:T(8,128)(2,1)S(1)} %get-tuple-element.27.refs_5_.refs_4_), custom_call_target="tpu_custom_call" | custom-call | flops 4026531840 | bytes 3145728 | tf_op jit(solution)/shard_map/cache_odd/cache_odd/pallas_call | solution.py:491
  30.2 0.5 collective-permute-start.9
  30.7 3.4 %cache_even.1.own_rest = f32[3,136,512]{2,1,0:T(8,128)S(1)} custom-call(s32[1]{0:T(128)} %bitcast.rank.refs_0_, s32[2,16]{1,0:T(2,128)S(1)} %bitcast.27, bf16[3,64,1024]{2,1,0:T(8,128)(2,1)S(1)} %collective-permute-done.8.refs_2_, bf16[8,2048,128]{2,1,0:T(8,128)(2,1)S(1)} %get-tuple-element.26.refs_4_.refs_3_, ...), custom_call_target="tpu_custom_call" | custom-call | flops 805306368 | bytes 3145728 | tf_op jit(solution)/shard_map/cache_even/cache_even/pallas_call | solution.py:491
  34.2 0.3 merge_cores.1
  34.4 0.9 %collective-permute-start.11 = (bf16[144,512]{1,0:T(8,128)(2,1)S(1)}, bf16[144,512]{1,0:T(8,128)(2,1)S(1)}, u32[]{:S(2)}, u32[]{:S(2)}) collective-permute-start(bf16[144,512]{1,0:T(8,128)(2,1)S(1)} %get-tuple-element.31), channel_id=1, source_target_pairs={{0,2},{1,3},{2,0},{3,1},{4,6},{5,7},{6,4},{7,5},{8,10},{9,11},{10,... | collective-permute-start | bytes 442376 | tf_op jit(solution)/shard_map/exchange_parts/ppermute | solution.py:184
  35.3 0.5 collective-permute-start.12
  35.8 2.2 %collective-permute-start.13 = (bf16[144,512]{1,0:T(8,128)(2,1)S(1)}, bf16[144,512]{1,0:T(8,128)(2,1)S(1)}, u32[]{:S(2)}, u32[]{:S(2)}) collective-permute-start(bf16[144,512]{1,0:T(8,128)(2,1)S(1)} %get-tuple-element.33), channel_id=1, source_target_pairs={{0,6},{1,7},{2,4},{3,5},{4,2},{5,3},{6,0},{7,1},{8,14},{9,15},{10,... | collective-permute-start | bytes 442376 | tf_op jit(solution)/shard_map/exchange_parts/ppermute | solution.py:184
  38.0 1.1 %new_tokens.1 = (f32[128,512]{1,0:T(8,128)S(1)}, f32[8,512]{1,0:T(8,128)S(1)}) custom-call(bf16[64,1024]{1,0:T(8,128)(2,1)S(1)} %get-tuple-element.25.refs_2_.refs_0_, bf16[64,8192]{1,0:T(8,128)(2,1)S(1)} %get-tuple-element.34.refs_1_, bf16[8192,128]{1,0:T(8,128)(2,1)S(1)} %bitcast.18, bf16[8192,128]{1,0:T(8,128)(2,1)S(1)} %bitcast.19, ...), custom_call_target="tpu_custom_call" | custom-call | flops 1073741824 | bytes 5242880 | tf_op jit(solution)/shard_map/new_tokens/new_tokens/pallas_call | solution.py:661
  39.1 2.0 %collective-permute-done.11.got_a = bf16[144,512]{1,0:T(8,128)(2,1)S(1)} collective-permute-done((bf16[144,512]{1,0:T(8,128)(2,1)S(1)}, bf16[144,512]{1,0:T(8,128)(2,1)S(1)}, u32[]{:S(2)}, u32[]{:S(2)}) %collective-permute-start.11) | collective-permute-done | bytes 147488 | tf_op jit(solution)/shard_map/exchange_parts/ppermute | solution.py:184
  41.1 0.2 collective-permute-done.12.got_b
  41.3 3.6 %collective-permute-done.13.got_c = bf16[144,512]{1,0:T(8,128)(2,1)S(1)} collective-permute-done((bf16[144,512]{1,0:T(8,128)(2,1)S(1)}, bf16[144,512]{1,0:T(8,128)(2,1)S(1)}, u32[]{:S(2)}, u32[]{:S(2)}) %collective-permute-start.13) | collective-permute-done | bytes 147488 | tf_op jit(solution)/shard_map/exchange_parts/ppermute | solution.py:184
  45.0 3.2 %project.1 = (f32[32,8192]{1,0:T(8,128)S(1)}, bf16[32,8192]{1,0:T(8,128)(2,1)S(1)}) custom-call(s32[1]{0:T(128)} %bitcast.rank.refs_0_, f32[136,512]{1,0:T(8,128)S(1)} %get-tuple-element.30.kept, bf16[144,512]{1,0:T(8,128)(2,1)S(1)} %collective-permute-done.11.got_a, bf16[144,512]{1,0:T(8,128)(2,1)S(1)} %collective-permute-done.12.got_b, ...), custom_call_target="tpu_custom_call" | custom-call | flops 2147483648 | bytes 18874368 | tf_op jit(solution)/shard_map/project/project/pallas_call | solution.py:706
  48.4 1.8 %collective-permute-done.14.got = bf16[32,8192]{1,0:T(8,128)(2,1)S(1)} collective-permute-done((bf16[32,8192]{1,0:T(8,128)(2,1)S(1)}, bf16[32,8192]{1,0:T(8,128)(2,1)S(1)}, u32[]{:S(2)}, u32[]{:S(2)}) %collective-permute-start.14) | collective-permute-done | bytes 524320 | tf_op jit(solution)/shard_map/reduce_cores/ppermute | solution.py:184
  50.4 1.4 %collective-permute-start.17 = (bf16[8,8192]{1,0:T(8,128)(2,1)S(1)}, bf16[8,8192]{1,0:T(8,128)(2,1)S(1)}, u32[]{:S(2)}, u32[]{:S(2)}) collective-permute-start(bf16[8,8192]{1,0:T(8,128)(2,1)S(1)} %get-tuple-element.42), channel_id=1, source_target_pairs={{0,2},{1,3},{2,0},{3,1},{4,6},{5,7},{6,4},{7,5},{8,10},{9,11},{10,... | collective-permute-start | bytes 393224 | tf_op jit(solution)/shard_map/reduce_on_next_section/ppermute | solution.py:184
  51.8 2.7 %collective-permute-start.16 = (bf16[8,8192]{1,0:T(8,128)(2,1)S(1)}, bf16[8,8192]{1,0:T(8,128)(2,1)S(1)}, u32[]{:S(2)}, u32[]{:S(2)}) collective-permute-start(bf16[8,8192]{1,0:T(8,128)(2,1)S(1)} %get-tuple-element.40), channel_id=1, source_target_pairs={{0,10},{1,11},{2,8},{3,9},{4,14},{5,15},{6,12},{7,13},{8,18},{9,19... | collective-permute-start | bytes 393224 | tf_op jit(solution)/shard_map/reduce_on_next_section/ppermute | solution.py:192
  54.5 1.5 %collective-permute-done.17.across = bf16[8,8192]{1,0:T(8,128)(2,1)S(1)} collective-permute-done((bf16[8,8192]{1,0:T(8,128)(2,1)S(1)}, bf16[8,8192]{1,0:T(8,128)(2,1)S(1)}, u32[]{:S(2)}, u32[]{:S(2)}) %collective-permute-start.17) | collective-permute-done | bytes 131104 | tf_op jit(solution)/shard_map/reduce_on_next_section/ppermute | solution.py:184
  56.0 1.1 %collective-permute-start.18 = (bf16[8,8192]{1,0:T(8,128)(2,1)S(1)}, bf16[8,8192]{1,0:T(8,128)(2,1)S(1)}, u32[]{:S(2)}, u32[]{:S(2)}) collective-permute-start(bf16[8,8192]{1,0:T(8,128)(2,1)S(1)} %add_across.1), channel_id=1, source_target_pairs={{0,12},{1,13},{2,14},{3,15},{4,8},{5,9},{6,10},{7,11},{8,20},{9,21... | collective-permute-start | bytes 393224 | tf_op jit(solution)/shard_map/reduce_on_next_section/ppermute | solution.py:192
  57.1 2.8 %collective-permute-done.15 = bf16[8,8192]{1,0:T(8,128)(2,1)S(1)} collective-permute-done((bf16[8,8192]{1,0:T(8,128)(2,1)S(1)}, bf16[8,8192]{1,0:T(8,128)(2,1)S(1)}, u32[]{:S(2)}, u32[]{:S(2)}) %collective-permute-start.15) | collective-permute-done | bytes 131104 | tf_op jit(solution)/shard_map/reduce_on_next_section/ppermute | solution.py:192
  59.9 2.7 %collective-permute-done.16 = bf16[8,8192]{1,0:T(8,128)(2,1)S(1)} collective-permute-done((bf16[8,8192]{1,0:T(8,128)(2,1)S(1)}, bf16[8,8192]{1,0:T(8,128)(2,1)S(1)}, u32[]{:S(2)}, u32[]{:S(2)}) %collective-permute-start.16) | collective-permute-done | bytes 131104 | tf_op jit(solution)/shard_map/reduce_on_next_section/ppermute | solution.py:192
  62.6 2.2 %collective-permute-done.18 = bf16[8,8192]{1,0:T(8,128)(2,1)S(1)} collective-permute-done((bf16[8,8192]{1,0:T(8,128)(2,1)S(1)}, bf16[8,8192]{1,0:T(8,128)(2,1)S(1)}, u32[]{:S(2)}, u32[]{:S(2)}) %collective-permute-start.18) | collective-permute-done | bytes 131104 | tf_op jit(solution)/shard_map/reduce_on_next_section/ppermute | solution.py:192
  64.9 0.7 %fusion = bf16[1,8,8192]{2,1,0:T(8,128)(2,1)} fusion(bf16[8,8192]{1,0:T(8,128)(2,1)S(1)} %collective-permute-done.18, bf16[8,8192]{1,0:T(8,128)(2,1)S(1)} %collective-permute-done.16, bf16[8,8192]{1,0:T(8,128)(2,1)S(1)} %collective-permute-done.15), kind=kLoop, calls=%fused_computation.1 | loop fusion | flops 393216 | bytes 524288 | tf_op jit(solution)/shard_map/broadcast_in_dim | solution.py:734
  (51 shorter events, 1.2 us)
Async XLA Ops:
  0.0 10.7 %collective-permute-start.2 = (bf16[8,8192]{1,0:T(8,128)(2,1)}, bf16[8,8192]{1,0:T(8,128)(2,1)S(1)}, u32[]{:S(2)}, u32[]{:S(2)}) collective-permute-start(bf16[8,8192]{1,0:T(8,128)(2,1)} %bitcast.20), channel_id=1, source_target_pairs={{0,6},{1,7},{2,4},{3,5},{4,2},{5,3},{6,0},{7,1},{8,14},{9,15},{10,... | collective-permute-start | bytes 393224 | tf_op jit(solution)/shard_map/gather_tokens/ppermute | solution.py:184
  3.9 6.9 %collective-permute-start.1 = (bf16[8,8192]{1,0:T(8,128)(2,1)}, bf16[8,8192]{1,0:T(8,128)(2,1)S(1)}, u32[]{:S(2)}, u32[]{:S(2)}) collective-permute-start(bf16[8,8192]{1,0:T(8,128)(2,1)} %bitcast.21), channel_id=1, source_target_pairs={{0,4},{1,5},{2,6},{3,7},{4,0},{5,1},{6,2},{7,3},{8,12},{9,13},{10,... | collective-permute-start | bytes 393224 | tf_op jit(solution)/shard_map/gather_tokens/ppermute | solution.py:184
  4.4 6.4 %collective-permute-start = (bf16[8,8192]{1,0:T(8,128)(2,1)}, bf16[8,8192]{1,0:T(8,128)(2,1)S(1)}, u32[]{:S(2)}, u32[]{:S(2)}) collective-permute-start(bf16[8,8192]{1,0:T(8,128)(2,1)} %bitcast.22), channel_id=1, source_target_pairs={{0,2},{1,3},{2,0},{3,1},{4,6},{5,7},{6,4},{7,5},{8,10},{9,11},{10,... | collective-permute-start | bytes 393224 | tf_op jit(solution)/shard_map/gather_tokens/ppermute | solution.py:184
  4.5 8.3 %slice-start = ((s8[16777216]{0:T(1024)(128)(4,1)}), s8[4194304]{0:T(1024)(128)(4,1)S(1)}, s32[]{:S(2)}) async-start(s8[16777216]{0:T(1024)(128)(4,1)} %bitcast.12), calls=%async_computation | async-start | bytes 8388608
  4.5 6.3 %copy-start.2 = (bf16[1,8,8192]{2,1,0:T(8,128)(2,1)S(1)}, bf16[1,8,8192]{2,1,0:T(8,128)(2,1)}, u32[]{:S(2)}) copy-start(bf16[1,8,8192]{2,1,0:T(8,128)(2,1)} %param.10) | copy-start | bytes 393220
  4.5 8.3 %slice-start.1 = ((s8[16777216]{0:T(1024)(128)(4,1)}), s8[4194304]{0:T(1024)(128)(4,1)S(1)}, s32[]{:S(2)}) async-start(s8[16777216]{0:T(1024)(128)(4,1)} %bitcast.12), calls=%async_computation.1 | async-start | bytes 8388608
  4.5 8.3 %slice-start.2 = ((s8[16777216]{0:T(1024)(128)(4,1)}), s8[4194304]{0:T(1024)(128)(4,1)S(1)}, s32[]{:S(2)}) async-start(s8[16777216]{0:T(1024)(128)(4,1)} %bitcast.12), calls=%async_computation.2 | async-start | bytes 8388608
  4.5 8.4 %slice-start.3 = ((s8[16777216]{0:T(1024)(128)(4,1)}), s8[4194304]{0:T(1024)(128)(4,1)S(1)}, s32[]{:S(2)}) async-start(s8[16777216]{0:T(1024)(128)(4,1)} %bitcast.12), calls=%async_computation.3 | async-start | bytes 8388608
  4.5 8.4 %copy-start.3 = (bf16[1,8192]{1,0:T(2,128)(2,1)S(1)}, bf16[1,8192]{1,0:T(2,128)(2,1)}, u32[]{:S(2)}) copy-start(bf16[1,8192]{1,0:T(2,128)(2,1)} %refs_2_.1) | copy-start | bytes 49156
  10.8 2.0 %collective-permute-start.3 = (bf16[4,8,8192]{2,1,0:T(8,128)(2,1)S(1)}, bf16[4,8,8192]{2,1,0:T(8,128)(2,1)S(1)}, u32[]{:S(2)}, u32[]{:S(2)}) collective-permute-start(bf16[4,8,8192]{2,1,0:T(8,128)(2,1)S(1)} %join_tokens.1.refs_0_), channel_id=1, source_target_pairs={{0,1},{1,0},{2,3},{3,2},{4,5},{5,4},{6,7},{7,6},{8,9},{9,8},{10,11... | collective-permute-start | bytes 1572872 | tf_op jit(solution)/shard_map/gather_tokens/ppermute | solution.py:184
  12.9 7.0 %copy-start.4 = (s32[1,2,16]{2,1,0:T(2,128)S(1)}, s32[1,2,16]{2,1,0:T(2,128)}, u32[]{:S(2)}) copy-start(s32[1,2,16]{2,1,0:T(2,128)} %param.18) | copy-start | bytes 388
  16.4 3.4 %collective-permute-start.4 = (bf16[64,1024]{1,0:T(8,128)(2,1)S(1)}, bf16[64,1024]{1,0:T(8,128)(2,1)S(1)}, u32[]{:S(2)}, u32[]{:S(2)}) collective-permute-start(bf16[64,1024]{1,0:T(8,128)(2,1)S(1)} %get-tuple-element.25.refs_2_.refs_0_), channel_id=1, source_target_pairs={{0,1},{1,0},{2,3},{3,2},{4,5},{5,4},{6,7},{7,6},{8,9},{9,8},{10,11... | collective-permute-start | bytes 393224 | tf_op jit(solution)/shard_map/gather_queries/ppermute | solution.py:184
  16.6 6.8 %collective-permute-start.7 = (bf16[64,1024]{1,0:T(8,128)(2,1)S(1)}, bf16[64,1024]{1,0:T(8,128)(2,1)S(1)}, u32[]{:S(2)}, u32[]{:S(2)}) collective-permute-start(bf16[64,1024]{1,0:T(8,128)(2,1)S(1)} %get-tuple-element.25.refs_2_.refs_0_), channel_id=1, source_target_pairs={{0,7},{1,6},{2,5},{3,4},{4,3},{5,2},{6,1},{7,0},{8,15},{9,14},{10,... | collective-permute-start | bytes 393224 | tf_op jit(solution)/shard_map/gather_queries/ppermute | solution.py:184
  19.5 6.8 %collective-permute-start.6 = (bf16[64,1024]{1,0:T(8,128)(2,1)S(1)}, bf16[64,1024]{1,0:T(8,128)(2,1)S(1)}, u32[]{:S(2)}, u32[]{:S(2)}) collective-permute-start(bf16[64,1024]{1,0:T(8,128)(2,1)S(1)} %get-tuple-element.25.refs_2_.refs_0_), channel_id=1, source_target_pairs={{0,5},{1,4},{2,7},{3,6},{4,1},{5,0},{6,3},{7,2},{8,13},{9,12},{10,... | collective-permute-start | bytes 393224 | tf_op jit(solution)/shard_map/gather_queries/ppermute | solution.py:184
  19.8 6.6 %collective-permute-start.5 = (bf16[64,1024]{1,0:T(8,128)(2,1)S(1)}, bf16[64,1024]{1,0:T(8,128)(2,1)S(1)}, u32[]{:S(2)}, u32[]{:S(2)}) collective-permute-start(bf16[64,1024]{1,0:T(8,128)(2,1)S(1)} %get-tuple-element.25.refs_2_.refs_0_), channel_id=1, source_target_pairs={{0,3},{1,2},{2,1},{3,0},{4,7},{5,6},{6,5},{7,4},{8,11},{9,10},{10,... | collective-permute-start | bytes 393224 | tf_op jit(solution)/shard_map/gather_queries/ppermute | solution.py:184
  26.4 4.3 %collective-permute-start.8 = (bf16[3,64,1024]{2,1,0:T(8,128)(2,1)S(1)}, bf16[3,64,1024]{2,1,0:T(8,128)(2,1)S(1)}, u32[]{:S(2)}, u32[]{:S(2)}) collective-permute-start(bf16[3,64,1024]{2,1,0:T(8,128)(2,1)S(1)} %join_queries.1.refs_2_), channel_id=1, source_target_pairs={{0,1},{1,0},{2,3},{3,2},{4,5},{5,4},{6,7},{7,6},{8,9},{9,8},{10,11... | collective-permute-start | bytes 1179656 | tf_op jit(solution)/shard_map/gather_queries/ppermute | solution.py:184
  26.6 11.3 %copy-start.1 = (bf16[1,8192,128]{2,1,0:T(8,128)(2,1)S(1)}, bf16[1,8192,128]{2,1,0:T(8,128)(2,1)}, u32[]{:S(2)}) copy-start(bf16[1,8192,128]{2,1,0:T(8,128)(2,1)} %param.14) | copy-start | bytes 6291460
  26.6 18.3 %slice-start.4 = ((s8[16777216]{0:T(1024)(128)(4,1)}), s8[4194304]{0:T(1024)(128)(4,1)S(1)}, s32[]{:S(2)}) async-start(s8[16777216]{0:T(1024)(128)(4,1)} %bitcast.15), calls=%async_computation.4 | async-start | bytes 8388608
  26.6 18.3 %slice-start.5 = ((s8[16777216]{0:T(1024)(128)(4,1)}), s8[4194304]{0:T(1024)(128)(4,1)S(1)}, s32[]{:S(2)}) async-start(s8[16777216]{0:T(1024)(128)(4,1)} %bitcast.15), calls=%async_computation.5 | async-start | bytes 8388608
  30.1 4.0 %collective-permute-start.10 = (bf16[3,144,512]{2,1,0:T(8,128)(2,1)S(1)}, bf16[3,144,512]{2,1,0:T(8,128)(2,1)S(1)}, u32[]{:S(2)}, u32[]{:S(2)}) collective-permute-start(bf16[3,144,512]{2,1,0:T(8,128)(2,1)S(1)} %cache_odd.1), channel_id=1, source_target_pairs={{0,1},{1,0},{2,3},{3,2},{4,5},{5,4},{6,7},{7,6},{8,9},{9,8},{10,11... | collective-permute-start | bytes 1327112 | tf_op jit(solution)/shard_map/cache_odd/ppermute | solution.py:184
  30.2 7.8 %copy-start = (bf16[1,8192,128]{2,1,0:T(8,128)(2,1)S(1)}, bf16[1,8192,128]{2,1,0:T(8,128)(2,1)}, u32[]{:S(2)}) copy-start(bf16[1,8192,128]{2,1,0:T(8,128)(2,1)} %param.13) | copy-start | bytes 6291460
  30.2 14.8 %slice-start.6 = ((s8[16777216]{0:T(1024)(128)(4,1)}), s8[4194304]{0:T(1024)(128)(4,1)S(1)}, s32[]{:S(2)}) async-start(s8[16777216]{0:T(1024)(128)(4,1)} %bitcast.15), calls=%async_computation.6 | async-start | bytes 8388608
  30.2 14.8 %slice-start.7 = ((s8[16777216]{0:T(1024)(128)(4,1)}), s8[4194304]{0:T(1024)(128)(4,1)S(1)}, s32[]{:S(2)}) async-start(s8[16777216]{0:T(1024)(128)(4,1)} %bitcast.15), calls=%async_computation.7 | async-start | bytes 8388608
  30.2 3.9 %collective-permute-start.9 = (bf16[1,144,512]{2,1,0:T(8,128)(2,1)S(1)}, bf16[1,144,512]{2,1,0:T(8,128)(2,1)S(1)}, u32[]{:S(2)}, u32[]{:S(2)}) collective-permute-start(bf16[1,144,512]{2,1,0:T(8,128)(2,1)S(1)} %get-tuple-element.29), channel_id=1, source_target_pairs={{0,1},{1,0},{2,3},{3,2},{4,5},{5,4},{6,7},{7,6},{8,9},{9,8},{10,11... | collective-permute-start | bytes 442376 | tf_op jit(solution)/shard_map/cache_near/ppermute | solution.py:184
  34.4 6.7 %collective-permute-start.11 = (bf16[144,512]{1,0:T(8,128)(2,1)S(1)}, bf16[144,512]{1,0:T(8,128)(2,1)S(1)}, u32[]{:S(2)}, u32[]{:S(2)}) collective-permute-start(bf16[144,512]{1,0:T(8,128)(2,1)S(1)} %get-tuple-element.31), channel_id=1, source_target_pairs={{0,2},{1,3},{2,0},{3,1},{4,6},{5,7},{6,4},{7,5},{8,10},{9,11},{10,... | collective-permute-start | bytes 442376 | tf_op jit(solution)/shard_map/exchange_parts/ppermute | solution.py:184
  35.3 6.0 %collective-permute-start.12 = (bf16[144,512]{1,0:T(8,128)(2,1)S(1)}, bf16[144,512]{1,0:T(8,128)(2,1)S(1)}, u32[]{:S(2)}, u32[]{:S(2)}) collective-permute-start(bf16[144,512]{1,0:T(8,128)(2,1)S(1)} %get-tuple-element.32), channel_id=1, source_target_pairs={{0,4},{1,5},{2,6},{3,7},{4,0},{5,1},{6,2},{7,3},{8,12},{9,13},{10,... | collective-permute-start | bytes 442376 | tf_op jit(solution)/shard_map/exchange_parts/ppermute | solution.py:184
  35.8 9.2 %collective-permute-start.13 = (bf16[144,512]{1,0:T(8,128)(2,1)S(1)}, bf16[144,512]{1,0:T(8,128)(2,1)S(1)}, u32[]{:S(2)}, u32[]{:S(2)}) collective-permute-start(bf16[144,512]{1,0:T(8,128)(2,1)S(1)} %get-tuple-element.33), channel_id=1, source_target_pairs={{0,6},{1,7},{2,4},{3,5},{4,2},{5,3},{6,0},{7,1},{8,14},{9,15},{10,... | collective-permute-start | bytes 442376 | tf_op jit(solution)/shard_map/exchange_parts/ppermute | solution.py:184
  48.3 2.0 %collective-permute-start.14 = (bf16[32,8192]{1,0:T(8,128)(2,1)S(1)}, bf16[32,8192]{1,0:T(8,128)(2,1)S(1)}, u32[]{:S(2)}, u32[]{:S(2)}) collective-permute-start(bf16[32,8192]{1,0:T(8,128)(2,1)S(1)} %get-tuple-element.38), channel_id=1, source_target_pairs={{0,1},{1,0},{2,3},{3,2},{4,5},{5,4},{6,7},{7,6},{8,9},{9,8},{10,11... | collective-permute-start | bytes 1572872 | tf_op jit(solution)/shard_map/reduce_cores/ppermute | solution.py:184
  50.4 5.6 %collective-permute-start.17 = (bf16[8,8192]{1,0:T(8,128)(2,1)S(1)}, bf16[8,8192]{1,0:T(8,128)(2,1)S(1)}, u32[]{:S(2)}, u32[]{:S(2)}) collective-permute-start(bf16[8,8192]{1,0:T(8,128)(2,1)S(1)} %get-tuple-element.42), channel_id=1, source_target_pairs={{0,2},{1,3},{2,0},{3,1},{4,6},{5,7},{6,4},{7,5},{8,10},{9,11},{10,... | collective-permute-start | bytes 393224 | tf_op jit(solution)/shard_map/reduce_on_next_section/ppermute | solution.py:184
  51.8 8.2 %collective-permute-start.15 = (bf16[8,8192]{1,0:T(8,128)(2,1)S(1)}, bf16[8,8192]{1,0:T(8,128)(2,1)S(1)}, u32[]{:S(2)}, u32[]{:S(2)}) collective-permute-start(bf16[8,8192]{1,0:T(8,128)(2,1)S(1)} %get-tuple-element.39), channel_id=1, source_target_pairs={{0,8},{1,9},{2,10},{3,11},{4,12},{5,13},{6,14},{7,15},{8,16},{9,17... | collective-permute-start | bytes 393224 | tf_op jit(solution)/shard_map/reduce_on_next_section/ppermute | solution.py:192
  51.8 10.9 %collective-permute-start.16 = (bf16[8,8192]{1,0:T(8,128)(2,1)S(1)}, bf16[8,8192]{1,0:T(8,128)(2,1)S(1)}, u32[]{:S(2)}, u32[]{:S(2)}) collective-permute-start(bf16[8,8192]{1,0:T(8,128)(2,1)S(1)} %get-tuple-element.40), channel_id=1, source_target_pairs={{0,10},{1,11},{2,8},{3,9},{4,14},{5,15},{6,12},{7,13},{8,18},{9,19... | collective-permute-start | bytes 393224 | tf_op jit(solution)/shard_map/reduce_on_next_section/ppermute | solution.py:192
  56.0 8.9 %collective-permute-start.18 = (bf16[8,8192]{1,0:T(8,128)(2,1)S(1)}, bf16[8,8192]{1,0:T(8,128)(2,1)S(1)}, u32[]{:S(2)}, u32[]{:S(2)}) collective-permute-start(bf16[8,8192]{1,0:T(8,128)(2,1)S(1)} %add_across.1), channel_id=1, source_target_pairs={{0,12},{1,13},{2,14},{3,15},{4,8},{5,9},{6,10},{7,11},{8,20},{9,21... | collective-permute-start | bytes 393224 | tf_op jit(solution)/shard_map/reduce_on_next_section/ppermute | solution.py:192

commit v6 on v5

--- a/solution.py
+++ b/solution.py
@@ -532,7 +532,8 @@
     stats,
     weights,
     own,
-    sent,
+    sent_near,
+    sent_far,
     rows,
     sorted_rows,
 ):
@@ -573,15 +574,18 @@
             sorted_rows[...], weights[:, c : c + step], preferred_element_type=jnp.float32
         )
         own[:, c : c + step] = product[:half]
-        sent[:, c : c + step] = product[half:].astype(jnp.bfloat16)
-
-
-def pair_kernel(own, got, resid, *outs):
-    count = resid.shape[0]
+        sent = product[half:].astype(jnp.bfloat16)
+        sent_near[:, c : c + step] = sent[: half // 2]
+        sent_far[:, c : c + step] = sent[half // 2 :]
+
+
+def pair_kernel(first, own, got, *outs, resid=None):
+    count = outs[0].shape[0]
+    other = got[...].astype(jnp.float32)
     for i, out in enumerate(outs):
-        rows = slice(i * count, (i + 1) * count)
-        block = own[rows] + got[...].astype(jnp.float32)[rows]
-        if i == 0:
+        block = own[(first + i) * count : (first + i + 1) * count]
+        block = block + other[i * count : (i + 1) * count]
+        if resid is not None and i == 0:
             block = resid[...].astype(jnp.float32) + block
         out[...] = block.astype(out.dtype)
 
@@ -703,12 +707,13 @@
     with jax.named_scope("exchange_parts"):
         parts = [swapped(block, bits) for block, bits in zip(sent, SAME_CORE)]
     with jax.named_scope("project"):
-        own, other = call(
+        own, near, far = call(
             output_kernel,
             "project",
             [
                 jax.ShapeDtypeStruct((tok // 2, width), jnp.float32),
-                jax.ShapeDtypeStruct((tok // 2, width), jnp.bfloat16),
+                jax.ShapeDtypeStruct((tok // 4, width), jnp.bfloat16),
+                jax.ShapeDtypeStruct((tok // 4, width), jnp.bfloat16),
             ],
             [IN_SMEM] + [IN_VMEM] * 7,
             flops=8 * tok * width * own_cols // 2,
@@ -721,9 +726,20 @@
     with jax.named_scope("reduce_cores"):
         row = jax.ShapeDtypeStruct((count, width), jnp.bfloat16)
         row_f32 = jax.ShapeDtypeStruct((count, width), jnp.float32)
-        at_own, at_x, at_y, to_x = call(
-            pair_kernel, "reduce_cores", [row, row, row_f32, row], [IN_VMEM] * 3, nbytes=2 * MIB
-        )(own, swapped(other, 1), tokens[0])
+        at_y, to_x = call(
+            lambda *refs: pair_kernel(2, *refs),
+            "reduce_far",
+            [row_f32, row],
+            [IN_VMEM] * 2,
+            nbytes=MIB,
+        )(own, swapped(far, 1))
+        at_own, at_x = call(
+            lambda own, got, resid, *outs: pair_kernel(0, own, got, *outs, resid=resid),
+            "reduce_near",
+            [row, row],
+            [IN_VMEM] * 3,
+            nbytes=MIB,
+        )(own, swapped(near, 1), tokens[0])
     with jax.named_scope("reduce_on_next_section"):
         across = swapped(to_x, EVEN[1])
         from_own, from_x = onward(at_own, EVEN[0]), onward(at_x, EVEN[1])

time: 65.5 us -> 65 us (level)
  starting transfers between devices: 17.6 us -> 20.5 us
  waiting for transfers between devices: 22.1 us -> 19.3 us
  Pallas kernels: 23.1 us -> 21.9 us
    ppermute x3, starting transfers between devices: 3.8 us -> 5.8 us  [onward(): return lax.ppermute(block, ('section', 'seq'), route)]
    ppermute x16 -> x17, waiting for transfers between devices: 14.4 us -> 12.4 us  [swapped(): return lax.ppermute(block, 'seq', [(i, i ^ bits) for i in range(n)])]
    pallas_call x3, Pallas kernels: 9.84 us -> 8.69 us  [cache_part(): call(lambda *refs: cache_kernel(scale, order, *refs), name, outs, [IN_SME...]
    ppermute x16 -> x17, starting transfers between devices: 13.8 us -> 14.7 us  [swapped(): return lax.ppermute(block, 'seq', [(i, i ^ bits) for i in range(n)])]
    ppermute x3, waiting for transfers between devices: 7.75 us -> 6.91 us  [onward(): return lax.ppermute(block, ('section', 'seq'), route)]
  transfers between devices with their start and end apart: 19 -> 20, of which waited for: 11 -> 11; matrix products, arithmetic and copies ran while one was open for 0% -> 0% of each run, Pallas kernels for 24% -> 23%
where the time goes in v6:
time: 65 us; the launch traced here: 64.5 us
  Pallas kernels  21.9 us (34%)
  starting transfers between devices  20.5 us (32%)
  waiting for transfers between devices  19.3 us (30%)
  between operations  1.67 us (3%)
  other arithmetic  1 us (2%)
    ppermute x17, starting transfers between devices, swapped(): return lax.ppermute(block, 'seq', [(i, i ^ bits) for i in range(n)])  14.7 us
    ppermute x17, waiting for transfers between devices, swapped(): return lax.ppermute(block, 'seq', [(i, i ^ bits) for i in range(n)])  12.4 us
    pallas_call x3, Pallas kernels, cache_part(): call(lambda *refs: cache_kernel(scale, order, *refs), name, outs, [IN_SME...  8.69 us
    ppermute x3, waiting for transfers between devices, onward(): return lax.ppermute(block, ('section', 'seq'), route)  6.91 us
    ppermute x3, starting transfers between devices, onward(): return lax.ppermute(block, ('section', 'seq'), route)  5.8 us
    pallas_call x1, Pallas kernels, cache_by_head(): call(by_head_kernel, 'cache_by_head', [jax.ShapeDtypeStruct((heads, ctx,...  4.79 us
    pallas_call x1, Pallas kernels, on_device_owned(): call(query_kernel, 'queries', [jax.ShapeDtypeStruct((tok, own_cols), jnp....  3.57 us
    pallas_call x1, Pallas kernels, on_device_owned(): call(output_kernel, 'project', [jax.ShapeDtypeStruct((tok // 2, width), j...  3.25 us
  transfers between devices with their start and end apart: 20, of which 11 were waited for; matrix products, arithmetic and copies ran while one was open for 0% of the time, Pallas kernels for 23%

profile of v6, /device:TPU:0, one launch (start us, length us, event | category | flops | bytes accessed | tf_op | source)
XLA Modules:
  0.0 64.5 jit_solution(10946937450283102930)
XLA Ops:
  0.0 3.9 %collective-permute-start.2 = (bf16[8,8192]{1,0:T(8,128)(2,1)}, bf16[8,8192]{1,0:T(8,128)(2,1)S(1)}, u32[]{:S(2)}, u32[]{:S(2)}) collective-permute-start(bf16[8,8192]{1,0:T(8,128)(2,1)} %bitcast.20), channel_id=1, source_target_pairs={{0,6},{1,7},{2,4},{3,5},{4,2},{5,3},{6,0},{7,1},{8,14},{9,15},{10,... | collective-permute-start | bytes 393224 | tf_op jit(solution)/shard_map/gather_tokens/ppermute | solution.py:184
  3.9 0.5 collective-permute-start.1
  4.5 4.8 %cache_by_head.1 = (bf16[8,2048,128]{2,1,0:T(8,128)(2,1)S(1)}, bf16[8,128,2048]{2,1,0:T(8,128)(2,1)S(1)}, f32[8,128]{1,0:T(8,128)S(1)}) custom-call(s32[1]{0:T(128)} %bitcast.rank.refs_0_, bf16[2048,8,128]{2,1,0:T(8,128)(2,1)} %bitcast.28, bf16[2048,8,128]{2,1,0:T(8,128)(2,1)} %bitcast.29), custom_call_target="tpu_custom_call" | custom-call | flops 10000000000 | bytes 4194304 | tf_op jit(solution)/shard_map/cache_layout/cache_by_head/pallas_call | solution.py:308
  11.2 1.6 %collective-permute-done.3.refs_1_ = bf16[4,8,8192]{2,1,0:T(8,128)(2,1)S(1)} collective-permute-done((bf16[4,8,8192]{2,1,0:T(8,128)(2,1)S(1)}, bf16[4,8,8192]{2,1,0:T(8,128)(2,1)S(1)}, u32[]{:S(2)}, u32[]{:S(2)}) %collective-permute-start.3) | collective-permute-done | bytes 524320 | tf_op jit(solution)/shard_map/gather_tokens/ppermute | solution.py:184
  12.9 3.6 %queries.1 = (bf16[64,1024]{1,0:T(8,128)(2,1)S(1)}, bf16[64,8192]{1,0:T(8,128)(2,1)S(1)}) custom-call(s32[1]{0:T(128)} %bitcast.rank.refs_0_, bf16[4,8,8192]{2,1,0:T(8,128)(2,1)S(1)} %join_tokens.1.refs_0_, bf16[4,8,8192]{2,1,0:T(8,128)(2,1)S(1)} %collective-permute-done.3.refs_1_, bf16[1,8192]{1,0:T(2,128)(2,1)S(1)} %copy-done.3, ...), custom_call_target="tpu_custom_call" | custom-call | flops 2147483648 | bytes 16777216 | tf_op jit(solution)/shard_map/queries/queries/pallas_call | solution.py:639
  16.6 2.9 %collective-permute-start.7 = (bf16[64,1024]{1,0:T(8,128)(2,1)S(1)}, bf16[64,1024]{1,0:T(8,128)(2,1)S(1)}, u32[]{:S(2)}, u32[]{:S(2)}) collective-permute-start(bf16[64,1024]{1,0:T(8,128)(2,1)S(1)} %get-tuple-element.26.refs_2_.refs_0_), channel_id=1, source_target_pairs={{0,7},{1,6},{2,5},{3,4},{4,3},{5,2},{6,1},{7,0},{8,15},{9,14},{10,... | collective-permute-start | bytes 393224 | tf_op jit(solution)/shard_map/gather_queries/ppermute | solution.py:184
  19.5 0.3 collective-permute-start.6
  19.9 2.6 %cache_near.1 = (f32[1,136,512]{2,1,0:T(8,128)S(1)}, bf16[1,144,512]{2,1,0:T(8,128)(2,1)S(1)}) custom-call(s32[1]{0:T(128)} %bitcast.rank.refs_0_, s32[2,16]{1,0:T(2,128)S(1)} %bitcast.25, bf16[64,1024]{1,0:T(8,128)(2,1)S(1)} %get-tuple-element.26.refs_2_.refs_0_, bf16[64,1024]{1,0:T(8,128)(2,1)S(1)} %collective-permute-done.4.refs_3_, ...), custom_call_target="tpu_custom_call" | custom-call | flops 536870912 | bytes 2097152 | tf_op jit(solution)/shard_map/cache_near/cache_near/pallas_call | solution.py:491
  22.5 0.9 %collective-permute-done.7.refs_2_ = bf16[64,1024]{1,0:T(8,128)(2,1)S(1)} collective-permute-done((bf16[64,1024]{1,0:T(8,128)(2,1)S(1)}, bf16[64,1024]{1,0:T(8,128)(2,1)S(1)}, u32[]{:S(2)}, u32[]{:S(2)}) %collective-permute-start.7) | collective-permute-done | bytes 131104 | tf_op jit(solution)/shard_map/gather_queries/ppermute | solution.py:184
  23.4 3.0 %collective-permute-done.6.refs_1_ = bf16[64,1024]{1,0:T(8,128)(2,1)S(1)} collective-permute-done((bf16[64,1024]{1,0:T(8,128)(2,1)S(1)}, bf16[64,1024]{1,0:T(8,128)(2,1)S(1)}, u32[]{:S(2)}, u32[]{:S(2)}) %collective-permute-start.6) | collective-permute-done | bytes 131104 | tf_op jit(solution)/shard_map/gather_queries/ppermute | solution.py:184
  26.7 3.0 %cache_odd.1 = bf16[3,144,512]{2,1,0:T(8,128)(2,1)S(1)} custom-call(s32[1]{0:T(128)} %bitcast.rank.refs_0_, s32[2,16]{1,0:T(2,128)S(1)} %bitcast.26, bf16[3,64,1024]{2,1,0:T(8,128)(2,1)S(1)} %join_queries.1.refs_2_, bf16[8,2048,128]{2,1,0:T(8,128)(2,1)S(1)} %get-tuple-element.27.refs_4_.refs_3_, bf16[8,128,2048]{2,1,0:T(8,128)(2,1)S(1)} %get-tuple-element.28.refs_5_.refs_4_), custom_call_target="tpu_custom_call" | custom-call | flops 4026531840 | bytes 3145728 | tf_op jit(solution)/shard_map/cache_odd/cache_odd/pallas_call | solution.py:491
  29.7 0.4 collective-permute-start.10
  30.3 3.0 %cache_even.1.own_rest = f32[3,136,512]{2,1,0:T(8,128)S(1)} custom-call(s32[1]{0:T(128)} %bitcast.rank.refs_0_, s32[2,16]{1,0:T(2,128)S(1)} %bitcast.27, bf16[3,64,1024]{2,1,0:T(8,128)(2,1)S(1)} %collective-permute-done.8.refs_2_, bf16[8,2048,128]{2,1,0:T(8,128)(2,1)S(1)} %get-tuple-element.27.refs_4_.refs_3_, ...), custom_call_target="tpu_custom_call" | custom-call | flops 805306368 | bytes 3145728 | tf_op jit(solution)/shard_map/cache_even/cache_even/pallas_call | solution.py:491
  33.3 0.3 merge_cores.1
  33.6 1.7 %collective-permute-start.11 = (bf16[144,512]{1,0:T(8,128)(2,1)S(1)}, bf16[144,512]{1,0:T(8,128)(2,1)S(1)}, u32[]{:S(2)}, u32[]{:S(2)}) collective-permute-start(bf16[144,512]{1,0:T(8,128)(2,1)S(1)} %get-tuple-element.32), channel_id=1, source_target_pairs={{0,2},{1,3},{2,0},{3,1},{4,6},{5,7},{6,4},{7,5},{8,10},{9,11},{10,... | collective-permute-start | bytes 442376 | tf_op jit(solution)/shard_map/exchange_parts/ppermute | solution.py:184
  35.5 1.7 %collective-permute-start.13 = (bf16[144,512]{1,0:T(8,128)(2,1)S(1)}, bf16[144,512]{1,0:T(8,128)(2,1)S(1)}, u32[]{:S(2)}, u32[]{:S(2)}) collective-permute-start(bf16[144,512]{1,0:T(8,128)(2,1)S(1)} %get-tuple-element.34), channel_id=1, source_target_pairs={{0,6},{1,7},{2,4},{3,5},{4,2},{5,3},{6,0},{7,1},{8,14},{9,15},{10,... | collective-permute-start | bytes 442376 | tf_op jit(solution)/shard_map/exchange_parts/ppermute | solution.py:184
  37.2 1.1 %new_tokens.1 = (f32[128,512]{1,0:T(8,128)S(1)}, f32[8,512]{1,0:T(8,128)S(1)}) custom-call(bf16[64,1024]{1,0:T(8,128)(2,1)S(1)} %get-tuple-element.26.refs_2_.refs_0_, bf16[64,8192]{1,0:T(8,128)(2,1)S(1)} %get-tuple-element.35.refs_1_, bf16[8192,128]{1,0:T(8,128)(2,1)S(1)} %bitcast.18, bf16[8192,128]{1,0:T(8,128)(2,1)S(1)} %bitcast.19, ...), custom_call_target="tpu_custom_call" | custom-call | flops 1073741824 | bytes 5242880 | tf_op jit(solution)/shard_map/new_tokens/new_tokens/pallas_call | solution.py:665
  38.3 2.0 %collective-permute-done.11.got_a = bf16[144,512]{1,0:T(8,128)(2,1)S(1)} collective-permute-done((bf16[144,512]{1,0:T(8,128)(2,1)S(1)}, bf16[144,512]{1,0:T(8,128)(2,1)S(1)}, u32[]{:S(2)}, u32[]{:S(2)}) %collective-permute-start.11) | collective-permute-done | bytes 147488 | tf_op jit(solution)/shard_map/exchange_parts/ppermute | solution.py:184
  40.3 2.3 %collective-permute-done.12.got_b = bf16[144,512]{1,0:T(8,128)(2,1)S(1)} collective-permute-done((bf16[144,512]{1,0:T(8,128)(2,1)S(1)}, bf16[144,512]{1,0:T(8,128)(2,1)S(1)}, u32[]{:S(2)}, u32[]{:S(2)}) %collective-permute-start.12) | collective-permute-done | bytes 147488 | tf_op jit(solution)/shard_map/exchange_parts/ppermute | solution.py:184
  42.6 1.1 %collective-permute-done.13.got_c = bf16[144,512]{1,0:T(8,128)(2,1)S(1)} collective-permute-done((bf16[144,512]{1,0:T(8,128)(2,1)S(1)}, bf16[144,512]{1,0:T(8,128)(2,1)S(1)}, u32[]{:S(2)}, u32[]{:S(2)}) %collective-permute-start.13) | collective-permute-done | bytes 147488 | tf_op jit(solution)/shard_map/exchange_parts/ppermute | solution.py:184
  43.7 3.2 %project.1 = (f32[32,8192]{1,0:T(8,128)S(1)}, bf16[16,8192]{1,0:T(8,128)(2,1)S(1)}, bf16[16,8192]{1,0:T(8,128)(2,1)S(1)}) custom-call(s32[1]{0:T(128)} %bitcast.rank.refs_0_, f32[136,512]{1,0:T(8,128)S(1)} %get-tuple-element.31.kept, bf16[144,512]{1,0:T(8,128)(2,1)S(1)} %collective-permute-done.11.got_a, bf16[144,512]{1,0:T(8,128)(2,1)S(1)} %collective-permute-done.12.got_b, ...), custom_call_target="tpu_custom_call" | custom-call | flops 2147483648 | bytes 18874368 | tf_op jit(solution)/shard_map/project/project/pallas_call | solution.py:710
  47.0 0.4 collective-permute-start.17
  47.6 1.0 %collective-permute-done.17.refs_1_ = bf16[16,8192]{1,0:T(8,128)(2,1)S(1)} collective-permute-done((bf16[16,8192]{1,0:T(8,128)(2,1)S(1)}, bf16[16,8192]{1,0:T(8,128)(2,1)S(1)}, u32[]{:S(2)}, u32[]{:S(2)}) %collective-permute-start.17) | collective-permute-done | bytes 262176 | tf_op jit(solution)/shard_map/reduce_cores/ppermute | solution.py:184
  48.7 1.8 %collective-permute-start.18 = (bf16[8,8192]{1,0:T(8,128)(2,1)S(1)}, bf16[8,8192]{1,0:T(8,128)(2,1)S(1)}, u32[]{:S(2)}, u32[]{:S(2)}) collective-permute-start(bf16[8,8192]{1,0:T(8,128)(2,1)S(1)} %get-tuple-element.44), channel_id=1, source_target_pairs={{0,2},{1,3},{2,0},{3,1},{4,6},{5,7},{6,4},{7,5},{8,10},{9,11},{10,... | collective-permute-start | bytes 393224 | tf_op jit(solution)/shard_map/reduce_on_next_section/ppermute | solution.py:184
  50.6 1.1 %collective-permute-start.15 = (bf16[8,8192]{1,0:T(8,128)(2,1)S(1)}, bf16[8,8192]{1,0:T(8,128)(2,1)S(1)}, u32[]{:S(2)}, u32[]{:S(2)}) collective-permute-start(bf16[8,8192]{1,0:T(8,128)(2,1)S(1)} %get-tuple-element.40), channel_id=1, source_target_pairs={{0,8},{1,9},{2,10},{3,11},{4,12},{5,13},{6,14},{7,15},{8,16},{9,17... | collective-permute-start | bytes 393224 | tf_op jit(solution)/shard_map/reduce_on_next_section/ppermute | solution.py:192
  51.6 2.4 %collective-permute-start.16 = (bf16[8,8192]{1,0:T(8,128)(2,1)S(1)}, bf16[8,8192]{1,0:T(8,128)(2,1)S(1)}, u32[]{:S(2)}, u32[]{:S(2)}) collective-permute-start(bf16[8,8192]{1,0:T(8,128)(2,1)S(1)} %get-tuple-element.41), channel_id=1, source_target_pairs={{0,10},{1,11},{2,8},{3,9},{4,14},{5,15},{6,12},{7,13},{8,18},{9,19... | collective-permute-start | bytes 393224 | tf_op jit(solution)/shard_map/reduce_on_next_section/ppermute | solution.py:192
  54.0 0.5 collective-permute-done.18.across
  54.5 2.4 %collective-permute-start.19 = (bf16[8,8192]{1,0:T(8,128)(2,1)S(1)}, bf16[8,8192]{1,0:T(8,128)(2,1)S(1)}, u32[]{:S(2)}, u32[]{:S(2)}) collective-permute-start(bf16[8,8192]{1,0:T(8,128)(2,1)S(1)} %add_across.1), channel_id=1, source_target_pairs={{0,12},{1,13},{2,14},{3,15},{4,8},{5,9},{6,10},{7,11},{8,20},{9,21... | collective-permute-start | bytes 393224 | tf_op jit(solution)/shard_map/reduce_on_next_section/ppermute | solution.py:192
  56.9 1.9 %collective-permute-done.15 = bf16[8,8192]{1,0:T(8,128)(2,1)S(1)} collective-permute-done((bf16[8,8192]{1,0:T(8,128)(2,1)S(1)}, bf16[8,8192]{1,0:T(8,128)(2,1)S(1)}, u32[]{:S(2)}, u32[]{:S(2)}) %collective-permute-start.15) | collective-permute-done | bytes 131104 | tf_op jit(solution)/shard_map/reduce_on_next_section/ppermute | solution.py:192
  58.8 3.0 %collective-permute-done.16 = bf16[8,8192]{1,0:T(8,128)(2,1)S(1)} collective-permute-done((bf16[8,8192]{1,0:T(8,128)(2,1)S(1)}, bf16[8,8192]{1,0:T(8,128)(2,1)S(1)}, u32[]{:S(2)}, u32[]{:S(2)}) %collective-permute-start.16) | collective-permute-done | bytes 131104 | tf_op jit(solution)/shard_map/reduce_on_next_section/ppermute | solution.py:192
  61.8 2.0 %collective-permute-done.19 = bf16[8,8192]{1,0:T(8,128)(2,1)S(1)} collective-permute-done((bf16[8,8192]{1,0:T(8,128)(2,1)S(1)}, bf16[8,8192]{1,0:T(8,128)(2,1)S(1)}, u32[]{:S(2)}, u32[]{:S(2)}) %collective-permute-start.19) | collective-permute-done | bytes 131104 | tf_op jit(solution)/shard_map/reduce_on_next_section/ppermute | solution.py:192
  63.8 0.7 %fusion = bf16[1,8,8192]{2,1,0:T(8,128)(2,1)} fusion(bf16[8,8192]{1,0:T(8,128)(2,1)S(1)} %collective-permute-done.19, bf16[8,8192]{1,0:T(8,128)(2,1)S(1)} %collective-permute-done.16, bf16[8,8192]{1,0:T(8,128)(2,1)S(1)} %collective-permute-done.15), kind=kLoop, calls=%fused_computation.1 | loop fusion | flops 393216 | bytes 524288 | tf_op jit(solution)/shard_map/broadcast_in_dim | solution.py:750
  (54 shorter events, 1.7 us)
Async XLA Ops:
  0.0 10.7 %collective-permute-start.2 = (bf16[8,8192]{1,0:T(8,128)(2,1)}, bf16[8,8192]{1,0:T(8,128)(2,1)S(1)}, u32[]{:S(2)}, u32[]{:S(2)}) collective-permute-start(bf16[8,8192]{1,0:T(8,128)(2,1)} %bitcast.20), channel_id=1, source_target_pairs={{0,6},{1,7},{2,4},{3,5},{4,2},{5,3},{6,0},{7,1},{8,14},{9,15},{10,... | collective-permute-start | bytes 393224 | tf_op jit(solution)/shard_map/gather_tokens/ppermute | solution.py:184
  3.9 6.9 %collective-permute-start.1 = (bf16[8,8192]{1,0:T(8,128)(2,1)}, bf16[8,8192]{1,0:T(8,128)(2,1)S(1)}, u32[]{:S(2)}, u32[]{:S(2)}) collective-permute-start(bf16[8,8192]{1,0:T(8,128)(2,1)} %bitcast.21), channel_id=1, source_target_pairs={{0,4},{1,5},{2,6},{3,7},{4,0},{5,1},{6,2},{7,3},{8,12},{9,13},{10,... | collective-permute-start | bytes 393224 | tf_op jit(solution)/shard_map/gather_tokens/ppermute | solution.py:184
  4.4 6.4 %collective-permute-start = (bf16[8,8192]{1,0:T(8,128)(2,1)}, bf16[8,8192]{1,0:T(8,128)(2,1)S(1)}, u32[]{:S(2)}, u32[]{:S(2)}) collective-permute-start(bf16[8,8192]{1,0:T(8,128)(2,1)} %bitcast.22), channel_id=1, source_target_pairs={{0,2},{1,3},{2,0},{3,1},{4,6},{5,7},{6,4},{7,5},{8,10},{9,11},{10,... | collective-permute-start | bytes 393224 | tf_op jit(solution)/shard_map/gather_tokens/ppermute | solution.py:184
  4.5 8.3 %slice-start = ((s8[16777216]{0:T(1024)(128)(4,1)}), s8[4194304]{0:T(1024)(128)(4,1)S(1)}, s32[]{:S(2)}) async-start(s8[16777216]{0:T(1024)(128)(4,1)} %bitcast.12), calls=%async_computation | async-start | bytes 8388608
  4.5 8.3 %slice-start.1 = ((s8[16777216]{0:T(1024)(128)(4,1)}), s8[4194304]{0:T(1024)(128)(4,1)S(1)}, s32[]{:S(2)}) async-start(s8[16777216]{0:T(1024)(128)(4,1)} %bitcast.12), calls=%async_computation.1 | async-start | bytes 8388608
  4.5 8.3 %slice-start.2 = ((s8[16777216]{0:T(1024)(128)(4,1)}), s8[4194304]{0:T(1024)(128)(4,1)S(1)}, s32[]{:S(2)}) async-start(s8[16777216]{0:T(1024)(128)(4,1)} %bitcast.12), calls=%async_computation.2 | async-start | bytes 8388608
  4.5 8.4 %slice-start.3 = ((s8[16777216]{0:T(1024)(128)(4,1)}), s8[4194304]{0:T(1024)(128)(4,1)S(1)}, s32[]{:S(2)}) async-start(s8[16777216]{0:T(1024)(128)(4,1)} %bitcast.12), calls=%async_computation.3 | async-start | bytes 8388608
  4.5 8.4 %copy-start.3 = (bf16[1,8192]{1,0:T(2,128)(2,1)S(1)}, bf16[1,8192]{1,0:T(2,128)(2,1)}, u32[]{:S(2)}) copy-start(bf16[1,8192]{1,0:T(2,128)(2,1)} %refs_2_.1) | copy-start | bytes 49156
  10.8 2.0 %collective-permute-start.3 = (bf16[4,8,8192]{2,1,0:T(8,128)(2,1)S(1)}, bf16[4,8,8192]{2,1,0:T(8,128)(2,1)S(1)}, u32[]{:S(2)}, u32[]{:S(2)}) collective-permute-start(bf16[4,8,8192]{2,1,0:T(8,128)(2,1)S(1)} %join_tokens.1.refs_0_), channel_id=1, source_target_pairs={{0,1},{1,0},{2,3},{3,2},{4,5},{5,4},{6,7},{7,6},{8,9},{9,8},{10,11... | collective-permute-start | bytes 1572872 | tf_op jit(solution)/shard_map/gather_tokens/ppermute | solution.py:184
  12.9 7.0 %copy-start.4 = (s32[1,2,16]{2,1,0:T(2,128)S(1)}, s32[1,2,16]{2,1,0:T(2,128)}, u32[]{:S(2)}) copy-start(s32[1,2,16]{2,1,0:T(2,128)} %param.18) | copy-start | bytes 388
  16.4 3.4 %collective-permute-start.4 = (bf16[64,1024]{1,0:T(8,128)(2,1)S(1)}, bf16[64,1024]{1,0:T(8,128)(2,1)S(1)}, u32[]{:S(2)}, u32[]{:S(2)}) collective-permute-start(bf16[64,1024]{1,0:T(8,128)(2,1)S(1)} %get-tuple-element.26.refs_2_.refs_0_), channel_id=1, source_target_pairs={{0,1},{1,0},{2,3},{3,2},{4,5},{5,4},{6,7},{7,6},{8,9},{9,8},{10,11... | collective-permute-start | bytes 393224 | tf_op jit(solution)/shard_map/gather_queries/ppermute | solution.py:184
  16.6 6.8 %collective-permute-start.7 = (bf16[64,1024]{1,0:T(8,128)(2,1)S(1)}, bf16[64,1024]{1,0:T(8,128)(2,1)S(1)}, u32[]{:S(2)}, u32[]{:S(2)}) collective-permute-start(bf16[64,1024]{1,0:T(8,128)(2,1)S(1)} %get-tuple-element.26.refs_2_.refs_0_), channel_id=1, source_target_pairs={{0,7},{1,6},{2,5},{3,4},{4,3},{5,2},{6,1},{7,0},{8,15},{9,14},{10,... | collective-permute-start | bytes 393224 | tf_op jit(solution)/shard_map/gather_queries/ppermute | solution.py:184
  19.5 6.8 %collective-permute-start.6 = (bf16[64,1024]{1,0:T(8,128)(2,1)S(1)}, bf16[64,1024]{1,0:T(8,128)(2,1)S(1)}, u32[]{:S(2)}, u32[]{:S(2)}) collective-permute-start(bf16[64,1024]{1,0:T(8,128)(2,1)S(1)} %get-tuple-element.26.refs_2_.refs_0_), channel_id=1, source_target_pairs={{0,5},{1,4},{2,7},{3,6},{4,1},{5,0},{6,3},{7,2},{8,13},{9,12},{10,... | collective-permute-start | bytes 393224 | tf_op jit(solution)/shard_map/gather_queries/ppermute | solution.py:184
  19.8 6.6 %collective-permute-start.5 = (bf16[64,1024]{1,0:T(8,128)(2,1)S(1)}, bf16[64,1024]{1,0:T(8,128)(2,1)S(1)}, u32[]{:S(2)}, u32[]{:S(2)}) collective-permute-start(bf16[64,1024]{1,0:T(8,128)(2,1)S(1)} %get-tuple-element.26.refs_2_.refs_0_), channel_id=1, source_target_pairs={{0,3},{1,2},{2,1},{3,0},{4,7},{5,6},{6,5},{7,4},{8,11},{9,10},{10,... | collective-permute-start | bytes 393224 | tf_op jit(solution)/shard_map/gather_queries/ppermute | solution.py:184
  26.4 3.9 %collective-permute-start.8 = (bf16[3,64,1024]{2,1,0:T(8,128)(2,1)S(1)}, bf16[3,64,1024]{2,1,0:T(8,128)(2,1)S(1)}, u32[]{:S(2)}, u32[]{:S(2)}) collective-permute-start(bf16[3,64,1024]{2,1,0:T(8,128)(2,1)S(1)} %join_queries.1.refs_2_), channel_id=1, source_target_pairs={{0,1},{1,0},{2,3},{3,2},{4,5},{5,4},{6,7},{7,6},{8,9},{9,8},{10,11... | collective-permute-start | bytes 1179656 | tf_op jit(solution)/shard_map/gather_queries/ppermute | solution.py:184
  26.6 10.5 %copy-start.1 = (bf16[1,8192,128]{2,1,0:T(8,128)(2,1)S(1)}, bf16[1,8192,128]{2,1,0:T(8,128)(2,1)}, u32[]{:S(2)}) copy-start(bf16[1,8192,128]{2,1,0:T(8,128)(2,1)} %param.14) | copy-start | bytes 6291460
  26.6 17.1 %slice-start.4 = ((s8[16777216]{0:T(1024)(128)(4,1)}), s8[4194304]{0:T(1024)(128)(4,1)S(1)}, s32[]{:S(2)}) async-start(s8[16777216]{0:T(1024)(128)(4,1)} %bitcast.15), calls=%async_computation.4 | async-start | bytes 8388608
  26.6 17.1 %slice-start.5 = ((s8[16777216]{0:T(1024)(128)(4,1)}), s8[4194304]{0:T(1024)(128)(4,1)S(1)}, s32[]{:S(2)}) async-start(s8[16777216]{0:T(1024)(128)(4,1)} %bitcast.15), calls=%async_computation.5 | async-start | bytes 8388608
  29.7 3.6 %collective-permute-start.10 = (bf16[3,144,512]{2,1,0:T(8,128)(2,1)S(1)}, bf16[3,144,512]{2,1,0:T(8,128)(2,1)S(1)}, u32[]{:S(2)}, u32[]{:S(2)}) collective-permute-start(bf16[3,144,512]{2,1,0:T(8,128)(2,1)S(1)} %cache_odd.1), channel_id=1, source_target_pairs={{0,1},{1,0},{2,3},{3,2},{4,5},{5,4},{6,7},{7,6},{8,9},{9,8},{10,11... | collective-permute-start | bytes 1327112 | tf_op jit(solution)/shard_map/cache_odd/ppermute | solution.py:184
  30.1 7.1 %copy-start = (bf16[1,8192,128]{2,1,0:T(8,128)(2,1)S(1)}, bf16[1,8192,128]{2,1,0:T(8,128)(2,1)}, u32[]{:S(2)}) copy-start(bf16[1,8192,128]{2,1,0:T(8,128)(2,1)} %param.13) | copy-start | bytes 6291460
  30.1 13.6 %slice-start.6 = ((s8[16777216]{0:T(1024)(128)(4,1)}), s8[4194304]{0:T(1024)(128)(4,1)S(1)}, s32[]{:S(2)}) async-start(s8[16777216]{0:T(1024)(128)(4,1)} %bitcast.15), calls=%async_computation.6 | async-start | bytes 8388608
  30.1 13.6 %slice-start.7 = ((s8[16777216]{0:T(1024)(128)(4,1)}), s8[4194304]{0:T(1024)(128)(4,1)S(1)}, s32[]{:S(2)}) async-start(s8[16777216]{0:T(1024)(128)(4,1)} %bitcast.15), calls=%async_computation.7 | async-start | bytes 8388608
  30.1 3.2 %collective-permute-start.9 = (bf16[1,144,512]{2,1,0:T(8,128)(2,1)S(1)}, bf16[1,144,512]{2,1,0:T(8,128)(2,1)S(1)}, u32[]{:S(2)}, u32[]{:S(2)}) collective-permute-start(bf16[1,144,512]{2,1,0:T(8,128)(2,1)S(1)} %get-tuple-element.30), channel_id=1, source_target_pairs={{0,1},{1,0},{2,3},{3,2},{4,5},{5,4},{6,7},{7,6},{8,9},{9,8},{10,11... | collective-permute-start | bytes 442376 | tf_op jit(solution)/shard_map/cache_near/ppermute | solution.py:184
  33.6 6.7 %collective-permute-start.11 = (bf16[144,512]{1,0:T(8,128)(2,1)S(1)}, bf16[144,512]{1,0:T(8,128)(2,1)S(1)}, u32[]{:S(2)}, u32[]{:S(2)}) collective-permute-start(bf16[144,512]{1,0:T(8,128)(2,1)S(1)} %get-tuple-element.32), channel_id=1, source_target_pairs={{0,2},{1,3},{2,0},{3,1},{4,6},{5,7},{6,4},{7,5},{8,10},{9,11},{10,... | collective-permute-start | bytes 442376 | tf_op jit(solution)/shard_map/exchange_parts/ppermute | solution.py:184
  35.3 7.3 %collective-permute-start.12 = (bf16[144,512]{1,0:T(8,128)(2,1)S(1)}, bf16[144,512]{1,0:T(8,128)(2,1)S(1)}, u32[]{:S(2)}, u32[]{:S(2)}) collective-permute-start(bf16[144,512]{1,0:T(8,128)(2,1)S(1)} %get-tuple-element.33), channel_id=1, source_target_pairs={{0,4},{1,5},{2,6},{3,7},{4,0},{5,1},{6,2},{7,3},{8,12},{9,13},{10,... | collective-permute-start | bytes 442376 | tf_op jit(solution)/shard_map/exchange_parts/ppermute | solution.py:184
  35.5 8.2 %collective-permute-start.13 = (bf16[144,512]{1,0:T(8,128)(2,1)S(1)}, bf16[144,512]{1,0:T(8,128)(2,1)S(1)}, u32[]{:S(2)}, u32[]{:S(2)}) collective-permute-start(bf16[144,512]{1,0:T(8,128)(2,1)S(1)} %get-tuple-element.34), channel_id=1, source_target_pairs={{0,6},{1,7},{2,4},{3,5},{4,2},{5,3},{6,0},{7,1},{8,14},{9,15},{10,... | collective-permute-start | bytes 442376 | tf_op jit(solution)/shard_map/exchange_parts/ppermute | solution.py:184
  47.0 1.6 %collective-permute-start.17 = (bf16[16,8192]{1,0:T(8,128)(2,1)S(1)}, bf16[16,8192]{1,0:T(8,128)(2,1)S(1)}, u32[]{:S(2)}, u32[]{:S(2)}) collective-permute-start(bf16[16,8192]{1,0:T(8,128)(2,1)S(1)} %get-tuple-element.42), channel_id=1, source_target_pairs={{0,1},{1,0},{2,3},{3,2},{4,5},{5,4},{6,7},{7,6},{8,9},{9,8},{10,11... | collective-permute-start | bytes 786440 | tf_op jit(solution)/shard_map/reduce_cores/ppermute | solution.py:184
  47.4 3.0 %collective-permute-start.14 = (bf16[16,8192]{1,0:T(8,128)(2,1)S(1)}, bf16[16,8192]{1,0:T(8,128)(2,1)S(1)}, u32[]{:S(2)}, u32[]{:S(2)}) collective-permute-start(bf16[16,8192]{1,0:T(8,128)(2,1)S(1)} %get-tuple-element.39), channel_id=1, source_target_pairs={{0,1},{1,0},{2,3},{3,2},{4,5},{5,4},{6,7},{7,6},{8,9},{9,8},{10,11... | collective-permute-start | bytes 786440 | tf_op jit(solution)/shard_map/reduce_cores/ppermute | solution.py:184
  48.7 5.8 %collective-permute-start.18 = (bf16[8,8192]{1,0:T(8,128)(2,1)S(1)}, bf16[8,8192]{1,0:T(8,128)(2,1)S(1)}, u32[]{:S(2)}, u32[]{:S(2)}) collective-permute-start(bf16[8,8192]{1,0:T(8,128)(2,1)S(1)} %get-tuple-element.44), channel_id=1, source_target_pairs={{0,2},{1,3},{2,0},{3,1},{4,6},{5,7},{6,4},{7,5},{8,10},{9,11},{10,... | collective-permute-start | bytes 393224 | tf_op jit(solution)/shard_map/reduce_on_next_section/ppermute | solution.py:184
  50.6 8.2 %collective-permute-start.15 = (bf16[8,8192]{1,0:T(8,128)(2,1)S(1)}, bf16[8,8192]{1,0:T(8,128)(2,1)S(1)}, u32[]{:S(2)}, u32[]{:S(2)}) collective-permute-start(bf16[8,8192]{1,0:T(8,128)(2,1)S(1)} %get-tuple-element.40), channel_id=1, source_target_pairs={{0,8},{1,9},{2,10},{3,11},{4,12},{5,13},{6,14},{7,15},{8,16},{9,17... | collective-permute-start | bytes 393224 | tf_op jit(solution)/shard_map/reduce_on_next_section/ppermute | solution.py:192
  51.6 10.2 %collective-permute-start.16 = (bf16[8,8192]{1,0:T(8,128)(2,1)S(1)}, bf16[8,8192]{1,0:T(8,128)(2,1)S(1)}, u32[]{:S(2)}, u32[]{:S(2)}) collective-permute-start(bf16[8,8192]{1,0:T(8,128)(2,1)S(1)} %get-tuple-element.41), channel_id=1, source_target_pairs={{0,10},{1,11},{2,8},{3,9},{4,14},{5,15},{6,12},{7,13},{8,18},{9,19... | collective-permute-start | bytes 393224 | tf_op jit(solution)/shard_map/reduce_on_next_section/ppermute | solution.py:192
  54.5 9.3 %collective-permute-start.19 = (bf16[8,8192]{1,0:T(8,128)(2,1)S(1)}, bf16[8,8192]{1,0:T(8,128)(2,1)S(1)}, u32[]{:S(2)}, u32[]{:S(2)}) collective-permute-start(bf16[8,8192]{1,0:T(8,128)(2,1)S(1)} %add_across.1), channel_id=1, source_target_pairs={{0,12},{1,13},{2,14},{3,15},{4,8},{5,9},{6,10},{7,11},{8,20},{9,21... | collective-permute-start | bytes 393224 | tf_op jit(solution)/shard_map/reduce_on_next_section/ppermute | solution.py:192
  (1 other events, 6.3 us)
